TPU v7x, 32 devices: a whole 2x2x4 slice. The times are simulated.
32 devices in a mesh: slab: 8 (over z, y), brick: 4 (over x, core).
Axes of the slice: x: 2, y: 2, z: 4, core: 2. Of those that a mesh axis runs over, the one named last changes fastest.
Arguments:
- positions: float32 [2048, 3, 128], P(('slab', 'brick')), may hold values from -6 to 6
- velocities: float32 [2048, 3, 128], P(('slab', 'brick')), may hold values from -6 to 6
- radii: float32 [2048, 128], P(('slab', 'brick')), may hold values from 0.6 to 1.2
- cell_of: int32 [2048, 128], P(('slab', 'brick')), may hold values from 0 to 65535
- block_route: int32 [2048, 1], P(('slab', 'brick')), may hold values from 0 to 11; in each aligned block of 64 rows (0 to 63, 64 to 127, ...) at most 11 rows name the same one
- ghost_list: int32 [512], P(('slab', 'brick')), may hold values from 0 to 63
- tile_home: int32 [4096], P(('slab', 'brick')), may hold values from 0 to 63
- tile_partner: int32 [4096], P(('slab', 'brick')), may hold values from 0 to 95
- fluid: float32 [3, 32, 128, 512], P(None, 'slab', 'brick'), may hold values from -6 to 6
Outputs:
- velocity_next: float32 [2048, 3, 128], P(('slab', 'brick'))
- fluid_next: float32 [3, 32, 128, 512], P(None, 'slab', 'brick')
Inputs may be any that keep to these rules, and one draw needn't show every extreme that they name: `block_route`: within the blocks of one device no code appears more than 11 times, and some device's blocks reach 11 for some code.
All inputs are finite; a program needn't handle non-finite values.
Results may differ from a plain program's by a relative error of at most 0.00013.
Values sent between devices are 32-bit elements; how exact they have to be, the bound alone decides.
No kernel may reach another device: no remote copies, remote signals or barrier semaphores. Data moves between devices by JAX's collectives and lax.ppermute only.
A program may use at most 64 MiB of HBM per device.

v0:
```python
import functools
import math

import jax
import jax.numpy as jnp
from jax import lax
from jax.experimental import pallas as pl
from jax.experimental.pallas import tpu as pltpu
from jax.sharding import PartitionSpec as P

stiffness = 0.01
damping = 0.005
viscosity = 0.1
coupling = 0.5
relaxation = 0.5

f32 = jnp.float32
bf16 = jnp.bfloat16
VMEM = pl.BlockSpec(memory_space=pltpu.VMEM)
SMEM = pl.BlockSpec(memory_space=pltpu.SMEM)
ANY = pl.BlockSpec(memory_space=pl.ANY)
HBM = pl.BlockSpec(memory_space=pltpu.HBM)
UNROLL = 8
GROUP = 2


def rows_up(count):
    return -(-count // 8) * 8


def call(body, outs, ins, scratch, name, flops=0, nbytes=1 << 20, places=None):
    return pl.pallas_call(
        body,
        out_shape=outs,
        in_specs=ins,
        out_specs=places or [VMEM] * len(outs),
        scratch_shapes=scratch,
        name=name,
        compiler_params=pltpu.CompilerParams(vmem_limit_bytes=40 << 20),
        cost_estimate=pl.CostEstimate(flops=flops, bytes_accessed=nbytes, transcendentals=0),
    )


def rounded(x):
    return x.astype(bf16).astype(f32)


def iota(shape, dim):
    return lax.broadcasted_iota(jnp.int32, shape, dim)


planes = 7


def copy_all(pairs, sems):
    copies = [pltpu.make_async_copy(*pair, sems.at[i]) for i, pair in enumerate(pairs)]
    for copy in copies:
        copy.start()
    return copies


def wait_all(copies):
    for copy in copies:
        copy.wait()


def pack_kernel(ghost_ref, state, fluid, up, down, right, left):
    count = ghost_ref.shape[0] // 4
    width = state.shape[2]
    nx, ny, nz = fluid.shape[1:]
    for group in range(4):
        i, j = group // 2, group % 2
        slab_to, brick_to = (up if i else down), (right if j else left)
        for g in range(count):
            block = pl.ds(ghost_ref[group * count + g], 1)
            for c in range(planes):
                row = state[c, block, :]
                at = c * 2 * count + j * count + g
                slab_to[at : at + 1, :] = row
                at = c * 2 * count + i * count + g
                brick_to[at : at + 1, :] = row
    for slab_to, x in ((up, nx - 1), (down, 0)):
        for c in range(3):
            for k in range(nz // width):
                at = planes * 2 * count + (c * (nz // width) + k) * ny
                slab_to[at : at + ny, :] = fluid[c, x, :, k * width : (k + 1) * width]
    for brick_to, y in ((right, ny - 1), (left, 0)):
        for c in range(3):
            for x in range(nx):
                for k in range(nz // width):
                    at = planes * 2 * count + (c * nx + x) * (nz // width) + k
                    brick_to[at : at + 1, :] = fluid[
                        c, x, y : y + 1, k * width : (k + 1) * width
                    ]


def three_parts(x):
    one = rounded(x)
    rest = x - one
    two = rounded(rest)
    return one, two, rest - two


def put_rows(ref, stride, rows):
    count = rows[0].shape[0]
    for k, row in enumerate(rows):
        ref[pl.ds(k, count, stride=stride), :] = row


def pair_factors(place):
    parts = [three_parts(plane) for plane in place]
    own = three_parts(
        place[3] * place[3] - place[0] * place[0] - place[1] * place[1] - place[2] * place[2]
    )
    return [[part[k] for part in parts] for k in range(3)], list(own)


def home_rows(place):
    (one, two, three), own = pair_factors(place)
    ones, zeros = jnp.ones_like(place[0]), jnp.zeros_like(place[0])
    rows = one + one + two + two + one + three
    return [2.0 * row for row in rows] + own + [ones] * 3 + [zeros] * 2


def partner_rows(place):
    (one, two, three), own = pair_factors(place)
    ones, zeros = jnp.ones_like(place[0]), jnp.zeros_like(place[0])
    return one + two + one + two + three + one + [ones] * 3 + own + [zeros] * 2


def value_rows(values):
    highs = [rounded(plane) for plane in values]
    ones, zeros = jnp.ones_like(values[0]), jnp.zeros_like(values[0])
    lows = [plane - high for plane, high in zip(values, highs)]
    return highs + [ones, zeros] + lows + [zeros, zeros]


def prepare_partners(place, speeds, rows, columns, values):
    count, width = place[0].shape
    put_rows(rows, 32, partner_rows(place))
    put_rows(values, 16, value_rows(place[0:3] + speeds))

    def turn(b, _):
        block = rows[pl.ds(pl.multiple_of(b * 32, 32), 32), :]
        columns[b] = jnp.transpose(block).astype(bf16)
        return 0

    lax.fori_loop(0, count, turn, 0, unroll=4)


def list_tiles(home_ref, partner_ref, homes, partners, lower, upper, spare):
    def one(t, count):
        partner = partner_ref[t]
        homes[count] = home_ref[t]
        partners[count] = partner - lower
        return count + jnp.where((partner >= lower) & (partner < upper), 1, 0)

    count = lax.fori_loop(0, home_ref.shape[0], one, 0, unroll=4)
    for pad in range(UNROLL):
        homes[count + pad] = spare
        partners[count + pad] = 0
    return count


def add_tiles(count, homes, partners, home_side, partner_side, values, sums):
    def some(step, _):
        for k in range(UNROLL):
            home = homes[step * UNROLL + k]
            partner = partners[step * UNROLL + k]
            factors = home_side[pl.ds(pl.multiple_of(home * 32, 32), 32), :].astype(bf16)
            weight = jnp.dot(partner_side[partner], factors, preferred_element_type=f32)
            weight = jnp.maximum(weight, 0.0)
            high = weight.astype(bf16)
            low = (weight - high.astype(f32)).astype(bf16)
            value = values[pl.ds(pl.multiple_of(partner * 16, 16), 16), :].astype(bf16)
            at = pl.ds(pl.multiple_of(home * 16, 16), 16)
            sums[at, :] += jnp.dot(
                jnp.concatenate([value, value], axis=1),
                jnp.concatenate([high, low], axis=0),
                preferred_element_type=f32,
            )
        return 0

    lax.fori_loop(0, (count + UNROLL - 1) // UNROLL, some, 0)


def dot(left, right):
    return jnp.dot(left.astype(bf16), right.astype(bf16), preferred_element_type=f32)


def plan_sort(cap, cell, route, columns, depth, spots, plan, bounds):
    nblocks, width = cell.shape
    shift = depth.bit_length() - 1
    number = cell[...]
    right = (number >> shift) >= columns // 2
    deep = (number & (depth - 1)) >= depth // 2
    kind = jnp.where(right, 2, 0) + jnp.where(deep, 1, 0)
    members = [jnp.where(kind == j, 1.0, 0.0) for j in range(4)]
    before = jnp.where(iota((width, width), 0) < iota((width, width), 1), 1.0, 0.0)
    stacked = jnp.concatenate(members, axis=0)
    ranks = dot(stacked, before)
    lengths = dot(stacked, jnp.ones((width, width), f32))
    ranks = [ranks[j * nblocks : (j + 1) * nblocks] for j in range(4)]
    lengths = [lengths[j * nblocks : (j + 1) * nblocks] for j in range(4)]

    across = jnp.broadcast_to(route[...].astype(f32), (nblocks, nblocks))
    same = across == jnp.transpose(across)
    earlier = iota((nblocks, nblocks), 1) < iota((nblocks, nblocks), 0)
    side_by_side = jnp.concatenate(lengths, axis=1)
    ahead = dot(jnp.where(same & earlier, 1.0, 0.0), side_by_side)
    whole = dot(jnp.where(same, 1.0, 0.0), side_by_side)
    rows = bounds.shape[0]
    of_code = jnp.broadcast_to(route[...], (rows, nblocks)) == iota((rows, nblocks), 0)
    totals = dot(jnp.where(of_code, 1.0, 0.0), side_by_side)

    lane = iota((nblocks, width), 1)
    bound_lane = iota((rows, width), 1)
    spot = jnp.zeros((nblocks, width), f32)
    first, chunk_first = jnp.zeros((nblocks, width), f32), jnp.zeros((nblocks, width), f32)
    bound, line = jnp.zeros((rows, width), f32), jnp.zeros((rows, width), f32)
    table = jnp.zeros((nblocks, width), jnp.int32)
    own_code = jnp.transpose(across).astype(jnp.int32)
    own_code = jnp.concatenate([own_code] * (width // nblocks), axis=1)
    for j in range(4):
        at = slice(j * width, (j + 1) * width)
        spot = spot + members[j] * (first + ranks[j])
        where = (chunk_first + ahead[:, at]).astype(jnp.int32)
        start, there = first.astype(jnp.int32), where & (width - 1)
        parts = [
            own_code * (cap + 2) + (where >> (width.bit_length() - 1)),
            there,
            start,
            lengths[j].astype(jnp.int32),
            (there - start) & (width - 1),
            (start - there) & (width - 1),
        ]
        for k, part in enumerate(parts):
            table = jnp.where(lane == 4 * k + j, part, table)
        first = first + lengths[j]
        chunk_first = chunk_first + whole[:, at]
        bound = bound + totals[:, at]
        line = jnp.where(bound_lane == j, bound, line)
    spots[...] = spot
    plan[...] = table
    bounds[...] = line


def block_order(spots, b):
    width = spots.shape[1]
    row = jnp.broadcast_to(spots[pl.ds(b, 1), :].astype(bf16), (width, width))
    hit = iota((width, width), 0).astype(f32).astype(bf16) == row
    return jnp.where(hit, jnp.ones((), bf16), jnp.zeros((), bf16))


def sort_blocks(plan, spots, data, sorted_rows, tiles):
    nblocks, width = spots.shape
    lane = iota((8, width), 1)

    def order(b, _):
        rows = data[pl.ds(pl.multiple_of(b * 16, 16), 16), :].astype(bf16)
        both = lax.dot_general(
            rows, block_order(spots, b), (((1,), (1,)), ((), ())), preferred_element_type=f32
        )
        sorted_rows[b] = both[0:8] + both[8:16]
        return 0

    def spread(b, _):
        block = sorted_rows[b]
        for j in range(4):
            tile, at, length = plan[b, j], plan[b, 4 + j], plan[b, 12 + j]
            moved = pltpu.roll(block, plan[b, 16 + j], 1)
            here = (lane >= at) & (lane < at + length)
            pltpu.store(tiles.at[tile], moved, mask=here)
            pltpu.store(tiles.at[tile + 1], moved, mask=lane < at + length - width)
        return 0

    lax.fori_loop(0, nblocks, order, 0, unroll=8)
    lax.fori_loop(0, nblocks, spread, 0, unroll=8)


def own_contacts(cap, columns, depth, home_list, partner_list, state, cell, route,
                 home_side, sums, spots, plan, bounds,
                 rows, partner_side, values, homes, partners, home_ref, partner_ref, sems):
    nblocks, width = state.shape[1:]
    copies = copy_all([(home_list, home_ref), (partner_list, partner_ref)], sems)
    plan_sort(cap, cell, route, columns, depth, spots, plan, bounds)
    place = [state[c] for c in range(4)]
    put_rows(home_side, 32, home_rows(place))
    prepare_partners(place, [state[c] for c in (4, 5, 6)], rows, partner_side, values)
    home_side[nblocks * 32 :, :] = jnp.zeros((32, width), f32)
    sums[...] = jnp.zeros(sums.shape, f32)
    wait_all(copies)
    count = list_tiles(home_ref, partner_ref, homes, partners, 0, nblocks, nblocks)
    add_tiles(count, homes, partners, home_side, partner_side, values, sums)


def diffuse(fluid, below, above, before, after, skip, diffused):
    nx, ny, nz = fluid.shape[1:]
    width = before.shape[1]
    deep = iota((ny, nz), 1)

    def face(ref, c, x):
        at = skip + (c * nx + x) * (nz // width)
        return jnp.concatenate(
            [ref[at + k : at + k + 1, :] for k in range(nz // width)], axis=1
        )

    def layer(ref, c):
        at = [skip + (c * (nz // width) + k) * ny for k in range(nz // width)]
        return jnp.concatenate([ref[start : start + ny, :] for start in at], axis=1)

    for x in range(nx):
        for c in range(3):
            here = fluid[c, x]
            near = (layer(below, c) if x == 0 else fluid[c, x - 1]) + (
                layer(above, c) if x == nx - 1 else fluid[c, x + 1]
            )
            near = near + jnp.concatenate([face(before, c, x), here[:-1]], axis=0)
            near = near + jnp.concatenate([here[1:], face(after, c, x)], axis=0)
            near = near + jnp.where(deep == 0, 0.0, pltpu.roll(here, 1, 1))
            near = near + jnp.where(deep == nz - 1, 0.0, pltpu.roll(here, nz - 1, 1))
            diffused[c, x] = here + viscosity * (near - 6.0 * here)


def brick_ahead(ahead, nbrick):
    return lax.rem(lax.axis_index("brick") + ahead, nbrick)


def ghost_contacts(nbrick, cap, partner_blocks, home_list, partner_list, plan, below,
                   above, before, after, home_side, own_sums, state, cell, spots, bounds, fluid,
                   updated, diffused, *rest):
    outgoings = rest[:nbrick]
    (rows, columns, values, sums, data, sorted_rows, tiles, homes, partners,
     home_ref, partner_ref, plan_ref, flow, sems) = rest[nbrick:]
    nblocks, width = state.shape[1:]
    per = partner_blocks // 4
    copies = copy_all(
        [
            (home_list, home_ref),
            (partner_list, partner_ref),
            (plan, plan_ref),
            (fluid, flow),
        ],
        sems,
    )
    stacked = [
        jnp.concatenate(
            [ref[c * per : (c + 1) * per, :] for ref in (below, above, before, after)], axis=0
        )
        for c in range(planes)
    ]
    prepare_partners(stacked[0:4], stacked[4:7], rows, columns, values)
    sums[...] = own_sums[...]
    wait_all(copies)
    count = list_tiles(home_ref, partner_ref, homes, partners, nblocks, nblocks + 4 * per, nblocks)
    add_tiles(count, homes, partners, home_side, columns, values, sums)
    diffuse(flow, below, above, before, after, planes * per, diffused)

    def total(k):
        high = sums[pl.ds(k, nblocks, stride=16), :]
        return high + sums[pl.ds(k + 8, nblocks, stride=16), :]

    weights = total(6)
    radius = state[3]
    inverse = 1.0 / (radius * radius * radius)
    fresh = []
    for c in range(3):
        speed = state[c + 4]
        spring = state[c] * weights - total(c)
        friction = total(c + 3) - speed * weights
        fresh.append(speed + (stiffness * spring + damping * friction) * inverse)
        updated[c] = fresh[c]

    number = cell[...]
    zeros = jnp.zeros_like(radius)
    highs = [rounded(plane) for plane in [radius] + fresh]
    lows = [plane - high for plane, high in zip([radius] + fresh, highs)]
    highs.append(((number >> 8) * 256).astype(f32))
    lows.append((number & 255).astype(f32))
    put_rows(data, 16, highs + [zeros] * 3 + lows + [zeros] * 3)
    sort_blocks(plan_ref, spots, data, sorted_rows, tiles)

    chunk = rows_up(5 * cap + 1)
    flat = tiles.reshape(tiles.shape[0] * 8, width)
    for ahead, outgoing in enumerate(outgoings):
        target = brick_ahead(ahead, nbrick)
        for side in range(3):
            code, row = side * nbrick + target, side * chunk
            for c in range(5):
                outgoing[row + c * cap : row + (c + 1) * cap, :] = flat[
                    pl.ds(code * (cap + 2) * 8 + c, cap, stride=8), :
                ]
            outgoing[row + 5 * cap : row + 5 * cap + 1, :] = bounds[pl.ds(code, 1), :]


def list_stride(segments, cap):
    return (segments + 1) * cap


def list_arrived(arrived, starts, ends, cap, places, counts):
    base, goal = places
    width = arrived.shape[1]
    stride = list_stride(len(starts), cap)
    shift = width.bit_length() - 1
    lane = iota((1, width), 1)
    filled = [jnp.int32(0)] * 4
    for start, end in zip(starts, ends):
        row = arrived[start + 5 * cap : start + 5 * cap + 1, :]
        edge = jnp.int32(0)
        for j in range(4):
            next_edge = jnp.sum(jnp.where(lane == j, row, 0.0)).astype(jnp.int32)
            first = edge >> shift
            last = jnp.where(next_edge > edge, (next_edge + width - 1) >> shift, first)
            for i in range(cap):
                base[j * stride + filled[j] + i] = start + first + i
                goal[j * stride + filled[j] + i] = end + first + i
            filled[j] = filled[j] + last - first
            edge = next_edge
    for j in range(4):
        counts[j] = filled[j]


def cell_parts(arrived, row, cap, columns, depth, bucket):
    cell = arrived[pl.ds(row + 4 * cap, 1), :].astype(jnp.int32)
    shift = (2 * depth).bit_length() - 1
    column = (cell >> shift) - (bucket // 2) * columns
    level = (cell & (2 * depth - 1)) - (bucket % 2) * depth - depth // 2
    return column.astype(f32), level.astype(f32)


def all_levels(depth, width):
    return (iota((depth, width), 0) - depth // 2).astype(f32).astype(bf16)


def level_hot(level, levels):
    hit = levels == jnp.broadcast_to(level.astype(bf16), levels.shape)
    return jnp.where(hit, jnp.ones((), bf16), jnp.zeros((), bf16))


def steps_of(counts):
    longest = jnp.maximum(
        jnp.maximum(counts[0], counts[1]), jnp.maximum(counts[2], counts[3])
    )
    return lax.shift_right_logical(longest + GROUP - 1, GROUP.bit_length() - 1)


def tile_of(counts, bucket, index, width):
    count = counts[bucket]
    real = jnp.full((1, width), jnp.where(index < count, 1, 0), jnp.int32) > 0
    return jnp.minimum(index, jnp.maximum(count - 1, 0)), real


def deposit(segments, counts, arrived, base, cap, total):
    columns, depth = total.shape[0] // 16, total.shape[1]
    width = arrived.shape[1]
    stride = list_stride(segments, cap)
    numbers = iota((columns, width), 0).astype(f32).astype(bf16)
    levels = all_levels(depth, width)

    def some(step, _):
        sums = []
        for bucket in range(4):
            high_of, low_of, level_of = [], [], []
            for k in range(GROUP):
                index, real = tile_of(counts, bucket, step * GROUP + k, width)
                row = base[bucket * stride + index]
                column, level = cell_parts(arrived, row, cap, columns, depth, bucket)
                radius = arrived[pl.ds(row, 1), :]
                mass = radius * radius * radius
                loads = [mass] + [mass * arrived[pl.ds(row + c * cap, 1), :] for c in (1, 2, 3)]
                hit = numbers == jnp.broadcast_to(column.astype(bf16), (columns, width))
                highs, lows = [], []
                for load in loads:
                    load = jnp.where(real, load, 0.0)
                    high = load.astype(bf16)
                    low = (load - high.astype(f32)).astype(bf16)
                    for parts, part in ((highs, high), (lows, low)):
                        part = jnp.broadcast_to(part, (columns, width))
                        parts.append(jnp.where(hit, part, jnp.zeros((), bf16)))
                high_of.append(jnp.concatenate(highs, axis=0))
                low_of.append(jnp.concatenate(lows, axis=0))
                level_of.append(level_hot(level, levels))
            both = lax.dot_general(
                jnp.concatenate(
                    [jnp.concatenate(high_of, axis=1), jnp.concatenate(low_of, axis=1)], axis=0
                ),
                jnp.concatenate(level_of, axis=1),
                (((1,), (1,)), ((), ())),
                preferred_element_type=f32,
            )
            sums.append(both[0 : 4 * columns] + both[4 * columns :])
        for bucket in range(4):
            total[bucket * 4 * columns : (bucket + 1) * 4 * columns, :] += sums[bucket]
        return 0

    lax.fori_loop(0, steps_of(counts), some, 0)


def sample(segments, counts, arrived, places, cap, table, answers):
    columns, depth = table.shape[0] // 24, table.shape[1]
    width = arrived.shape[1]
    stride = list_stride(segments, cap)
    levels = all_levels(depth, width)
    numbers = iota((columns, width), 0).astype(f32)
    answers[...] = jnp.zeros(answers.shape, f32)

    def some(step, _):
        found = []
        for bucket in range(4):
            hots, hits = [], []
            for k in range(GROUP):
                index, real = tile_of(counts, bucket, step * GROUP + k, width)
                row = places[0][bucket * stride + index]
                column, level = cell_parts(arrived, row, cap, columns, depth, bucket)
                hots.append(level_hot(level, levels))
                hits.append((numbers == column, real, places[1][bucket * stride + index]))
            along = jnp.dot(
                table[bucket * 6 * columns : (bucket + 1) * 6 * columns, :],
                jnp.concatenate(hots, axis=1),
                preferred_element_type=f32,
            )
            for k, (hit, real, goal) in enumerate(hits):
                part = along[:, k * width : (k + 1) * width]
                for c in range(3):
                    value = part[c * columns : (c + 1) * columns]
                    value = value + part[(c + 3) * columns : (c + 4) * columns]
                    value = jnp.sum(jnp.where(hit, value, 0.0), axis=0, keepdims=True)
                    found.append((goal + c * cap, jnp.where(real, value, 0.0)))
        for goal, value in found:
            answers[pl.ds(goal, 1), :] += value
        return 0

    lax.fori_loop(0, steps_of(counts), some, 0)


def first_deposit(nbrick, cap, crossed, total, base, goal, counts):
    chunk = rows_up(5 * cap + 1)
    total[...] = jnp.zeros(total.shape, f32)
    starts = [b * chunk for b in range(nbrick)]
    list_arrived(crossed, starts, starts, cap, (base, goal), counts)
    deposit(nbrick, counts, crossed, base, cap, total)


def advance(nbrick, cap, above, below, start, fluid, diffused, fluid_next, table, answers_up,
            answers_down, arrived, answers, total, flow, fresh_flow, base, goal, counts, sems):
    reading = pltpu.make_async_copy(fluid, flow, sems.at[0])
    reading.start()
    chunk = rows_up(5 * cap + 1)
    back = rows_up(3 * cap)
    rows = nbrick * chunk
    arrived[0:rows, :] = above[...]
    arrived[rows:, :] = below[...]
    starts = [i * chunk for i in range(2 * nbrick)]
    ends = [i * back for i in range(2 * nbrick)]
    total[...] = start[...]
    list_arrived(arrived, starts, ends, cap, (base, goal), counts)
    deposit(2 * nbrick, counts, arrived, base, cap, total)
    reading.wait()

    nx, ny, nz = flow.shape[1:]
    columns, depth = nx * ny // 2, nz // 2
    for x in range(nx):
        buckets = [2 * (x * ny // columns) + deep for deep in range(2)]
        at = x * ny % columns

        def load(c):
            spots = [4 * columns * bucket + c * columns + at for bucket in buckets]
            return jnp.concatenate([total[spot : spot + ny, :] for spot in spots], axis=1)

        volume = load(0)
        for c in range(3):
            moved = load(c + 1) - volume * flow[c, x]
            fresh = diffused[c, x] + coupling * moved
            fresh_flow[c, x] = fresh
            high = fresh.astype(bf16)
            low = (fresh - high.astype(f32)).astype(bf16)
            for deep, bucket in enumerate(buckets):
                spot = 6 * columns * bucket + c * columns + at
                half = slice(deep * depth, (deep + 1) * depth)
                table[spot : spot + ny, :] = high[:, half]
                table[spot + 3 * columns : spot + 3 * columns + ny, :] = low[:, half]
    writing = pltpu.make_async_copy(fresh_flow, fluid_next, sems.at[1])
    writing.start()
    sample(2 * nbrick, counts, arrived, (base, goal), cap, table, answers)
    answers_up[...] = answers[0 : nbrick * back, :]
    answers_down[...] = answers[nbrick * back :, :]
    writing.wait()


def last_sample(nbrick, cap, crossed, table, answers, base, goal, counts):
    chunk = rows_up(5 * cap + 1)
    back = rows_up(3 * cap)
    starts = [b * chunk for b in range(nbrick)]
    ends = [b * back for b in range(nbrick)]
    list_arrived(crossed, starts, ends, cap, (base, goal), counts)
    sample(nbrick, counts, crossed, (base, goal), cap, table, answers)


def relax(nbrick, cap, plan, updated, spots, *rest):
    returneds = rest[:nbrick]
    velocity_next, picked, sorted_rows, tiles, plan_ref, sems = rest[nbrick:]
    copies = copy_all([(plan, plan_ref)], sems)
    nblocks, width = spots.shape
    back = rows_up(3 * cap)
    flat = tiles.reshape(tiles.shape[0] * 8, width)
    for ahead, returned in enumerate(returneds):
        target = brick_ahead(ahead, nbrick)
        for side in range(3):
            code, row = side * nbrick + target, side * back
            for c in range(3):
                flat[pl.ds(code * (cap + 2) * 8 + c, cap, stride=8), :] = returned[
                    row + c * cap : row + (c + 1) * cap, :
                ]
    lane = iota((8, width), 1)
    wait_all(copies)

    def gather(b, _):
        block = jnp.zeros((8, width), f32)
        for j in range(4):
            tile, at = plan_ref[b, j], plan_ref[b, 4 + j]
            first, length = plan_ref[b, 8 + j], plan_ref[b, 12 + j]
            run = jnp.where(lane >= at, tiles[tile], tiles[tile + 1])
            run = pltpu.roll(run, plan_ref[b, 20 + j], 1)
            block = jnp.where((lane >= first) & (lane < first + length), run, block)
        sorted_rows[b] = block
        return 0

    def order(b, _):
        block = sorted_rows[b]
        high = rounded(block)
        both = jnp.dot(
            jnp.concatenate([high, block - high], axis=0).astype(bf16),
            block_order(spots, b),
            preferred_element_type=f32,
        )
        picked[b] = both[0:8] + both[8:16]
        return 0

    lax.fori_loop(0, nblocks, gather, 0, unroll=8)
    lax.fori_loop(0, nblocks, order, 0, unroll=8)
    flat = picked.reshape(nblocks * 8, width)
    for c in range(3):
        now = updated[c]
        velocity_next[c] = now + relaxation * (flat[pl.ds(c, nblocks, stride=8), :] - now)


def on_device(
    positions, velocities, radii, cell_of, block_route, ghost_list, tile_home, tile_partner, fluid
):
    nblocks, _, width = positions.shape
    nbrick = lax.axis_size("brick")
    _, nx, ny, nz = fluid.shape
    columns = nx * ny
    codes = 3 * nbrick
    cap = max(2, (2 * nblocks + codes - 1) // codes)
    chunk, back = rows_up(5 * cap + 1), rows_up(3 * cap)
    per = ghost_list.shape[0] // 2
    tiles = tile_home.shape[0]
    routes = block_route.reshape(-1)
    positions = jnp.transpose(positions, (1, 0, 2))
    velocities = jnp.transpose(velocities, (1, 0, 2))

    def struct(*shape, dtype=f32):
        return jax.ShapeDtypeStruct(shape, dtype)

    def shifted(x, axis, step):
        if step == 0:
            return x
        count = lax.axis_size(axis)
        return lax.ppermute(x, axis, [(i, (i + step) % count) for i in range(count)])

    def ints(count):
        return pltpu.SMEM((count,), jnp.int32)

    state = jnp.concatenate([positions, radii[None], velocities], axis=0)
    ghost_rows, chunks = planes * per, 3 * (nz // width)
    up, down, right, left = call(
        pack_kernel,
        [struct(ghost_rows + chunks * ny, width)] * 2 + [struct(ghost_rows + chunks * nx, width)] * 2,
        [SMEM] + [VMEM] * 2,
        [],
        "pack",
    )(ghost_list, state, fluid)
    below = shifted(up, "slab", 1)
    above = shifted(down, "slab", -1)
    before = shifted(right, "brick", 1)
    after = shifted(left, "brick", -1)

    def sides(count):
        return [
            pltpu.VMEM((count * 32, width), f32),
            pltpu.VMEM((count, width, 32), bf16),
            pltpu.VMEM((count * 16, width), f32),
        ]

    lists = [ints(tiles + UNROLL)] * 2
    contact_flops = tiles * width * width * 200
    chunk_tiles = pltpu.VMEM((codes * (cap + 2), 8, width), f32)
    block_tiles = pltpu.VMEM((nblocks, 8, width), f32)
    plan_copy = pltpu.SMEM((nblocks, width), jnp.int32)
    home_side, sums, spots, plan, bounds = call(
        functools.partial(own_contacts, cap, columns, nz),
        [
            struct((nblocks + 1) * 32, width),
            struct((nblocks + 1) * 16, width),
            struct(nblocks, width),
            struct(nblocks, width, dtype=jnp.int32),
            struct(rows_up(codes), width),
        ],
        [HBM] * 2 + [VMEM] * 3,
        sides(nblocks) + lists + [ints(tiles)] * 2 + [pltpu.SemaphoreType.DMA((2,))],
        "own_contacts",
        contact_flops,
    )(tile_home, tile_partner, state, cell_of, routes.reshape(1, nblocks))
    updated, diffused, *outgoing = call(
        functools.partial(ghost_contacts, nbrick, cap, 4 * per),
        [struct(3, nblocks, width), struct(3, nx, ny, nz)] + [struct(3 * chunk, width)] * nbrick,
        [HBM] * 2 + [ANY] + [VMEM] * 10 + [HBM],
        sides(4 * per)
        + [pltpu.VMEM(((nblocks + 1) * 16, width), f32)]
        + [pltpu.VMEM((nblocks * 16, width), f32), block_tiles, chunk_tiles]
        + lists
        + [ints(tiles), ints(tiles), plan_copy]
        + [pltpu.VMEM((3, nx, ny, nz), f32), pltpu.SemaphoreType.DMA((4,))],
        "ghost_contacts",
        contact_flops // 2,
    )(tile_home, tile_partner, plan, below, above, before, after,
      home_side, sums, state, cell_of, spots, bounds, fluid)

    crossed = [shifted(part, "brick", ahead) for ahead, part in enumerate(outgoing)]

    def side(k):
        return jnp.concatenate([part[k * chunk : (k + 1) * chunk] for part in crossed], axis=0)

    from_above = shifted(side(0), "slab", -1)
    from_below = shifted(side(2), "slab", 1)
    crossed = side(1)

    def places(count):
        return [ints(4 * list_stride(count, cap))] * 2 + [ints(4)]

    block_flops = 8 * columns * nz * width
    (started,) = call(
        functools.partial(first_deposit, nbrick, cap),
        [struct(8 * columns, nz // 2)],
        [VMEM],
        places(nbrick),
        "first_deposit",
        block_flops * nblocks // 3,
    )(crossed)
    fluid_next, table, answers_up, answers_down = call(
        functools.partial(advance, nbrick, cap),
        [
            struct(3, nx, ny, nz),
            struct(12 * columns, nz // 2, dtype=bf16),
            struct(nbrick * back, width),
            struct(nbrick * back, width),
        ],
        [VMEM] * 3 + [HBM, VMEM],
        [
            pltpu.VMEM((2 * nbrick * chunk, width), f32),
            pltpu.VMEM((2 * nbrick * back, width), f32),
            pltpu.VMEM((8 * columns, nz // 2), f32),
        ]
        + [pltpu.VMEM((3, nx, ny, nz), f32)] * 2
        + places(2 * nbrick)
        + [pltpu.SemaphoreType.DMA((2,))],
        "advance",
        block_flops * nblocks,
        places=[HBM] + [VMEM] * 3,
    )(from_above, from_below, started, fluid, diffused)
    answers_up = shifted(answers_up, "slab", 1)
    answers_down = shifted(answers_down, "slab", -1)
    (answers,) = call(
        functools.partial(last_sample, nbrick, cap),
        [struct(nbrick * back, width)],
        [VMEM] * 2,
        places(nbrick),
        "last_sample",
        block_flops * nblocks // 4,
    )(crossed, table)
    returned = []
    for behind in range(nbrick):
        at = slice(behind * back, (behind + 1) * back)
        part = jnp.concatenate([answers_up[at], answers[at], answers_down[at]], axis=0)
        returned.append(shifted(part, "brick", -behind))
    (velocity_next,) = call(
        functools.partial(relax, nbrick, cap),
        [struct(3, nblocks, width)],
        [ANY] + [VMEM] * (2 + nbrick),
        [block_tiles, block_tiles, chunk_tiles, plan_copy]
        + [pltpu.SemaphoreType.DMA((1,))],
        "relax",
    )(plan, updated, spots, *returned)
    return (jnp.transpose(velocity_next, (1, 0, 2)), fluid_next)


def solution(mesh):
    placed = (
        P(("slab", "brick"), None, None),
        P(("slab", "brick"), None, None),
        P(("slab", "brick"), None),
        P(("slab", "brick"), None),
        P(("slab", "brick"), None),
        P(("slab", "brick")),
        P(("slab", "brick")),
        P(("slab", "brick")),
        P(None, "slab", "brick", None),
    )
    return jax.shard_map(
        on_device,
        mesh=mesh,
        in_specs=placed,
        out_specs=(P(("slab", "brick"), None, None), P(None, "slab", "brick", None)),
        check_vma=False,
    )
```

profile of v0, /device:TPU:0, one launch (start us, length us, event | category | flops | bytes accessed | tf_op | source)
XLA Modules:
  0.0 77.4 jit_solution(7815937534122634278)
XLA Ops:
  0.7 1.0 %pad_maximum_fusion.state = f32[7,64,128]{2,1,0:T(8,128)S(1)} fusion(f32[3,64,128]{2,1,0:T(8,128)} %bitcast.6, f32[1,64,128]{2,1,0:T(8,128)} %bitcast.9, f32[3,64,128]{2,1,0:T(8,128)} %bitcast.7), kind=kLoop, calls=%fused_computation | loop fusion | flops 114688 | bytes 458752 | tf_op jit(solution)/shard_map/concatenate | solution.py:675
  1.7 1.1 %copy-done = f32[3,4,32,512]{3,2,1,0:T(8,128)S(1)} copy-done((f32[3,4,32,512]{3,2,1,0:T(8,128)S(1)}, f32[3,4,32,512]{3,2,1,0:T(8,128)}, u32[]{:S(2)}) %copy-start) | copy-done | bytes 786456
  2.8 0.7 copy-done.3
  3.5 0.7 pack.1
  4.1 3.0 %collective-permute-start = (f32[440,128]{1,0:T(8,128)S(1)}, f32[440,128]{1,0:T(8,128)S(1)}, u32[]{:S(2)}, u32[]{:S(2)}) collective-permute-start(f32[440,128]{1,0:T(8,128)S(1)} %get-tuple-element.22), channel_id=1, source_target_pairs={{0,4},{4,8},{8,12},{12,16},{16,20},{20,24},{24,28},{28,0},{1,5},{5... | collective-permute-start | bytes 675848 | tf_op jit(solution)/shard_map/ppermute | solution.py:670
  7.2 3.1 %collective-permute-start.1 = (f32[440,128]{1,0:T(8,128)S(1)}, f32[440,128]{1,0:T(8,128)S(1)}, u32[]{:S(2)}, u32[]{:S(2)}) collective-permute-start(f32[440,128]{1,0:T(8,128)S(1)} %get-tuple-element.23), channel_id=1, source_target_pairs={{0,28},{4,0},{8,4},{12,8},{16,12},{20,16},{24,20},{28,24},{1,29},{... | collective-permute-start | bytes 675848 | tf_op jit(solution)/shard_map/ppermute | solution.py:670
  10.3 1.7 %collective-permute-start.3 = (f32[104,128]{1,0:T(8,128)S(1)}, f32[104,128]{1,0:T(8,128)S(1)}, u32[]{:S(2)}, u32[]{:S(2)}) collective-permute-start(f32[104,128]{1,0:T(8,128)S(1)} %get-tuple-element.25), channel_id=1, source_target_pairs={{0,3},{1,0},{2,1},{3,2},{4,7},{5,4},{6,5},{7,6},{8,11},{9,8},{10,9... | collective-permute-start | bytes 159752 | tf_op jit(solution)/shard_map/ppermute | solution.py:670
  12.0 9.3 %own_contacts.1 = (f32[2080,128]{1,0:T(8,128)S(1)}, f32[1040,128]{1,0:T(8,128)S(1)}, f32[64,128]{1,0:T(8,128)S(1)}, s32[64,128]{1,0:T(8,128)S(1)}, f32[16,128]{1,0:T(8,128)S(1)}) custom-call(s32[128]{0:T(128)S(1)} %copy-done.4, s32[128]{0:T(128)S(1)} %copy-done.5, f32[7,64,128]{2,1,0:T(8,128)S(1)} %pad_maximum_fusion.state, s32[64,128]{1,0:T(8,128)S(1)} %copy-done.2, ...), custom_call_target="tpu_custom_call" | custom-call | flops 419430400 | bytes 1048576 | tf_op jit(solution)/shard_map/own_contacts/pallas_call | solution.py:701
  21.4 8.1 %ghost_contacts.1 = (f32[3,64,128]{2,1,0:T(8,128)S(1)}, f32[3,4,32,512]{3,2,1,0:T(8,128)S(1)}, f32[168,128]{1,0:T(8,128)S(1)}, f32[168,128]{1,0:T(8,128)S(1)}, f...) custom-call(s32[128]{0:T(128)S(1)} %copy-done.4, s32[128]{0:T(128)S(1)} %copy-done.5, ...), custom_call_target="tpu_custom_call" | custom-call | flops 209715200 | bytes 1048576 | tf_op jit(solution)/shard_map/ghost_contacts/pallas_call | solution.py:715
  29.6 1.7 %collective-permute-start.5 = (f32[168,128]{1,0:T(8,128)S(1)}, f32[168,128]{1,0:T(8,128)S(1)}, u32[]{:S(2)}, u32[]{:S(2)}) collective-permute-start(f32[168,128]{1,0:T(8,128)S(1)} %get-tuple-element.33), channel_id=1, source_target_pairs={{0,2},{1,3},{2,0},{3,1},{4,6},{5,7},{6,4},{7,5},{8,10},{9,11},{10,... | collective-permute-start | bytes 258056 | tf_op jit(solution)/shard_map/ppermute | solution.py:670
  31.3 1.4 %collective-permute-start.6 = (f32[168,128]{1,0:T(8,128)S(1)}, f32[168,128]{1,0:T(8,128)S(1)}, u32[]{:S(2)}, u32[]{:S(2)}) collective-permute-start(f32[168,128]{1,0:T(8,128)S(1)} %get-tuple-element.34), channel_id=1, source_target_pairs={{0,3},{1,0},{2,1},{3,2},{4,7},{5,4},{6,5},{7,6},{8,11},{9,8},{10,9... | collective-permute-start | bytes 258056 | tf_op jit(solution)/shard_map/ppermute | solution.py:670
  32.6 1.1 %collective-permute-done.4 = f32[168,128]{1,0:T(8,128)S(1)} collective-permute-done((f32[168,128]{1,0:T(8,128)S(1)}, f32[168,128]{1,0:T(8,128)S(1)}, u32[]{:S(2)}, u32[]{:S(2)}) %collective-permute-start.4) | collective-permute-done | bytes 86048 | tf_op jit(solution)/shard_map/ppermute | solution.py:670
  33.8 1.2 %collective-permute-done.5 = f32[168,128]{1,0:T(8,128)S(1)} collective-permute-done((f32[168,128]{1,0:T(8,128)S(1)}, f32[168,128]{1,0:T(8,128)S(1)}, u32[]{:S(2)}, u32[]{:S(2)}) %collective-permute-start.5) | collective-permute-done | bytes 86048 | tf_op jit(solution)/shard_map/ppermute | solution.py:670
  35.4 1.9 %collective-permute-start.7 = (f32[224,128]{1,0:T(8,128)S(1)}, f32[224,128]{1,0:T(8,128)S(1)}, u32[]{:S(2)}, u32[]{:S(2)}) collective-permute-start(f32[224,128]{1,0:T(8,128)S(1)} %pad_maximum_fusion.1), channel_id=1, source_target_pairs={{0,28},{4,0},{8,4},{12,8},{16,12},{20,16},{24,20},{28,24},{1,29},{... | collective-permute-start | bytes 344072 | tf_op jit(solution)/shard_map/ppermute | solution.py:670
  37.5 2.4 %first_deposit.1.start = f32[1024,256]{1,0:T(8,128)S(1)} custom-call(f32[224,128]{1,0:T(8,128)S(1)} %pad_maximum_fusion.3.crossed), custom_call_target="tpu_custom_call" | custom-call | flops 1431655808 | bytes 1048576 | tf_op jit(solution)/shard_map/first_deposit/pallas_call | solution.py:743
  39.9 1.3 %collective-permute-done.7.above = f32[224,128]{1,0:T(8,128)S(1)} collective-permute-done((f32[224,128]{1,0:T(8,128)S(1)}, f32[224,128]{1,0:T(8,128)S(1)}, u32[]{:S(2)}, u32[]{:S(2)}) %collective-permute-start.7) | collective-permute-done | bytes 114720 | tf_op jit(solution)/shard_map/ppermute | solution.py:670
  41.2 4.4 %collective-permute-done.8.below = f32[224,128]{1,0:T(8,128)S(1)} collective-permute-done((f32[224,128]{1,0:T(8,128)S(1)}, f32[224,128]{1,0:T(8,128)S(1)}, u32[]{:S(2)}, u32[]{:S(2)}) %collective-permute-start.8) | collective-permute-done | bytes 114720 | tf_op jit(solution)/shard_map/ppermute | solution.py:670
  45.6 12.9 %advance.1 = (f32[3,4,32,512]{3,2,1,0:T(8,128)}, bf16[1536,256]{1,0:T(8,128)(2,1)S(1)}, f32[160,128]{1,0:T(8,128)S(1)}, f32[160,128]{1,0:T(8,128)S(1)}) custom-call(f32[224,128]{1,0:T(8,128)S(1)} %collective-permute-done.7.above, f32[224,128]{1,0:T(8,128)S(1)} %collective-permute-done.8.below, f32[1024,256]{1,0:T(8,128)S(1)} %first_deposit.1.start, ...), custom_call_target="tpu_custom_call" | custom-call | flops 4294967296 | bytes 1048576 | tf_op jit(solution)/shard_map/advance/pallas_call | solution.py:751
  58.5 2.1 %last_sample.1 = f32[160,128]{1,0:T(8,128)S(1)} custom-call(f32[224,128]{1,0:T(8,128)S(1)} %pad_maximum_fusion.3.crossed, bf16[1536,256]{1,0:T(8,128)(2,1)S(1)} %get-tuple-element.37.table), custom_call_target="tpu_custom_call" | custom-call | flops 1073741824 | bytes 1048576 | tf_op jit(solution)/shard_map/last_sample/pallas_call | solution.py:774
  60.7 4.7 %collective-permute-start.10 = (f32[160,128]{1,0:T(8,128)S(1)}, f32[160,128]{1,0:T(8,128)S(1)}, u32[]{:S(2)}, u32[]{:S(2)}) collective-permute-start(f32[160,128]{1,0:T(8,128)S(1)} %get-tuple-element.38), channel_id=1, source_target_pairs={{0,28},{4,0},{8,4},{12,8},{16,12},{20,16},{24,20},{28,24},{1,29},{... | collective-permute-start | bytes 245768 | tf_op jit(solution)/shard_map/ppermute | solution.py:670
  65.4 2.4 %collective-permute-done.9 = f32[160,128]{1,0:T(8,128)S(1)} collective-permute-done((f32[160,128]{1,0:T(8,128)S(1)}, f32[160,128]{1,0:T(8,128)S(1)}, u32[]{:S(2)}, u32[]{:S(2)}) %collective-permute-start.9) | collective-permute-done | bytes 81952 | tf_op jit(solution)/shard_map/ppermute | solution.py:670
  68.5 1.6 %collective-permute-done.11.rest_1_ = f32[120,128]{1,0:T(8,128)S(1)} collective-permute-done((f32[120,128]{1,0:T(8,128)S(1)}, f32[120,128]{1,0:T(8,128)S(1)}, u32[]{:S(2)}, u32[]{:S(2)}) %collective-permute-start.11) | collective-permute-done | bytes 61472 | tf_op jit(solution)/shard_map/ppermute | solution.py:670
  70.1 2.7 %collective-permute-done.12.rest_2_ = f32[120,128]{1,0:T(8,128)S(1)} collective-permute-done((f32[120,128]{1,0:T(8,128)S(1)}, f32[120,128]{1,0:T(8,128)S(1)}, u32[]{:S(2)}, u32[]{:S(2)}) %collective-permute-start.12) | collective-permute-done | bytes 61472 | tf_op jit(solution)/shard_map/ppermute | solution.py:670
  73.0 4.5 %relax.1 = f32[3,64,128]{2,1,0:T(8,128)} custom-call(s32[64,128]{1,0:T(8,128)S(1)} %get-tuple-element.21.plan, f32[3,64,128]{2,1,0:T(8,128)S(1)} %get-tuple-element.30.updated, f32[64,128]{1,0:T(8,128)S(1)} %get-tuple-element.28.spots, f32[120,128]{1,0:T(8,128)S(1)} %pad_maximum_fusion.4.rest_0_, f32[120,128]{1,0:T(8,128)S(1)} %collective-permute-done.11.rest_1_, ...), custom_call_target="tpu_custom_call" | custom-call | bytes 1048576 | tf_op jit(solution)/shard_map/relax/pallas_call | solution.py:787
  (40 shorter events, 1.6 us)
Async XLA Ops:
  0.6 11.4 %copy-start.5 = (s32[128]{0:T(128)S(1)}, s32[128]{0:T(128)}, u32[]{:S(2)}) copy-start(s32[128]{0:T(128)} %partner_list.3) | copy-start | bytes 1540
  0.6 11.4 %copy-start.4 = (s32[128]{0:T(128)S(1)}, s32[128]{0:T(128)}, u32[]{:S(2)}) copy-start(s32[128]{0:T(128)} %home_list.3) | copy-start | bytes 1540
  0.7 11.4 %copy-start.2 = (s32[64,128]{1,0:T(8,128)S(1)}, s32[64,128]{1,0:T(8,128)}, u32[]{:S(2)}) copy-start(s32[64,128]{1,0:T(8,128)} %cell.3) | copy-start | bytes 98308
  0.7 11.4 %copy-start.6 = (s32[64,1]{0,1:T(1,128)S(1)}, s32[64,1]{0,1:T(1,128)}, u32[]{:S(2)}) copy-start(s32[64,1]{0,1:T(1,128)} %param.13) | copy-start | bytes 772
  1.7 1.1 %copy-start = (f32[3,4,32,512]{3,2,1,0:T(8,128)S(1)}, f32[3,4,32,512]{3,2,1,0:T(8,128)}, u32[]{:S(2)}) copy-start(f32[3,4,32,512]{3,2,1,0:T(8,128)} %fluid.5) | copy-start | bytes 2359300
  2.8 0.7 copy-start.3
  3.5 17.9 %copy-start.1 = (f32[3,4,32,512]{3,2,1,0:T(8,128)S(1)}, f32[3,4,32,512]{3,2,1,0:T(8,128)}, u32[]{:S(2)}) copy-start(f32[3,4,32,512]{3,2,1,0:T(8,128)} %fluid.5) | copy-start | bytes 2359300
  4.1 17.2 %collective-permute-start = (f32[440,128]{1,0:T(8,128)S(1)}, f32[440,128]{1,0:T(8,128)S(1)}, u32[]{:S(2)}, u32[]{:S(2)}) collective-permute-start(f32[440,128]{1,0:T(8,128)S(1)} %get-tuple-element.22), channel_id=1, source_target_pairs={{0,4},{4,8},{8,12},{12,16},{16,20},{20,24},{24,28},{28,0},{1,5},{5... | collective-permute-start | bytes 675848 | tf_op jit(solution)/shard_map/ppermute | solution.py:670
  7.2 14.2 %collective-permute-start.1 = (f32[440,128]{1,0:T(8,128)S(1)}, f32[440,128]{1,0:T(8,128)S(1)}, u32[]{:S(2)}, u32[]{:S(2)}) collective-permute-start(f32[440,128]{1,0:T(8,128)S(1)} %get-tuple-element.23), channel_id=1, source_target_pairs={{0,28},{4,0},{8,4},{12,8},{16,12},{20,16},{24,20},{28,24},{1,29},{... | collective-permute-start | bytes 675848 | tf_op jit(solution)/shard_map/ppermute | solution.py:670
  10.3 11.1 %collective-permute-start.2 = (f32[104,128]{1,0:T(8,128)S(1)}, f32[104,128]{1,0:T(8,128)S(1)}, u32[]{:S(2)}, u32[]{:S(2)}) collective-permute-start(f32[104,128]{1,0:T(8,128)S(1)} %get-tuple-element.24), channel_id=1, source_target_pairs={{0,1},{1,2},{2,3},{3,0},{4,5},{5,6},{6,7},{7,4},{8,9},{9,10},{10,1... | collective-permute-start | bytes 159752 | tf_op jit(solution)/shard_map/ppermute | solution.py:670
  10.3 11.1 %collective-permute-start.3 = (f32[104,128]{1,0:T(8,128)S(1)}, f32[104,128]{1,0:T(8,128)S(1)}, u32[]{:S(2)}, u32[]{:S(2)}) collective-permute-start(f32[104,128]{1,0:T(8,128)S(1)} %get-tuple-element.25), channel_id=1, source_target_pairs={{0,3},{1,0},{2,1},{3,2},{4,7},{5,4},{6,5},{7,6},{8,11},{9,8},{10,9... | collective-permute-start | bytes 159752 | tf_op jit(solution)/shard_map/ppermute | solution.py:670
  29.5 4.3 %collective-permute-start.4 = (f32[168,128]{1,0:T(8,128)S(1)}, f32[168,128]{1,0:T(8,128)S(1)}, u32[]{:S(2)}, u32[]{:S(2)}) collective-permute-start(f32[168,128]{1,0:T(8,128)S(1)} %get-tuple-element.32), channel_id=1, source_target_pairs={{0,1},{1,2},{2,3},{3,0},{4,5},{5,6},{6,7},{7,4},{8,9},{9,10},{10,1... | collective-permute-start | bytes 258056 | tf_op jit(solution)/shard_map/ppermute | solution.py:670
  29.6 5.4 %collective-permute-start.5 = (f32[168,128]{1,0:T(8,128)S(1)}, f32[168,128]{1,0:T(8,128)S(1)}, u32[]{:S(2)}, u32[]{:S(2)}) collective-permute-start(f32[168,128]{1,0:T(8,128)S(1)} %get-tuple-element.33), channel_id=1, source_target_pairs={{0,2},{1,3},{2,0},{3,1},{4,6},{5,7},{6,4},{7,5},{8,10},{9,11},{10,... | collective-permute-start | bytes 258056 | tf_op jit(solution)/shard_map/ppermute | solution.py:670
  31.3 4.1 %collective-permute-start.6 = (f32[168,128]{1,0:T(8,128)S(1)}, f32[168,128]{1,0:T(8,128)S(1)}, u32[]{:S(2)}, u32[]{:S(2)}) collective-permute-start(f32[168,128]{1,0:T(8,128)S(1)} %get-tuple-element.34), channel_id=1, source_target_pairs={{0,3},{1,0},{2,1},{3,2},{4,7},{5,4},{6,5},{7,6},{8,11},{9,8},{10,9... | collective-permute-start | bytes 258056 | tf_op jit(solution)/shard_map/ppermute | solution.py:670
  35.4 5.8 %collective-permute-start.7 = (f32[224,128]{1,0:T(8,128)S(1)}, f32[224,128]{1,0:T(8,128)S(1)}, u32[]{:S(2)}, u32[]{:S(2)}) collective-permute-start(f32[224,128]{1,0:T(8,128)S(1)} %pad_maximum_fusion.1), channel_id=1, source_target_pairs={{0,28},{4,0},{8,4},{12,8},{16,12},{20,16},{24,20},{28,24},{1,29},{... | collective-permute-start | bytes 344072 | tf_op jit(solution)/shard_map/ppermute | solution.py:670
  37.3 8.3 %collective-permute-start.8 = (f32[224,128]{1,0:T(8,128)S(1)}, f32[224,128]{1,0:T(8,128)S(1)}, u32[]{:S(2)}, u32[]{:S(2)}) collective-permute-start(f32[224,128]{1,0:T(8,128)S(1)} %pad_maximum_fusion.2), channel_id=1, source_target_pairs={{0,4},{4,8},{8,12},{12,16},{16,20},{20,24},{24,28},{28,0},{1,5},{5... | collective-permute-start | bytes 344072 | tf_op jit(solution)/shard_map/ppermute | solution.py:670
  60.6 7.2 %collective-permute-start.9 = (f32[160,128]{1,0:T(8,128)S(1)}, f32[160,128]{1,0:T(8,128)S(1)}, u32[]{:S(2)}, u32[]{:S(2)}) collective-permute-start(f32[160,128]{1,0:T(8,128)S(1)} %get-tuple-element.36), channel_id=1, source_target_pairs={{0,4},{4,8},{8,12},{12,16},{16,20},{20,24},{24,28},{28,0},{1,5},{5... | collective-permute-start | bytes 245768 | tf_op jit(solution)/shard_map/ppermute | solution.py:670
  60.7 7.1 %collective-permute-start.10 = (f32[160,128]{1,0:T(8,128)S(1)}, f32[160,128]{1,0:T(8,128)S(1)}, u32[]{:S(2)}, u32[]{:S(2)}) collective-permute-start(f32[160,128]{1,0:T(8,128)S(1)} %get-tuple-element.38), channel_id=1, source_target_pairs={{0,28},{4,0},{8,4},{12,8},{16,12},{20,16},{24,20},{28,24},{1,29},{... | collective-permute-start | bytes 245768 | tf_op jit(solution)/shard_map/ppermute | solution.py:670
  67.8 2.3 %collective-permute-start.11 = (f32[120,128]{1,0:T(8,128)S(1)}, f32[120,128]{1,0:T(8,128)S(1)}, u32[]{:S(2)}, u32[]{:S(2)}) collective-permute-start(f32[120,128]{1,0:T(8,128)S(1)} %pad_maximum_fusion.5), channel_id=1, source_target_pairs={{0,3},{1,0},{2,1},{3,2},{4,7},{5,4},{6,5},{7,6},{8,11},{9,8},{10,9... | collective-permute-start | bytes 184328 | tf_op jit(solution)/shard_map/ppermute | solution.py:670
  67.9 4.9 %collective-permute-start.12 = (f32[120,128]{1,0:T(8,128)S(1)}, f32[120,128]{1,0:T(8,128)S(1)}, u32[]{:S(2)}, u32[]{:S(2)}) collective-permute-start(f32[120,128]{1,0:T(8,128)S(1)} %pad_maximum_fusion.6), channel_id=1, source_target_pairs={{0,2},{1,3},{2,0},{3,1},{4,6},{5,7},{6,4},{7,5},{8,10},{9,11},{10,... | collective-permute-start | bytes 184328 | tf_op jit(solution)/shard_map/ppermute | solution.py:670
  68.0 5.0 %collective-permute-start.13 = (f32[120,128]{1,0:T(8,128)S(1)}, f32[120,128]{1,0:T(8,128)S(1)}, u32[]{:S(2)}, u32[]{:S(2)}) collective-permute-start(f32[120,128]{1,0:T(8,128)S(1)} %pad_maximum_fusion.7), channel_id=1, source_target_pairs={{0,1},{1,2},{2,3},{3,0},{4,5},{5,6},{6,7},{7,4},{8,9},{9,10},{10,1... | collective-permute-start | bytes 184328 | tf_op jit(solution)/shard_map/ppermute | solution.py:670
where the time goes:
time: 77.9 us; the launch traced here: 77.4 us
  Pallas kernels  39.9 us (51%)
  starting transfers between devices  18.4 us (24%)
  waiting for transfers between devices  15.3 us (20%)
  local copies, waits for them, and re-layouts  1.86 us (2%)
  other arithmetic  1.05 us (1%)
  between operations  0.87 us (1%)
    ppermute x14, starting transfers between devices, shifted(): lax.ppermute(x, axis, [(i, (i + step) % count) for i in range(count)])  18.4 us
    ppermute x14, waiting for transfers between devices, shifted(): lax.ppermute(x, axis, [(i, (i + step) % count) for i in range(count)])  15.3 us
    pallas_call x1, Pallas kernels, on_device(): call(functools.partial(advance, nbrick, cap), [struct(3, nx, ny, nz), str...  12.9 us
    pallas_call x1, Pallas kernels, on_device(): call(functools.partial(own_contacts, cap, columns, nz), [struct((nblocks...  9.31 us
    pallas_call x1, Pallas kernels, on_device(): call(functools.partial(ghost_contacts, nbrick, cap, 4 * per), [struct(3,...  8.13 us
    pallas_call x1, Pallas kernels, on_device(): call(functools.partial(relax, nbrick, cap), [struct(3, nblocks, width)],...  4.47 us
    pallas_call x1, Pallas kernels, on_device(): call(functools.partial(first_deposit, nbrick, cap), [struct(8 * columns,...  2.38 us
    pallas_call x1, Pallas kernels, on_device(): call(functools.partial(last_sample, nbrick, cap), [struct(nbrick * back,...  2.07 us
  transfers between devices with their start and end apart: 14, of which 9 were waited for; matrix products, arithmetic and copies ran while one was open for 0% of the time, Pallas kernels for 15%

commit v1 on v0

--- a/solution.py
+++ b/solution.py
@@ -28,7 +28,7 @@
     return -(-count // 8) * 8
 
 
-def call(body, outs, ins, scratch, name, flops=0, nbytes=1 << 20, places=None):
+def call(body, outs, ins, scratch, name, flops=0, nbytes=1 << 20, places=None, vmem=40 << 20):
     return pl.pallas_call(
         body,
         out_shape=outs,
@@ -36,7 +36,7 @@
         out_specs=places or [VMEM] * len(outs),
         scratch_shapes=scratch,
         name=name,
-        compiler_params=pltpu.CompilerParams(vmem_limit_bytes=40 << 20),
+        compiler_params=pltpu.CompilerParams(vmem_limit_bytes=vmem),
         cost_estimate=pl.CostEstimate(flops=flops, bytes_accessed=nbytes, transcendentals=0),
     )
 
@@ -327,11 +327,11 @@
 
 
 def ghost_contacts(nbrick, cap, partner_blocks, home_list, partner_list, plan, below,
-                   above, before, after, home_side, own_sums, state, cell, spots, bounds, fluid,
-                   updated, diffused, *rest):
+                   above, before, after, home_side, own_sums, state, cell, spots, bounds,
+                   updated, *rest):
     outgoings = rest[:nbrick]
     (rows, columns, values, sums, data, sorted_rows, tiles, homes, partners,
-     home_ref, partner_ref, plan_ref, flow, sems) = rest[nbrick:]
+     home_ref, partner_ref, plan_ref, sems) = rest[nbrick:]
     nblocks, width = state.shape[1:]
     per = partner_blocks // 4
     copies = copy_all(
@@ -339,7 +339,6 @@
             (home_list, home_ref),
             (partner_list, partner_ref),
             (plan, plan_ref),
-            (fluid, flow),
         ],
         sems,
     )
@@ -354,7 +353,6 @@
     wait_all(copies)
     count = list_tiles(home_ref, partner_ref, homes, partners, nblocks, nblocks + 4 * per, nblocks)
     add_tiles(count, homes, partners, home_side, columns, values, sums)
-    diffuse(flow, below, above, before, after, planes * per, diffused)
 
     def total(k):
         high = sums[pl.ds(k, nblocks, stride=16), :]
@@ -533,12 +531,16 @@
     lax.fori_loop(0, steps_of(counts), some, 0)
 
 
-def first_deposit(nbrick, cap, crossed, total, base, goal, counts):
+def first_deposit(nbrick, cap, skip, crossed, below, above, before, after, fluid, total, diffused,
+                  flow, base, goal, counts, sems):
+    reading = copy_all([(fluid, flow)], sems)
     chunk = rows_up(5 * cap + 1)
     total[...] = jnp.zeros(total.shape, f32)
     starts = [b * chunk for b in range(nbrick)]
     list_arrived(crossed, starts, starts, cap, (base, goal), counts)
     deposit(nbrick, counts, crossed, base, cap, total)
+    wait_all(reading)
+    diffuse(flow, below, above, before, after, skip, diffused)
 
 
 def advance(nbrick, cap, above, below, start, fluid, diffused, fluid_next, table, answers_up,
@@ -587,13 +589,16 @@
     writing.wait()
 
 
-def last_sample(nbrick, cap, crossed, table, answers, base, goal, counts):
+def last_sample(nbrick, cap, crossed, table, *rest):
+    answers, base, goal, counts = rest[nbrick:]
     chunk = rows_up(5 * cap + 1)
     back = rows_up(3 * cap)
     starts = [b * chunk for b in range(nbrick)]
     ends = [b * back for b in range(nbrick)]
     list_arrived(crossed, starts, ends, cap, (base, goal), counts)
     sample(nbrick, counts, crossed, (base, goal), cap, table, answers)
+    for b, part in enumerate(rest[:nbrick]):
+        part[...] = answers[b * back : (b + 1) * back, :]
 
 
 def relax(nbrick, cap, plan, updated, spots, *rest):
@@ -712,20 +717,19 @@
         "own_contacts",
         contact_flops,
     )(tile_home, tile_partner, state, cell_of, routes.reshape(1, nblocks))
-    updated, diffused, *outgoing = call(
+    updated, *outgoing = call(
         functools.partial(ghost_contacts, nbrick, cap, 4 * per),
-        [struct(3, nblocks, width), struct(3, nx, ny, nz)] + [struct(3 * chunk, width)] * nbrick,
-        [HBM] * 2 + [ANY] + [VMEM] * 10 + [HBM],
+        [struct(3, nblocks, width)] + [struct(3 * chunk, width)] * nbrick,
+        [HBM] * 2 + [ANY] + [VMEM] * 10,
         sides(4 * per)
         + [pltpu.VMEM(((nblocks + 1) * 16, width), f32)]
         + [pltpu.VMEM((nblocks * 16, width), f32), block_tiles, chunk_tiles]
         + lists
-        + [ints(tiles), ints(tiles), plan_copy]
-        + [pltpu.VMEM((3, nx, ny, nz), f32), pltpu.SemaphoreType.DMA((4,))],
+        + [ints(tiles), ints(tiles), plan_copy, pltpu.SemaphoreType.DMA((3,))],
         "ghost_contacts",
         contact_flops // 2,
     )(tile_home, tile_partner, plan, below, above, before, after,
-      home_side, sums, state, cell_of, spots, bounds, fluid)
+      home_side, sums, state, cell_of, spots, bounds)
 
     crossed = [shifted(part, "brick", ahead) for ahead, part in enumerate(outgoing)]
 
@@ -740,14 +744,16 @@
         return [ints(4 * list_stride(count, cap))] * 2 + [ints(4)]
 
     block_flops = 8 * columns * nz * width
-    (started,) = call(
-        functools.partial(first_deposit, nbrick, cap),
-        [struct(8 * columns, nz // 2)],
-        [VMEM],
-        places(nbrick),
+    started, diffused = call(
+        functools.partial(first_deposit, nbrick, cap, ghost_rows),
+        [struct(8 * columns, nz // 2), struct(3, nx, ny, nz)],
+        [VMEM] * 5 + [HBM],
+        [pltpu.VMEM((3, nx, ny, nz), f32)]
+        + places(nbrick)
+        + [pltpu.SemaphoreType.DMA((1,))],
         "first_deposit",
         block_flops * nblocks // 3,
-    )(crossed)
+    )(crossed, below, above, before, after, fluid)
     fluid_next, table, answers_up, answers_down = call(
         functools.partial(advance, nbrick, cap),
         [
@@ -771,18 +777,18 @@
     )(from_above, from_below, started, fluid, diffused)
     answers_up = shifted(answers_up, "slab", 1)
     answers_down = shifted(answers_down, "slab", -1)
-    (answers,) = call(
+    answers = call(
         functools.partial(last_sample, nbrick, cap),
-        [struct(nbrick * back, width)],
+        [struct(back, width)] * nbrick,
         [VMEM] * 2,
-        places(nbrick),
+        [pltpu.VMEM((nbrick * back, width), f32)] + places(nbrick),
         "last_sample",
         block_flops * nblocks // 4,
     )(crossed, table)
     returned = []
     for behind in range(nbrick):
         at = slice(behind * back, (behind + 1) * back)
-        part = jnp.concatenate([answers_up[at], answers[at], answers_down[at]], axis=0)
+        part = jnp.concatenate([answers_up[at], answers[behind], answers_down[at]], axis=0)
         returned.append(shifted(part, "brick", -behind))
     (velocity_next,) = call(
         functools.partial(relax, nbrick, cap),

time: 77.9 us -> 73.8 us (0.947)
  waiting for transfers between devices: 15.3 us -> 12.3 us
  Pallas kernels: 39.9 us -> 39 us
    ppermute x14, waiting for transfers between devices: 15.3 us -> 12.3 us  [shifted(): lax.ppermute(x, axis, [(i, (i + step) % count) for i in range(count)])]
    pallas_call x1, Pallas kernels: 12.9 us -> 12 us  [on_device(): call(functools.partial(advance, nbrick, cap), [struct(3, nx, ny, nz), str...]
  transfers between devices with their start and end apart: 14 -> 14, of which waited for: 9 -> 9; matrix products, arithmetic and copies ran while one was open for 0% -> 0% of each run, Pallas kernels for 15% -> 19%
where the time goes in v1:
time: 73.8 us; the launch traced here: 73.9 us
  Pallas kernels  39 us (53%)
  starting transfers between devices  18.8 us (25%)
  waiting for transfers between devices  12.3 us (17%)
  local copies, waits for them, and re-layouts  1.85 us (3%)
  other arithmetic  1.05 us (1%)
  between operations  0.85 us (1%)
    ppermute x14, starting transfers between devices, shifted(): lax.ppermute(x, axis, [(i, (i + step) % count) for i in range(count)])  18.8 us
    ppermute x14, waiting for transfers between devices, shifted(): lax.ppermute(x, axis, [(i, (i + step) % count) for i in range(count)])  12.3 us
    pallas_call x1, Pallas kernels, on_device(): call(functools.partial(advance, nbrick, cap), [struct(3, nx, ny, nz), str...  12 us
    pallas_call x1, Pallas kernels, on_device(): call(functools.partial(own_contacts, cap, columns, nz), [struct((nblocks...  8.93 us
    pallas_call x1, Pallas kernels, on_device(): call(functools.partial(ghost_contacts, nbrick, cap, 4 * per), [struct(3,...  7.91 us
    pallas_call x1, Pallas kernels, on_device(): call(functools.partial(relax, nbrick, cap), [struct(3, nblocks, width)],...  4.47 us
    pallas_call x1, Pallas kernels, on_device(): call(functools.partial(first_deposit, nbrick, cap, ghost_rows), [struct(8...  2.98 us
    pallas_call x1, Pallas kernels, on_device(): call(functools.partial(last_sample, nbrick, cap), [struct(back, width)] *...  2.07 us
  transfers between devices with their start and end apart: 14, of which 9 were waited for; matrix products, arithmetic and copies ran while one was open for 0% of the time, Pallas kernels for 19%

profile of v1, /device:TPU:0, one launch (start us, length us, event | category | flops | bytes accessed | tf_op | source)
XLA Modules:
  0.0 73.9 jit_solution(7749602460745850042)
XLA Ops:
  0.7 1.0 %pad_maximum_fusion.state = f32[7,64,128]{2,1,0:T(8,128)S(1)} fusion(f32[3,64,128]{2,1,0:T(8,128)} %bitcast.6, f32[1,64,128]{2,1,0:T(8,128)} %bitcast.9, f32[3,64,128]{2,1,0:T(8,128)} %bitcast.7), kind=kLoop, calls=%fused_computation | loop fusion | flops 114688 | bytes 458752 | tf_op jit(solution)/shard_map/concatenate | solution.py:680
  1.7 1.1 %copy-done = f32[3,4,32,512]{3,2,1,0:T(8,128)S(1)} copy-done((f32[3,4,32,512]{3,2,1,0:T(8,128)S(1)}, f32[3,4,32,512]{3,2,1,0:T(8,128)}, u32[]{:S(2)}) %copy-start) | copy-done | bytes 786456
  2.8 0.7 copy-done.3
  3.5 0.7 pack.1
  4.1 3.0 %collective-permute-start = (f32[440,128]{1,0:T(8,128)S(1)}, f32[440,128]{1,0:T(8,128)S(1)}, u32[]{:S(2)}, u32[]{:S(2)}) collective-permute-start(f32[440,128]{1,0:T(8,128)S(1)} %get-tuple-element.27), channel_id=1, source_target_pairs={{0,4},{4,8},{8,12},{12,16},{16,20},{20,24},{24,28},{28,0},{1,5},{5... | collective-permute-start | bytes 675848 | tf_op jit(solution)/shard_map/ppermute | solution.py:675
  7.2 3.1 %collective-permute-start.1 = (f32[440,128]{1,0:T(8,128)S(1)}, f32[440,128]{1,0:T(8,128)S(1)}, u32[]{:S(2)}, u32[]{:S(2)}) collective-permute-start(f32[440,128]{1,0:T(8,128)S(1)} %get-tuple-element.28), channel_id=1, source_target_pairs={{0,28},{4,0},{8,4},{12,8},{16,12},{20,16},{24,20},{28,24},{1,29},{... | collective-permute-start | bytes 675848 | tf_op jit(solution)/shard_map/ppermute | solution.py:675
  10.3 1.7 %collective-permute-start.3 = (f32[104,128]{1,0:T(8,128)S(1)}, f32[104,128]{1,0:T(8,128)S(1)}, u32[]{:S(2)}, u32[]{:S(2)}) collective-permute-start(f32[104,128]{1,0:T(8,128)S(1)} %get-tuple-element.30), channel_id=1, source_target_pairs={{0,3},{1,0},{2,1},{3,2},{4,7},{5,4},{6,5},{7,6},{8,11},{9,8},{10,9... | collective-permute-start | bytes 159752 | tf_op jit(solution)/shard_map/ppermute | solution.py:675
  12.0 8.9 %own_contacts.1 = (f32[2080,128]{1,0:T(8,128)S(1)}, f32[1040,128]{1,0:T(8,128)S(1)}, f32[64,128]{1,0:T(8,128)S(1)}, s32[64,128]{1,0:T(8,128)S(1)}, f32[16,128]{1,0:T(8,128)S(1)}) custom-call(s32[128]{0:T(128)S(1)} %copy-done.4, s32[128]{0:T(128)S(1)} %copy-done.5, f32[7,64,128]{2,1,0:T(8,128)S(1)} %pad_maximum_fusion.state, s32[64,128]{1,0:T(8,128)S(1)} %copy-done.2, ...), custom_call_target="tpu_custom_call" | custom-call | flops 419430400 | bytes 1048576 | tf_op jit(solution)/shard_map/own_contacts/pallas_call | solution.py:706
  21.0 7.9 %ghost_contacts.1 = (f32[3,64,128]{2,1,0:T(8,128)S(1)}, f32[168,128]{1,0:T(8,128)S(1)}, f32[168,128]{1,0:T(8,128)S(1)}, f32[168,128]{1,0:T(8,128)S(1)}, f32[168,128]{1,0:T(8,128)S(1)}) custom-call(s32[128]{0:T(128)S(1)} %copy-done.4, s32[128]{0:T(128)S(1)} %copy-done.5, s32[64,128]{1,0:T(8,128)S(1)} %get-tuple-element.26.plan, ...), custom_call_target="tpu_custom_call" | custom-call | flops 209715200 | bytes 1048576 | tf_op jit(solution)/shard_map/ghost_contacts/pallas_call | solution.py:720
  29.0 1.7 %collective-permute-start.5 = (f32[168,128]{1,0:T(8,128)S(1)}, f32[168,128]{1,0:T(8,128)S(1)}, u32[]{:S(2)}, u32[]{:S(2)}) collective-permute-start(f32[168,128]{1,0:T(8,128)S(1)} %get-tuple-element.38), channel_id=1, source_target_pairs={{0,2},{1,3},{2,0},{3,1},{4,6},{5,7},{6,4},{7,5},{8,10},{9,11},{10,... | collective-permute-start | bytes 258056 | tf_op jit(solution)/shard_map/ppermute | solution.py:675
  30.7 1.4 %collective-permute-start.6 = (f32[168,128]{1,0:T(8,128)S(1)}, f32[168,128]{1,0:T(8,128)S(1)}, u32[]{:S(2)}, u32[]{:S(2)}) collective-permute-start(f32[168,128]{1,0:T(8,128)S(1)} %get-tuple-element.39), channel_id=1, source_target_pairs={{0,3},{1,0},{2,1},{3,2},{4,7},{5,4},{6,5},{7,6},{8,11},{9,8},{10,9... | collective-permute-start | bytes 258056 | tf_op jit(solution)/shard_map/ppermute | solution.py:675
  32.0 1.1 %collective-permute-done.4 = f32[168,128]{1,0:T(8,128)S(1)} collective-permute-done((f32[168,128]{1,0:T(8,128)S(1)}, f32[168,128]{1,0:T(8,128)S(1)}, u32[]{:S(2)}, u32[]{:S(2)}) %collective-permute-start.4) | collective-permute-done | bytes 86048 | tf_op jit(solution)/shard_map/ppermute | solution.py:675
  33.2 1.2 %collective-permute-done.5 = f32[168,128]{1,0:T(8,128)S(1)} collective-permute-done((f32[168,128]{1,0:T(8,128)S(1)}, f32[168,128]{1,0:T(8,128)S(1)}, u32[]{:S(2)}, u32[]{:S(2)}) %collective-permute-start.5) | collective-permute-done | bytes 86048 | tf_op jit(solution)/shard_map/ppermute | solution.py:675
  34.8 1.9 %collective-permute-start.7 = (f32[224,128]{1,0:T(8,128)S(1)}, f32[224,128]{1,0:T(8,128)S(1)}, u32[]{:S(2)}, u32[]{:S(2)}) collective-permute-start(f32[224,128]{1,0:T(8,128)S(1)} %pad_maximum_fusion.1), channel_id=1, source_target_pairs={{0,28},{4,0},{8,4},{12,8},{16,12},{20,16},{24,20},{28,24},{1,29},{... | collective-permute-start | bytes 344072 | tf_op jit(solution)/shard_map/ppermute | solution.py:675
  36.9 3.0 %first_deposit.1 = (f32[1024,256]{1,0:T(8,128)S(1)}, f32[3,4,32,512]{3,2,1,0:T(8,128)S(1)}) custom-call(f32[224,128]{1,0:T(8,128)S(1)} %pad_maximum_fusion.3.crossed, f32[440,128]{1,0:T(8,128)S(1)} %collective-permute-done.below, f32[440,128]{1,0:T(8,128)S(1)} %collective-permute-done.1.above, f32[104,128]{1,0:T(8,128)S(1)} %collective-permute-done.2.before, ...), custom_call_target="tpu_custom_call" | custom-call | flops 1431655808 | bytes 1048576 | tf_op jit(solution)/shard_map/first_deposit/pallas_call | solution.py:747
  39.9 0.7 collective-permute-done.7.above
  40.6 4.4 %collective-permute-done.8.below = f32[224,128]{1,0:T(8,128)S(1)} collective-permute-done((f32[224,128]{1,0:T(8,128)S(1)}, f32[224,128]{1,0:T(8,128)S(1)}, u32[]{:S(2)}, u32[]{:S(2)}) %collective-permute-start.8) | collective-permute-done | bytes 114720 | tf_op jit(solution)/shard_map/ppermute | solution.py:675
  45.0 12.0 %advance.1 = (f32[3,4,32,512]{3,2,1,0:T(8,128)}, bf16[1536,256]{1,0:T(8,128)(2,1)S(1)}, f32[160,128]{1,0:T(8,128)S(1)}, f32[160,128]{1,0:T(8,128)S(1)}) custom-call(f32[224,128]{1,0:T(8,128)S(1)} %collective-permute-done.7.above, f32[224,128]{1,0:T(8,128)S(1)} %collective-permute-done.8.below, f32[1024,256]{1,0:T(8,128)S(1)} %get-tuple-element.40.start, ...), custom_call_target="tpu_custom_call" | custom-call | flops 4294967296 | bytes 1048576 | tf_op jit(solution)/shard_map/advance/pallas_call | solution.py:757
  57.1 4.7 %collective-permute-start.10 = (f32[160,128]{1,0:T(8,128)S(1)}, f32[160,128]{1,0:T(8,128)S(1)}, u32[]{:S(2)}, u32[]{:S(2)}) collective-permute-start(f32[160,128]{1,0:T(8,128)S(1)} %get-tuple-element.45), channel_id=1, source_target_pairs={{0,28},{4,0},{8,4},{12,8},{16,12},{20,16},{24,20},{28,24},{1,29},{... | collective-permute-start | bytes 245768 | tf_op jit(solution)/shard_map/ppermute | solution.py:675
  61.8 2.1 %last_sample.1 = (f32[40,128]{1,0:T(8,128)S(1)}, f32[40,128]{1,0:T(8,128)S(1)}, f32[40,128]{1,0:T(8,128)S(1)}, f32[40,128]{1,0:T(8,128)S(1)}) custom-call(f32[224,128]{1,0:T(8,128)S(1)} %pad_maximum_fusion.3.crossed, bf16[1536,256]{1,0:T(8,128)(2,1)S(1)} %get-tuple-element.43.table), custom_call_target="tpu_custom_call" | custom-call | flops 1073741824 | bytes 1048576 | tf_op jit(solution)/shard_map/last_sample/pallas_call | solution.py:780
  64.3 0.7 %collective-permute-start.12 = (f32[120,128]{1,0:T(8,128)S(1)}, f32[120,128]{1,0:T(8,128)S(1)}, u32[]{:S(2)}, u32[]{:S(2)}) collective-permute-start(f32[120,128]{1,0:T(8,128)S(1)} %pad_maximum_fusion.6), channel_id=1, source_target_pairs={{0,2},{1,3},{2,0},{3,1},{4,6},{5,7},{6,4},{7,5},{8,10},{9,11},{10,... | collective-permute-start | bytes 184328 | tf_op jit(solution)/shard_map/ppermute | solution.py:675
  65.2 1.2 %collective-permute-done.11.rest_1_ = f32[120,128]{1,0:T(8,128)S(1)} collective-permute-done((f32[120,128]{1,0:T(8,128)S(1)}, f32[120,128]{1,0:T(8,128)S(1)}, u32[]{:S(2)}, u32[]{:S(2)}) %collective-permute-start.11) | collective-permute-done | bytes 61472 | tf_op jit(solution)/shard_map/ppermute | solution.py:675
  66.5 2.7 %collective-permute-done.12.rest_2_ = f32[120,128]{1,0:T(8,128)S(1)} collective-permute-done((f32[120,128]{1,0:T(8,128)S(1)}, f32[120,128]{1,0:T(8,128)S(1)}, u32[]{:S(2)}, u32[]{:S(2)}) %collective-permute-start.12) | collective-permute-done | bytes 61472 | tf_op jit(solution)/shard_map/ppermute | solution.py:675
  69.4 4.5 %relax.1 = f32[3,64,128]{2,1,0:T(8,128)} custom-call(s32[64,128]{1,0:T(8,128)S(1)} %get-tuple-element.26.plan, f32[3,64,128]{2,1,0:T(8,128)S(1)} %get-tuple-element.35.updated, f32[64,128]{1,0:T(8,128)S(1)} %get-tuple-element.33.spots, f32[120,128]{1,0:T(8,128)S(1)} %pad_maximum_fusion.4.rest_0_, f32[120,128]{1,0:T(8,128)S(1)} %collective-permute-done.11.rest_1_, ...), custom_call_target="tpu_custom_call" | custom-call | bytes 1048576 | tf_op jit(solution)/shard_map/relax/pallas_call | solution.py:793
  (39 shorter events, 1.6 us)
Async XLA Ops:
  0.6 11.4 %copy-start.5 = (s32[128]{0:T(128)S(1)}, s32[128]{0:T(128)}, u32[]{:S(2)}) copy-start(s32[128]{0:T(128)} %partner_list.3) | copy-start | bytes 1540
  0.6 11.4 %copy-start.4 = (s32[128]{0:T(128)S(1)}, s32[128]{0:T(128)}, u32[]{:S(2)}) copy-start(s32[128]{0:T(128)} %home_list.3) | copy-start | bytes 1540
  0.7 11.4 %copy-start.2 = (s32[64,128]{1,0:T(8,128)S(1)}, s32[64,128]{1,0:T(8,128)}, u32[]{:S(2)}) copy-start(s32[64,128]{1,0:T(8,128)} %cell.3) | copy-start | bytes 98308
  0.7 11.4 %copy-start.6 = (s32[64,1]{0,1:T(1,128)S(1)}, s32[64,1]{0,1:T(1,128)}, u32[]{:S(2)}) copy-start(s32[64,1]{0,1:T(1,128)} %param.13) | copy-start | bytes 772
  1.7 1.1 %copy-start = (f32[3,4,32,512]{3,2,1,0:T(8,128)S(1)}, f32[3,4,32,512]{3,2,1,0:T(8,128)}, u32[]{:S(2)}) copy-start(f32[3,4,32,512]{3,2,1,0:T(8,128)} %fluid.5) | copy-start | bytes 2359300
  2.8 0.7 copy-start.3
  4.1 16.8 %collective-permute-start = (f32[440,128]{1,0:T(8,128)S(1)}, f32[440,128]{1,0:T(8,128)S(1)}, u32[]{:S(2)}, u32[]{:S(2)}) collective-permute-start(f32[440,128]{1,0:T(8,128)S(1)} %get-tuple-element.27), channel_id=1, source_target_pairs={{0,4},{4,8},{8,12},{12,16},{16,20},{20,24},{24,28},{28,0},{1,5},{5... | collective-permute-start | bytes 675848 | tf_op jit(solution)/shard_map/ppermute | solution.py:675
  7.2 13.8 %collective-permute-start.1 = (f32[440,128]{1,0:T(8,128)S(1)}, f32[440,128]{1,0:T(8,128)S(1)}, u32[]{:S(2)}, u32[]{:S(2)}) collective-permute-start(f32[440,128]{1,0:T(8,128)S(1)} %get-tuple-element.28), channel_id=1, source_target_pairs={{0,28},{4,0},{8,4},{12,8},{16,12},{20,16},{24,20},{28,24},{1,29},{... | collective-permute-start | bytes 675848 | tf_op jit(solution)/shard_map/ppermute | solution.py:675
  10.3 10.7 %collective-permute-start.2 = (f32[104,128]{1,0:T(8,128)S(1)}, f32[104,128]{1,0:T(8,128)S(1)}, u32[]{:S(2)}, u32[]{:S(2)}) collective-permute-start(f32[104,128]{1,0:T(8,128)S(1)} %get-tuple-element.29), channel_id=1, source_target_pairs={{0,1},{1,2},{2,3},{3,0},{4,5},{5,6},{6,7},{7,4},{8,9},{9,10},{10,1... | collective-permute-start | bytes 159752 | tf_op jit(solution)/shard_map/ppermute | solution.py:675
  10.3 10.7 %collective-permute-start.3 = (f32[104,128]{1,0:T(8,128)S(1)}, f32[104,128]{1,0:T(8,128)S(1)}, u32[]{:S(2)}, u32[]{:S(2)}) collective-permute-start(f32[104,128]{1,0:T(8,128)S(1)} %get-tuple-element.30), channel_id=1, source_target_pairs={{0,3},{1,0},{2,1},{3,2},{4,7},{5,4},{6,5},{7,6},{8,11},{9,8},{10,9... | collective-permute-start | bytes 159752 | tf_op jit(solution)/shard_map/ppermute | solution.py:675
  28.9 8.0 %copy-start.1 = (f32[3,4,32,512]{3,2,1,0:T(8,128)S(1)}, f32[3,4,32,512]{3,2,1,0:T(8,128)}, u32[]{:S(2)}) copy-start(f32[3,4,32,512]{3,2,1,0:T(8,128)} %fluid.5) | copy-start | bytes 2359300
  28.9 4.3 %collective-permute-start.4 = (f32[168,128]{1,0:T(8,128)S(1)}, f32[168,128]{1,0:T(8,128)S(1)}, u32[]{:S(2)}, u32[]{:S(2)}) collective-permute-start(f32[168,128]{1,0:T(8,128)S(1)} %get-tuple-element.37), channel_id=1, source_target_pairs={{0,1},{1,2},{2,3},{3,0},{4,5},{5,6},{6,7},{7,4},{8,9},{9,10},{10,1... | collective-permute-start | bytes 258056 | tf_op jit(solution)/shard_map/ppermute | solution.py:675
  29.0 5.4 %collective-permute-start.5 = (f32[168,128]{1,0:T(8,128)S(1)}, f32[168,128]{1,0:T(8,128)S(1)}, u32[]{:S(2)}, u32[]{:S(2)}) collective-permute-start(f32[168,128]{1,0:T(8,128)S(1)} %get-tuple-element.38), channel_id=1, source_target_pairs={{0,2},{1,3},{2,0},{3,1},{4,6},{5,7},{6,4},{7,5},{8,10},{9,11},{10,... | collective-permute-start | bytes 258056 | tf_op jit(solution)/shard_map/ppermute | solution.py:675
  30.7 4.1 %collective-permute-start.6 = (f32[168,128]{1,0:T(8,128)S(1)}, f32[168,128]{1,0:T(8,128)S(1)}, u32[]{:S(2)}, u32[]{:S(2)}) collective-permute-start(f32[168,128]{1,0:T(8,128)S(1)} %get-tuple-element.39), channel_id=1, source_target_pairs={{0,3},{1,0},{2,1},{3,2},{4,7},{5,4},{6,5},{7,6},{8,11},{9,8},{10,9... | collective-permute-start | bytes 258056 | tf_op jit(solution)/shard_map/ppermute | solution.py:675
  34.8 5.8 %collective-permute-start.7 = (f32[224,128]{1,0:T(8,128)S(1)}, f32[224,128]{1,0:T(8,128)S(1)}, u32[]{:S(2)}, u32[]{:S(2)}) collective-permute-start(f32[224,128]{1,0:T(8,128)S(1)} %pad_maximum_fusion.1), channel_id=1, source_target_pairs={{0,28},{4,0},{8,4},{12,8},{16,12},{20,16},{24,20},{28,24},{1,29},{... | collective-permute-start | bytes 344072 | tf_op jit(solution)/shard_map/ppermute | solution.py:675
  36.7 8.3 %collective-permute-start.8 = (f32[224,128]{1,0:T(8,128)S(1)}, f32[224,128]{1,0:T(8,128)S(1)}, u32[]{:S(2)}, u32[]{:S(2)}) collective-permute-start(f32[224,128]{1,0:T(8,128)S(1)} %pad_maximum_fusion.2), channel_id=1, source_target_pairs={{0,4},{4,8},{8,12},{12,16},{16,20},{20,24},{24,28},{28,0},{1,5},{5... | collective-permute-start | bytes 344072 | tf_op jit(solution)/shard_map/ppermute | solution.py:675
  57.0 7.2 %collective-permute-start.9 = (f32[160,128]{1,0:T(8,128)S(1)}, f32[160,128]{1,0:T(8,128)S(1)}, u32[]{:S(2)}, u32[]{:S(2)}) collective-permute-start(f32[160,128]{1,0:T(8,128)S(1)} %get-tuple-element.42), channel_id=1, source_target_pairs={{0,4},{4,8},{8,12},{12,16},{16,20},{20,24},{24,28},{28,0},{1,5},{5... | collective-permute-start | bytes 245768 | tf_op jit(solution)/shard_map/ppermute | solution.py:675
  57.1 7.1 %collective-permute-start.10 = (f32[160,128]{1,0:T(8,128)S(1)}, f32[160,128]{1,0:T(8,128)S(1)}, u32[]{:S(2)}, u32[]{:S(2)}) collective-permute-start(f32[160,128]{1,0:T(8,128)S(1)} %get-tuple-element.45), channel_id=1, source_target_pairs={{0,28},{4,0},{8,4},{12,8},{16,12},{20,16},{24,20},{28,24},{1,29},{... | collective-permute-start | bytes 245768 | tf_op jit(solution)/shard_map/ppermute | solution.py:675
  64.2 2.2 %collective-permute-start.11 = (f32[120,128]{1,0:T(8,128)S(1)}, f32[120,128]{1,0:T(8,128)S(1)}, u32[]{:S(2)}, u32[]{:S(2)}) collective-permute-start(f32[120,128]{1,0:T(8,128)S(1)} %pad_maximum_fusion.5), channel_id=1, source_target_pairs={{0,3},{1,0},{2,1},{3,2},{4,7},{5,4},{6,5},{7,6},{8,11},{9,8},{10,9... | collective-permute-start | bytes 184328 | tf_op jit(solution)/shard_map/ppermute | solution.py:675
  64.3 4.9 %collective-permute-start.12 = (f32[120,128]{1,0:T(8,128)S(1)}, f32[120,128]{1,0:T(8,128)S(1)}, u32[]{:S(2)}, u32[]{:S(2)}) collective-permute-start(f32[120,128]{1,0:T(8,128)S(1)} %pad_maximum_fusion.6), channel_id=1, source_target_pairs={{0,2},{1,3},{2,0},{3,1},{4,6},{5,7},{6,4},{7,5},{8,10},{9,11},{10,... | collective-permute-start | bytes 184328 | tf_op jit(solution)/shard_map/ppermute | solution.py:675
  65.1 4.3 %collective-permute-start.13 = (f32[120,128]{1,0:T(8,128)S(1)}, f32[120,128]{1,0:T(8,128)S(1)}, u32[]{:S(2)}, u32[]{:S(2)}) collective-permute-start(f32[120,128]{1,0:T(8,128)S(1)} %pad_maximum_fusion.7), channel_id=1, source_target_pairs={{0,1},{1,2},{2,3},{3,0},{4,5},{5,6},{6,7},{7,4},{8,9},{9,10},{10,1... | collective-permute-start | bytes 184328 | tf_op jit(solution)/shard_map/ppermute | solution.py:675

commit v2 on v1

--- a/solution.py
+++ b/solution.py
@@ -328,7 +328,7 @@
 
 def ghost_contacts(nbrick, cap, partner_blocks, home_list, partner_list, plan, below,
                    above, before, after, home_side, own_sums, state, cell, spots, bounds,
-                   updated, *rest):
+                   updated, down, *rest):
     outgoings = rest[:nbrick]
     (rows, columns, values, sums, data, sorted_rows, tiles, homes, partners,
      home_ref, partner_ref, plan_ref, sems) = rest[nbrick:]
@@ -380,10 +380,12 @@
 
     chunk = rows_up(5 * cap + 1)
     flat = tiles.reshape(tiles.shape[0] * 8, width)
-    for ahead, outgoing in enumerate(outgoings):
+    for ahead in range(nbrick):
         target = brick_ahead(ahead, nbrick)
-        for side in range(3):
-            code, row = side * nbrick + target, side * chunk
+        for side, (outgoing, row) in enumerate(
+            ((down, ahead * chunk), (outgoings[ahead], 0), (outgoings[ahead], chunk))
+        ):
+            code = side * nbrick + target
             for c in range(5):
                 outgoing[row + c * cap : row + (c + 1) * cap, :] = flat[
                     pl.ds(code * (cap + 2) * 8 + c, cap, stride=8), :
@@ -543,14 +545,18 @@
     diffuse(flow, below, above, before, after, skip, diffused)
 
 
-def advance(nbrick, cap, above, below, start, fluid, diffused, fluid_next, table, answers_up,
-            answers_down, arrived, answers, total, flow, fresh_flow, base, goal, counts, sems):
+def advance(nbrick, cap, start, fluid, diffused, below, *rest):
+    above, rest = rest[:nbrick], rest[nbrick:]
+    fluid_next, table, answers_below = rest[:3]
+    answers_above, rest = rest[3 : 3 + nbrick], rest[3 + nbrick :]
+    arrived, answers, total, flow, fresh_flow, base, goal, counts, sems = rest
     reading = pltpu.make_async_copy(fluid, flow, sems.at[0])
     reading.start()
     chunk = rows_up(5 * cap + 1)
     back = rows_up(3 * cap)
     rows = nbrick * chunk
-    arrived[0:rows, :] = above[...]
+    for b, part in enumerate(above):
+        arrived[b * chunk : (b + 1) * chunk, :] = part[...]
     arrived[rows:, :] = below[...]
     starts = [i * chunk for i in range(2 * nbrick)]
     ends = [i * back for i in range(2 * nbrick)]
@@ -584,8 +590,9 @@
     writing = pltpu.make_async_copy(fresh_flow, fluid_next, sems.at[1])
     writing.start()
     sample(2 * nbrick, counts, arrived, (base, goal), cap, table, answers)
-    answers_up[...] = answers[0 : nbrick * back, :]
-    answers_down[...] = answers[nbrick * back :, :]
+    for b, part in enumerate(answers_above):
+        part[...] = answers[b * back : (b + 1) * back, :]
+    answers_below[...] = answers[nbrick * back :, :]
     writing.wait()
 
 
@@ -601,17 +608,19 @@
         part[...] = answers[b * back : (b + 1) * back, :]
 
 
-def relax(nbrick, cap, plan, updated, spots, *rest):
+def relax(nbrick, cap, plan, updated, spots, down, *rest):
     returneds = rest[:nbrick]
     velocity_next, picked, sorted_rows, tiles, plan_ref, sems = rest[nbrick:]
     copies = copy_all([(plan, plan_ref)], sems)
     nblocks, width = spots.shape
     back = rows_up(3 * cap)
     flat = tiles.reshape(tiles.shape[0] * 8, width)
-    for ahead, returned in enumerate(returneds):
+    for ahead in range(nbrick):
         target = brick_ahead(ahead, nbrick)
-        for side in range(3):
-            code, row = side * nbrick + target, side * back
+        for side, (returned, row) in enumerate(
+            ((down, ahead * back), (returneds[ahead], 0), (returneds[ahead], back))
+        ):
+            code = side * nbrick + target
             for c in range(3):
                 flat[pl.ds(code * (cap + 2) * 8 + c, cap, stride=8), :] = returned[
                     row + c * cap : row + (c + 1) * cap, :
@@ -679,7 +688,7 @@
 
     state = jnp.concatenate([positions, radii[None], velocities], axis=0)
     ghost_rows, chunks = planes * per, 3 * (nz // width)
-    up, down, right, left = call(
+    up, low, right, left = call(
         pack_kernel,
         [struct(ghost_rows + chunks * ny, width)] * 2 + [struct(ghost_rows + chunks * nx, width)] * 2,
         [SMEM] + [VMEM] * 2,
@@ -687,7 +696,7 @@
         "pack",
     )(ghost_list, state, fluid)
     below = shifted(up, "slab", 1)
-    above = shifted(down, "slab", -1)
+    above = shifted(low, "slab", -1)
     before = shifted(right, "brick", 1)
     after = shifted(left, "brick", -1)
 
@@ -717,9 +726,10 @@
         "own_contacts",
         contact_flops,
     )(tile_home, tile_partner, state, cell_of, routes.reshape(1, nblocks))
-    updated, *outgoing = call(
+    updated, down, *outgoing = call(
         functools.partial(ghost_contacts, nbrick, cap, 4 * per),
-        [struct(3, nblocks, width)] + [struct(3 * chunk, width)] * nbrick,
+        [struct(3, nblocks, width), struct(nbrick * chunk, width)]
+        + [struct(2 * chunk, width)] * nbrick,
         [HBM] * 2 + [ANY] + [VMEM] * 10,
         sides(4 * per)
         + [pltpu.VMEM(((nblocks + 1) * 16, width), f32)]
@@ -731,14 +741,14 @@
     )(tile_home, tile_partner, plan, below, above, before, after,
       home_side, sums, state, cell_of, spots, bounds)
 
-    crossed = [shifted(part, "brick", ahead) for ahead, part in enumerate(outgoing)]
-
-    def side(k):
-        return jnp.concatenate([part[k * chunk : (k + 1) * chunk] for part in crossed], axis=0)
-
-    from_above = shifted(side(0), "slab", -1)
-    from_below = shifted(side(2), "slab", 1)
-    crossed = side(1)
+    down = shifted(down, "slab", -1)
+    near = [shifted(part, "brick", ahead) for ahead, part in enumerate(outgoing)]
+    from_below = shifted(jnp.concatenate([part[chunk:] for part in near], axis=0), "slab", 1)
+    from_above = [
+        shifted(down[ahead * chunk : (ahead + 1) * chunk], "brick", ahead)
+        for ahead in range(nbrick)
+    ]
+    crossed = jnp.concatenate([part[:chunk] for part in near], axis=0)
 
     def places(count):
         return [ints(4 * list_stride(count, cap))] * 2 + [ints(4)]
@@ -754,15 +764,15 @@
         "first_deposit",
         block_flops * nblocks // 3,
     )(crossed, below, above, before, after, fluid)
-    fluid_next, table, answers_up, answers_down = call(
+    fluid_next, table, answers_below, *answers_above = call(
         functools.partial(advance, nbrick, cap),
         [
             struct(3, nx, ny, nz),
             struct(12 * columns, nz // 2, dtype=bf16),
             struct(nbrick * back, width),
-            struct(nbrick * back, width),
-        ],
-        [VMEM] * 3 + [HBM, VMEM],
+        ]
+        + [struct(back, width)] * nbrick,
+        [VMEM, HBM] + [VMEM] * (2 + nbrick),
         [
             pltpu.VMEM((2 * nbrick * chunk, width), f32),
             pltpu.VMEM((2 * nbrick * back, width), f32),
@@ -773,31 +783,34 @@
         + [pltpu.SemaphoreType.DMA((2,))],
         "advance",
         block_flops * nblocks,
-        places=[HBM] + [VMEM] * 3,
-    )(from_above, from_below, started, fluid, diffused)
-    answers_up = shifted(answers_up, "slab", 1)
-    answers_down = shifted(answers_down, "slab", -1)
+        places=[HBM] + [VMEM] * (2 + nbrick),
+    )(started, fluid, diffused, from_below, *from_above)
+    answers_below = shifted(answers_below, "slab", -1)
+    answers_above = [
+        shifted(part, "brick", -behind) for behind, part in enumerate(answers_above)
+    ]
+    returned_down = shifted(jnp.concatenate(answers_above, axis=0), "slab", 1)
     answers = call(
         functools.partial(last_sample, nbrick, cap),
         [struct(back, width)] * nbrick,
         [VMEM] * 2,
         [pltpu.VMEM((nbrick * back, width), f32)] + places(nbrick),
         "last_sample",
-        block_flops * nblocks // 4,
+        block_flops * nblocks // 64,
     )(crossed, table)
     returned = []
     for behind in range(nbrick):
         at = slice(behind * back, (behind + 1) * back)
-        part = jnp.concatenate([answers_up[at], answers[behind], answers_down[at]], axis=0)
+        part = jnp.concatenate([answers[behind], answers_below[at]], axis=0)
         returned.append(shifted(part, "brick", -behind))
     (velocity_next,) = call(
         functools.partial(relax, nbrick, cap),
         [struct(3, nblocks, width)],
-        [ANY] + [VMEM] * (2 + nbrick),
+        [ANY] + [VMEM] * (3 + nbrick),
         [block_tiles, block_tiles, chunk_tiles, plan_copy]
         + [pltpu.SemaphoreType.DMA((1,))],
         "relax",
-    )(plan, updated, spots, *returned)
+    )(plan, updated, spots, returned_down, *returned)
     return (jnp.transpose(velocity_next, (1, 0, 2)), fluid_next)
 
 

time: 73.8 us -> 74.6 us (1.011)
  starting transfers between devices: 18.8 us -> 24.4 us
  waiting for transfers between devices: 12.3 us -> 8.92 us
  Pallas kernels: 39 us -> 37.2 us
    ppermute x14 -> x20, starting transfers between devices: 18.8 us -> 24.4 us  [shifted(): lax.ppermute(x, axis, [(i, (i + step) % count) for i in range(count)])]
    ppermute x14 -> x20, waiting for transfers between devices: 12.3 us -> 8.92 us  [shifted(): lax.ppermute(x, axis, [(i, (i + step) % count) for i in range(count)])]
    pallas_call x1, Pallas kernels: 12 us -> 9.26 us  [on_device(): call(functools.partial(advance, nbrick, cap), [struct(3, nx, ny, nz), str...]
  transfers between devices with their start and end apart: 14 -> 20, of which waited for: 9 -> 3; matrix products, arithmetic and copies ran while one was open for 0% -> 0% of each run, Pallas kernels for 19% -> 20%
where the time goes in v2:
time: 74.6 us; the launch traced here: 74.3 us
  Pallas kernels  37.2 us (50%)
  starting transfers between devices  24.4 us (33%)
  waiting for transfers between devices  8.92 us (12%)
  local copies, waits for them, and re-layouts  1.85 us (2%)
  other arithmetic  1.04 us (1%)
  between operations  0.94 us (1%)
    ppermute x20, starting transfers between devices, shifted(): lax.ppermute(x, axis, [(i, (i + step) % count) for i in range(count)])  24.4 us
    pallas_call x1, Pallas kernels, on_device(): call(functools.partial(advance, nbrick, cap), [struct(3, nx, ny, nz), str...  9.26 us
    pallas_call x1, Pallas kernels, on_device(): call(functools.partial(own_contacts, cap, columns, nz), [struct((nblocks...  8.93 us
    ppermute x20, waiting for transfers between devices, shifted(): lax.ppermute(x, axis, [(i, (i + step) % count) for i in range(count)])  8.92 us
    pallas_call x1, Pallas kernels, on_device(): call(functools.partial(ghost_contacts, nbrick, cap, 4 * per), [struct(3,...  7.9 us
    pallas_call x1, Pallas kernels, on_device(): call(functools.partial(relax, nbrick, cap), [struct(3, nblocks, width)],...  4.48 us
    pallas_call x1, Pallas kernels, on_device(): call(functools.partial(first_deposit, nbrick, cap, ghost_rows), [struct(8...  3.45 us
    pallas_call x1, Pallas kernels, on_device(): call(functools.partial(last_sample, nbrick, cap), [struct(back, width)] *...  2.48 us
  transfers between devices with their start and end apart: 20, of which 3 were waited for; matrix products, arithmetic and copies ran while one was open for 0% of the time, Pallas kernels for 20%

profile of v2, /device:TPU:0, one launch (start us, length us, event | category | flops | bytes accessed | tf_op | source)
XLA Modules:
  0.0 74.3 jit_solution(13884139410928596496)
XLA Ops:
  0.7 1.0 %pad_maximum_fusion.state = f32[7,64,128]{2,1,0:T(8,128)S(1)} fusion(f32[3,64,128]{2,1,0:T(8,128)} %bitcast.6, f32[1,64,128]{2,1,0:T(8,128)} %bitcast.9, f32[3,64,128]{2,1,0:T(8,128)} %bitcast.7), kind=kLoop, calls=%fused_computation | loop fusion | flops 114688 | bytes 458752 | tf_op jit(solution)/shard_map/concatenate | solution.py:689
  1.7 1.1 %copy-done = f32[3,4,32,512]{3,2,1,0:T(8,128)S(1)} copy-done((f32[3,4,32,512]{3,2,1,0:T(8,128)S(1)}, f32[3,4,32,512]{3,2,1,0:T(8,128)}, u32[]{:S(2)}) %copy-start) | copy-done | bytes 786456
  3.5 0.7 pack.1
  4.1 3.0 %collective-permute-start = (f32[440,128]{1,0:T(8,128)S(1)}, f32[440,128]{1,0:T(8,128)S(1)}, u32[]{:S(2)}, u32[]{:S(2)}) collective-permute-start(f32[440,128]{1,0:T(8,128)S(1)} %get-tuple-element.31), channel_id=1, source_target_pairs={{0,4},{4,8},{8,12},{12,16},{16,20},{20,24},{24,28},{28,0},{1,5},{5... | collective-permute-start | bytes 675848 | tf_op jit(solution)/shard_map/ppermute | solution.py:684
  7.2 3.1 %collective-permute-start.1 = (f32[440,128]{1,0:T(8,128)S(1)}, f32[440,128]{1,0:T(8,128)S(1)}, u32[]{:S(2)}, u32[]{:S(2)}) collective-permute-start(f32[440,128]{1,0:T(8,128)S(1)} %get-tuple-element.32), channel_id=1, source_target_pairs={{0,28},{4,0},{8,4},{12,8},{16,12},{20,16},{24,20},{28,24},{1,29},{... | collective-permute-start | bytes 675848 | tf_op jit(solution)/shard_map/ppermute | solution.py:684
  10.3 1.7 %collective-permute-start.3 = (f32[104,128]{1,0:T(8,128)S(1)}, f32[104,128]{1,0:T(8,128)S(1)}, u32[]{:S(2)}, u32[]{:S(2)}) collective-permute-start(f32[104,128]{1,0:T(8,128)S(1)} %get-tuple-element.34), channel_id=1, source_target_pairs={{0,3},{1,0},{2,1},{3,2},{4,7},{5,4},{6,5},{7,6},{8,11},{9,8},{10,9... | collective-permute-start | bytes 159752 | tf_op jit(solution)/shard_map/ppermute | solution.py:684
  12.0 8.9 %own_contacts.1 = (f32[2080,128]{1,0:T(8,128)S(1)}, f32[1040,128]{1,0:T(8,128)S(1)}, f32[64,128]{1,0:T(8,128)S(1)}, s32[64,128]{1,0:T(8,128)S(1)}, f32[16,128]{1,0:T(8,128)S(1)}) custom-call(s32[128]{0:T(128)S(1)} %copy-done.4, s32[128]{0:T(128)S(1)} %copy-done.5, f32[7,64,128]{2,1,0:T(8,128)S(1)} %pad_maximum_fusion.state, s32[64,128]{1,0:T(8,128)S(1)} %copy-done.2, ...), custom_call_target="tpu_custom_call" | custom-call | flops 419430400 | bytes 1048576 | tf_op jit(solution)/shard_map/own_contacts/pallas_call | solution.py:715
  21.0 7.9 %ghost_contacts.1 = (f32[3,64,128]{2,1,0:T(8,128)S(1)}, f32[224,128]{1,0:T(8,128)S(1)}, f32[112,128]{1,0:T(8,128)S(1)}, f32[112,128]{1,0:T(8,128)S(1)}, f32[112,128]{1,0:T(8,128)S(1)}, /*index=5*/f32[112,128]{1,0:T(8,128)S(1)}) custom-call(s32[128]{0:T(128)S(1)} %copy-done.4, s32[128]{0:T(128)S(1)} %copy-done.5, s32[64,128]{1,0:T(8,128)S(1)} %get-tuple-element.30.plan, ...), custom_call_target="tpu_custom_call" | custom-call | flops 209715200 | bytes 1048576 | tf_op jit(solution)/shard_map/ghost_contacts/pallas_call | solution.py:729
  29.0 1.7 %collective-permute-start.5 = (f32[112,128]{1,0:T(8,128)S(1)}, f32[112,128]{1,0:T(8,128)S(1)}, u32[]{:S(2)}, u32[]{:S(2)}) collective-permute-start(f32[112,128]{1,0:T(8,128)S(1)} %get-tuple-element.42), channel_id=1, source_target_pairs={{0,2},{1,3},{2,0},{3,1},{4,6},{5,7},{6,4},{7,5},{8,10},{9,11},{10,... | collective-permute-start | bytes 172040 | tf_op jit(solution)/shard_map/ppermute | solution.py:684
  30.7 1.4 %collective-permute-start.6 = (f32[112,128]{1,0:T(8,128)S(1)}, f32[112,128]{1,0:T(8,128)S(1)}, u32[]{:S(2)}, u32[]{:S(2)}) collective-permute-start(f32[112,128]{1,0:T(8,128)S(1)} %get-tuple-element.43), channel_id=1, source_target_pairs={{0,3},{1,0},{2,1},{3,2},{4,7},{5,4},{6,5},{7,6},{8,11},{9,8},{10,9... | collective-permute-start | bytes 172040 | tf_op jit(solution)/shard_map/ppermute | solution.py:684
  32.0 1.9 %collective-permute-start.8 = (f32[224,128]{1,0:T(8,128)S(1)}, f32[224,128]{1,0:T(8,128)S(1)}, u32[]{:S(2)}, u32[]{:S(2)}) collective-permute-start(f32[224,128]{1,0:T(8,128)S(1)} %get-tuple-element.46), channel_id=1, source_target_pairs={{0,28},{4,0},{8,4},{12,8},{16,12},{20,16},{24,20},{28,24},{1,29},{... | collective-permute-start | bytes 344072 | tf_op jit(solution)/shard_map/ppermute | solution.py:684
  34.2 2.6 %collective-permute-done.8 = f32[224,128]{1,0:T(8,128)S(1)} collective-permute-done((f32[224,128]{1,0:T(8,128)S(1)}, f32[224,128]{1,0:T(8,128)S(1)}, u32[]{:S(2)}, u32[]{:S(2)}) %collective-permute-start.8) | collective-permute-done | bytes 114720 | tf_op jit(solution)/shard_map/ppermute | solution.py:684
  36.9 0.7 collective-permute-start.10
  37.8 3.5 %first_deposit.1 = (f32[1024,256]{1,0:T(8,128)S(1)}, f32[3,4,32,512]{3,2,1,0:T(8,128)S(1)}) custom-call(f32[224,128]{1,0:T(8,128)S(1)} %pad_maximum_fusion.1.crossed, f32[440,128]{1,0:T(8,128)S(1)} %collective-permute-done.below, f32[440,128]{1,0:T(8,128)S(1)} %collective-permute-done.1.above, f32[104,128]{1,0:T(8,128)S(1)} %collective-permute-done.2.before, ...), custom_call_target="tpu_custom_call" | custom-call | flops 1431655808 | bytes 1048576 | tf_op jit(solution)/shard_map/first_deposit/pallas_call | solution.py:757
  41.3 1.0 %collective-permute-done.7.below = f32[224,128]{1,0:T(8,128)S(1)} collective-permute-done((f32[224,128]{1,0:T(8,128)S(1)}, f32[224,128]{1,0:T(8,128)S(1)}, u32[]{:S(2)}, u32[]{:S(2)}) %collective-permute-start.7) | collective-permute-done | bytes 114720 | tf_op jit(solution)/shard_map/ppermute | solution.py:684
  42.3 9.3 %advance.1 = (f32[3,4,32,512]{3,2,1,0:T(8,128)}, bf16[1536,256]{1,0:T(8,128)(2,1)S(1)}, f32[160,128]{1,0:T(8,128)S(1)}, f32[40,128]{1,0:T(8,128)S(1)}, f32[40,12...) custom-call(f32[1024,256]{1,0:T(8,128)S(1)} %get-tuple-element.44.start, ...), custom_call_target="tpu_custom_call" | custom-call | flops 4294967296 | bytes 1048576 | tf_op jit(solution)/shard_map/advance/pallas_call | solution.py:767
  51.5 1.6 %collective-permute-start.12 = (f32[40,128]{1,0:T(8,128)S(1)}, f32[40,128]{1,0:T(8,128)S(1)}, u32[]{:S(2)}, u32[]{:S(2)}) collective-permute-start(f32[40,128]{1,0:T(8,128)S(1)} %get-tuple-element.48), channel_id=1, source_target_pairs={{0,3},{1,0},{2,1},{3,2},{4,7},{5,4},{6,5},{7,6},{8,11},{9,8},{10,9... | collective-permute-start | bytes 61448 | tf_op jit(solution)/shard_map/ppermute | solution.py:684
  53.1 3.1 %collective-permute-start.13 = (f32[40,128]{1,0:T(8,128)S(1)}, f32[40,128]{1,0:T(8,128)S(1)}, u32[]{:S(2)}, u32[]{:S(2)}) collective-permute-start(f32[40,128]{1,0:T(8,128)S(1)} %get-tuple-element.49), channel_id=1, source_target_pairs={{0,2},{1,3},{2,0},{3,1},{4,6},{5,7},{6,4},{7,5},{8,10},{9,11},{10,... | collective-permute-start | bytes 61448 | tf_op jit(solution)/shard_map/ppermute | solution.py:684
  56.4 2.8 %collective-permute-start.16 = (f32[160,128]{1,0:T(8,128)S(1)}, f32[160,128]{1,0:T(8,128)S(1)}, u32[]{:S(2)}, u32[]{:S(2)}) collective-permute-start(f32[160,128]{1,0:T(8,128)S(1)} %get-tuple-element.53), channel_id=1, source_target_pairs={{0,28},{4,0},{8,4},{12,8},{16,12},{20,16},{24,20},{28,24},{1,29},{... | collective-permute-start | bytes 245768 | tf_op jit(solution)/shard_map/ppermute | solution.py:684
  59.2 2.5 %last_sample.1 = (f32[40,128]{1,0:T(8,128)S(1)}, f32[40,128]{1,0:T(8,128)S(1)}, f32[40,128]{1,0:T(8,128)S(1)}, f32[40,128]{1,0:T(8,128)S(1)}) custom-call(f32[224,128]{1,0:T(8,128)S(1)} %pad_maximum_fusion.1.crossed, bf16[1536,256]{1,0:T(8,128)(2,1)S(1)} %get-tuple-element.51.table), custom_call_target="tpu_custom_call" | custom-call | flops 67108864 | bytes 1048576 | tf_op jit(solution)/shard_map/last_sample/pallas_call | solution.py:793
  61.9 0.9 %collective-permute-start.17 = (f32[80,128]{1,0:T(8,128)S(1)}, f32[80,128]{1,0:T(8,128)S(1)}, u32[]{:S(2)}, u32[]{:S(2)}) collective-permute-start(f32[80,128]{1,0:T(8,128)S(1)} %pad_maximum_fusion.5), channel_id=1, source_target_pairs={{0,3},{1,0},{2,1},{3,2},{4,7},{5,4},{6,5},{7,6},{8,11},{9,8},{10,9... | collective-permute-start | bytes 122888 | tf_op jit(solution)/shard_map/ppermute | solution.py:684
  62.8 1.7 %collective-permute-start.18 = (f32[80,128]{1,0:T(8,128)S(1)}, f32[80,128]{1,0:T(8,128)S(1)}, u32[]{:S(2)}, u32[]{:S(2)}) collective-permute-start(f32[80,128]{1,0:T(8,128)S(1)} %pad_maximum_fusion.6), channel_id=1, source_target_pairs={{0,2},{1,3},{2,0},{3,1},{4,6},{5,7},{6,4},{7,5},{8,10},{9,11},{10,... | collective-permute-start | bytes 122888 | tf_op jit(solution)/shard_map/ppermute | solution.py:684
  64.6 5.3 %collective-permute-done.15.down = f32[160,128]{1,0:T(8,128)S(1)} collective-permute-done((f32[160,128]{1,0:T(8,128)S(1)}, f32[160,128]{1,0:T(8,128)S(1)}, u32[]{:S(2)}, u32[]{:S(2)}) %collective-permute-start.15) | collective-permute-done | bytes 81952 | tf_op jit(solution)/shard_map/ppermute | solution.py:684
  69.9 4.5 %relax.1 = f32[3,64,128]{2,1,0:T(8,128)} custom-call(s32[64,128]{1,0:T(8,128)S(1)} %get-tuple-element.30.plan, f32[3,64,128]{2,1,0:T(8,128)S(1)} %get-tuple-element.39.updated, f32[64,128]{1,0:T(8,128)S(1)} %get-tuple-element.37.spots, f32[160,128]{1,0:T(8,128)S(1)} %collective-permute-done.15.down, f32[80,128]{1,0:T(8,128)S(1)} %pad_maximum_fusion.4.rest_0_, ...), custom_call_target="tpu_custom_call" | custom-call | bytes 1048576 | tf_op jit(solution)/shard_map/relax/pallas_call | solution.py:806
  (51 shorter events, 1.5 us)
Async XLA Ops:
  0.6 11.4 %copy-start.5 = (s32[128]{0:T(128)S(1)}, s32[128]{0:T(128)}, u32[]{:S(2)}) copy-start(s32[128]{0:T(128)} %partner_list.3) | copy-start | bytes 1540
  0.6 11.4 %copy-start.4 = (s32[128]{0:T(128)S(1)}, s32[128]{0:T(128)}, u32[]{:S(2)}) copy-start(s32[128]{0:T(128)} %home_list.3) | copy-start | bytes 1540
  0.7 11.4 %copy-start.2 = (s32[64,128]{1,0:T(8,128)S(1)}, s32[64,128]{1,0:T(8,128)}, u32[]{:S(2)}) copy-start(s32[64,128]{1,0:T(8,128)} %cell.3) | copy-start | bytes 98308
  0.7 11.4 %copy-start.6 = (s32[64,1]{0,1:T(1,128)S(1)}, s32[64,1]{0,1:T(1,128)}, u32[]{:S(2)}) copy-start(s32[64,1]{0,1:T(1,128)} %param.13) | copy-start | bytes 772
  4.1 16.8 %collective-permute-start = (f32[440,128]{1,0:T(8,128)S(1)}, f32[440,128]{1,0:T(8,128)S(1)}, u32[]{:S(2)}, u32[]{:S(2)}) collective-permute-start(f32[440,128]{1,0:T(8,128)S(1)} %get-tuple-element.31), channel_id=1, source_target_pairs={{0,4},{4,8},{8,12},{12,16},{16,20},{20,24},{24,28},{28,0},{1,5},{5... | collective-permute-start | bytes 675848 | tf_op jit(solution)/shard_map/ppermute | solution.py:684
  7.2 13.8 %collective-permute-start.1 = (f32[440,128]{1,0:T(8,128)S(1)}, f32[440,128]{1,0:T(8,128)S(1)}, u32[]{:S(2)}, u32[]{:S(2)}) collective-permute-start(f32[440,128]{1,0:T(8,128)S(1)} %get-tuple-element.32), channel_id=1, source_target_pairs={{0,28},{4,0},{8,4},{12,8},{16,12},{20,16},{24,20},{28,24},{1,29},{... | collective-permute-start | bytes 675848 | tf_op jit(solution)/shard_map/ppermute | solution.py:684
  10.3 10.7 %collective-permute-start.2 = (f32[104,128]{1,0:T(8,128)S(1)}, f32[104,128]{1,0:T(8,128)S(1)}, u32[]{:S(2)}, u32[]{:S(2)}) collective-permute-start(f32[104,128]{1,0:T(8,128)S(1)} %get-tuple-element.33), channel_id=1, source_target_pairs={{0,1},{1,2},{2,3},{3,0},{4,5},{5,6},{6,7},{7,4},{8,9},{9,10},{10,1... | collective-permute-start | bytes 159752 | tf_op jit(solution)/shard_map/ppermute | solution.py:684
  10.3 10.7 %collective-permute-start.3 = (f32[104,128]{1,0:T(8,128)S(1)}, f32[104,128]{1,0:T(8,128)S(1)}, u32[]{:S(2)}, u32[]{:S(2)}) collective-permute-start(f32[104,128]{1,0:T(8,128)S(1)} %get-tuple-element.34), channel_id=1, source_target_pairs={{0,3},{1,0},{2,1},{3,2},{4,7},{5,4},{6,5},{7,6},{8,11},{9,8},{10,9... | collective-permute-start | bytes 159752 | tf_op jit(solution)/shard_map/ppermute | solution.py:684
  28.9 5.0 %collective-permute-start.4 = (f32[112,128]{1,0:T(8,128)S(1)}, f32[112,128]{1,0:T(8,128)S(1)}, u32[]{:S(2)}, u32[]{:S(2)}) collective-permute-start(f32[112,128]{1,0:T(8,128)S(1)} %get-tuple-element.41), channel_id=1, source_target_pairs={{0,1},{1,2},{2,3},{3,0},{4,5},{5,6},{6,7},{7,4},{8,9},{9,10},{10,1... | collective-permute-start | bytes 172040 | tf_op jit(solution)/shard_map/ppermute | solution.py:684
  29.0 4.9 %collective-permute-start.5 = (f32[112,128]{1,0:T(8,128)S(1)}, f32[112,128]{1,0:T(8,128)S(1)}, u32[]{:S(2)}, u32[]{:S(2)}) collective-permute-start(f32[112,128]{1,0:T(8,128)S(1)} %get-tuple-element.42), channel_id=1, source_target_pairs={{0,2},{1,3},{2,0},{3,1},{4,6},{5,7},{6,4},{7,5},{8,10},{9,11},{10,... | collective-permute-start | bytes 172040 | tf_op jit(solution)/shard_map/ppermute | solution.py:684
  30.7 3.3 %collective-permute-start.6 = (f32[112,128]{1,0:T(8,128)S(1)}, f32[112,128]{1,0:T(8,128)S(1)}, u32[]{:S(2)}, u32[]{:S(2)}) collective-permute-start(f32[112,128]{1,0:T(8,128)S(1)} %get-tuple-element.43), channel_id=1, source_target_pairs={{0,3},{1,0},{2,1},{3,2},{4,7},{5,4},{6,5},{7,6},{8,11},{9,8},{10,9... | collective-permute-start | bytes 172040 | tf_op jit(solution)/shard_map/ppermute | solution.py:684
  32.0 4.8 %collective-permute-start.8 = (f32[224,128]{1,0:T(8,128)S(1)}, f32[224,128]{1,0:T(8,128)S(1)}, u32[]{:S(2)}, u32[]{:S(2)}) collective-permute-start(f32[224,128]{1,0:T(8,128)S(1)} %get-tuple-element.46), channel_id=1, source_target_pairs={{0,28},{4,0},{8,4},{12,8},{16,12},{20,16},{24,20},{28,24},{1,29},{... | collective-permute-start | bytes 344072 | tf_op jit(solution)/shard_map/ppermute | solution.py:684
  34.0 8.3 %collective-permute-start.7 = (f32[224,128]{1,0:T(8,128)S(1)}, f32[224,128]{1,0:T(8,128)S(1)}, u32[]{:S(2)}, u32[]{:S(2)}) collective-permute-start(f32[224,128]{1,0:T(8,128)S(1)} %pad_maximum_fusion.2), channel_id=1, source_target_pairs={{0,4},{4,8},{8,12},{12,16},{16,20},{20,24},{24,28},{28,0},{1,5},{5... | collective-permute-start | bytes 344072 | tf_op jit(solution)/shard_map/ppermute | solution.py:684
  36.8 4.4 %collective-permute-start.11 = (f32[56,128]{1,0:T(8,128)S(1)}, f32[56,128]{1,0:T(8,128)S(1)}, u32[]{:S(2)}, u32[]{:S(2)}) collective-permute-start(f32[56,128]{1,0:T(8,128)S(1)} %get-tuple-element.58), channel_id=1, source_target_pairs={{0,3},{1,0},{2,1},{3,2},{4,7},{5,4},{6,5},{7,6},{8,11},{9,8},{10,9... | collective-permute-start | bytes 86024 | tf_op jit(solution)/shard_map/ppermute | solution.py:684
  36.9 4.4 %collective-permute-start.10 = (f32[56,128]{1,0:T(8,128)S(1)}, f32[56,128]{1,0:T(8,128)S(1)}, u32[]{:S(2)}, u32[]{:S(2)}) collective-permute-start(f32[56,128]{1,0:T(8,128)S(1)} %get-tuple-element.59), channel_id=1, source_target_pairs={{0,2},{1,3},{2,0},{3,1},{4,6},{5,7},{6,4},{7,5},{8,10},{9,11},{10,... | collective-permute-start | bytes 86024 | tf_op jit(solution)/shard_map/ppermute | solution.py:684
  37.6 3.7 %collective-permute-start.9 = (f32[56,128]{1,0:T(8,128)S(1)}, f32[56,128]{1,0:T(8,128)S(1)}, u32[]{:S(2)}, u32[]{:S(2)}) collective-permute-start(f32[56,128]{1,0:T(8,128)S(1)} %get-tuple-element.60), channel_id=1, source_target_pairs={{0,1},{1,2},{2,3},{3,0},{4,5},{5,6},{6,7},{7,4},{8,9},{9,10},{10,1... | collective-permute-start | bytes 86024 | tf_op jit(solution)/shard_map/ppermute | solution.py:684
  51.5 10.2 %collective-permute-start.12 = (f32[40,128]{1,0:T(8,128)S(1)}, f32[40,128]{1,0:T(8,128)S(1)}, u32[]{:S(2)}, u32[]{:S(2)}) collective-permute-start(f32[40,128]{1,0:T(8,128)S(1)} %get-tuple-element.48), channel_id=1, source_target_pairs={{0,3},{1,0},{2,1},{3,2},{4,7},{5,4},{6,5},{7,6},{8,11},{9,8},{10,9... | collective-permute-start | bytes 61448 | tf_op jit(solution)/shard_map/ppermute | solution.py:684
  53.1 8.6 %collective-permute-start.13 = (f32[40,128]{1,0:T(8,128)S(1)}, f32[40,128]{1,0:T(8,128)S(1)}, u32[]{:S(2)}, u32[]{:S(2)}) collective-permute-start(f32[40,128]{1,0:T(8,128)S(1)} %get-tuple-element.49), channel_id=1, source_target_pairs={{0,2},{1,3},{2,0},{3,1},{4,6},{5,7},{6,4},{7,5},{8,10},{9,11},{10,... | collective-permute-start | bytes 61448 | tf_op jit(solution)/shard_map/ppermute | solution.py:684
  56.3 5.5 %collective-permute-start.14 = (f32[40,128]{1,0:T(8,128)S(1)}, f32[40,128]{1,0:T(8,128)S(1)}, u32[]{:S(2)}, u32[]{:S(2)}) collective-permute-start(f32[40,128]{1,0:T(8,128)S(1)} %get-tuple-element.50), channel_id=1, source_target_pairs={{0,1},{1,2},{2,3},{3,0},{4,5},{5,6},{6,7},{7,4},{8,9},{9,10},{10,1... | collective-permute-start | bytes 61448 | tf_op jit(solution)/shard_map/ppermute | solution.py:684
  56.4 5.4 %collective-permute-start.16 = (f32[160,128]{1,0:T(8,128)S(1)}, f32[160,128]{1,0:T(8,128)S(1)}, u32[]{:S(2)}, u32[]{:S(2)}) collective-permute-start(f32[160,128]{1,0:T(8,128)S(1)} %get-tuple-element.53), channel_id=1, source_target_pairs={{0,28},{4,0},{8,4},{12,8},{16,12},{20,16},{24,20},{28,24},{1,29},{... | collective-permute-start | bytes 245768 | tf_op jit(solution)/shard_map/ppermute | solution.py:684
  61.8 8.1 %collective-permute-start.15 = (f32[160,128]{1,0:T(8,128)S(1)}, f32[160,128]{1,0:T(8,128)S(1)}, u32[]{:S(2)}, u32[]{:S(2)}) collective-permute-start(f32[160,128]{1,0:T(8,128)S(1)} %pad_maximum_fusion.3), channel_id=1, source_target_pairs={{0,4},{4,8},{8,12},{12,16},{16,20},{20,24},{24,28},{28,0},{1,5},{5... | collective-permute-start | bytes 245768 | tf_op jit(solution)/shard_map/ppermute | solution.py:684
  61.9 8.0 %collective-permute-start.17 = (f32[80,128]{1,0:T(8,128)S(1)}, f32[80,128]{1,0:T(8,128)S(1)}, u32[]{:S(2)}, u32[]{:S(2)}) collective-permute-start(f32[80,128]{1,0:T(8,128)S(1)} %pad_maximum_fusion.5), channel_id=1, source_target_pairs={{0,3},{1,0},{2,1},{3,2},{4,7},{5,4},{6,5},{7,6},{8,11},{9,8},{10,9... | collective-permute-start | bytes 122888 | tf_op jit(solution)/shard_map/ppermute | solution.py:684
  62.8 7.0 %collective-permute-start.18 = (f32[80,128]{1,0:T(8,128)S(1)}, f32[80,128]{1,0:T(8,128)S(1)}, u32[]{:S(2)}, u32[]{:S(2)}) collective-permute-start(f32[80,128]{1,0:T(8,128)S(1)} %pad_maximum_fusion.6), channel_id=1, source_target_pairs={{0,2},{1,3},{2,0},{3,1},{4,6},{5,7},{6,4},{7,5},{8,10},{9,11},{10,... | collective-permute-start | bytes 122888 | tf_op jit(solution)/shard_map/ppermute | solution.py:684
  64.5 5.3 %collective-permute-start.19 = (f32[80,128]{1,0:T(8,128)S(1)}, f32[80,128]{1,0:T(8,128)S(1)}, u32[]{:S(2)}, u32[]{:S(2)}) collective-permute-start(f32[80,128]{1,0:T(8,128)S(1)} %pad_maximum_fusion.7), channel_id=1, source_target_pairs={{0,1},{1,2},{2,3},{3,0},{4,5},{5,6},{6,7},{7,4},{8,9},{9,10},{10,1... | collective-permute-start | bytes 122888 | tf_op jit(solution)/shard_map/ppermute | solution.py:684
  (3 other events, 10.7 us)

commit v3 on v2

--- a/solution.py
+++ b/solution.py
@@ -20,7 +20,7 @@
 SMEM = pl.BlockSpec(memory_space=pltpu.SMEM)
 ANY = pl.BlockSpec(memory_space=pl.ANY)
 HBM = pl.BlockSpec(memory_space=pltpu.HBM)
-UNROLL = 8
+UNROLL = 16
 GROUP = 2
 
 
@@ -145,7 +145,7 @@
         columns[b] = jnp.transpose(block).astype(bf16)
         return 0
 
-    lax.fori_loop(0, count, turn, 0, unroll=4)
+    lax.fori_loop(0, count, turn, 0, unroll=8)
 
 
 def list_tiles(home_ref, partner_ref, homes, partners, lower, upper, spare):
@@ -274,8 +274,8 @@
             pltpu.store(tiles.at[tile + 1], moved, mask=lane < at + length - width)
         return 0
 
-    lax.fori_loop(0, nblocks, order, 0, unroll=8)
-    lax.fori_loop(0, nblocks, spread, 0, unroll=8)
+    lax.fori_loop(0, nblocks, order, 0, unroll=16)
+    lax.fori_loop(0, nblocks, spread, 0, unroll=16)
 
 
 def own_contacts(cap, columns, depth, home_list, partner_list, state, cell, route,
@@ -411,9 +411,16 @@
             next_edge = jnp.sum(jnp.where(lane == j, row, 0.0)).astype(jnp.int32)
             first = edge >> shift
             last = jnp.where(next_edge > edge, (next_edge + width - 1) >> shift, first)
-            for i in range(cap):
-                base[j * stride + filled[j] + i] = start + first + i
-                goal[j * stride + filled[j] + i] = end + first + i
+            at = j * stride + filled[j]
+
+            def put(some, at=at, first=first, start=start, end=end):
+                for i in some:
+                    base[at + i] = start + first + i
+                    goal[at + i] = end + first + i
+
+            few = min(4, cap)
+            put(range(few))
+            pl.when(last - first > few)(functools.partial(put, range(few, cap)))
             filled[j] = filled[j] + last - first
             edge = next_edge
     for j in range(4):
@@ -650,8 +657,8 @@
         picked[b] = both[0:8] + both[8:16]
         return 0
 
-    lax.fori_loop(0, nblocks, gather, 0, unroll=8)
-    lax.fori_loop(0, nblocks, order, 0, unroll=8)
+    lax.fori_loop(0, nblocks, gather, 0, unroll=16)
+    lax.fori_loop(0, nblocks, order, 0, unroll=16)
     flat = picked.reshape(nblocks * 8, width)
     for c in range(3):
         now = updated[c]

time: 74.6 us -> 72.8 us (0.976)
  Pallas kernels: 37.2 us -> 35.5 us
    pallas_call x1, Pallas kernels: 8.93 us -> 7.26 us  [on_device(): call(functools.partial(own_contacts, cap, columns, nz), [struct((nblocks...]
    pallas_call x1, Pallas kernels: 3.45 us -> 4.96 us  [on_device(): call(functools.partial(first_deposit, nbrick, cap, ghost_rows), [struct(8...]
    pallas_call x1, Pallas kernels: 7.9 us -> 6.64 us  [on_device(): call(functools.partial(ghost_contacts, nbrick, cap, 4 * per), [struct(3,...]
    pallas_call x1, Pallas kernels: 2.48 us -> 3.71 us  [on_device(): call(functools.partial(last_sample, nbrick, cap), [struct(back, width)] *...]
    pallas_call x1, Pallas kernels: 9.26 us -> 8.41 us  [on_device(): call(functools.partial(advance, nbrick, cap), [struct(3, nx, ny, nz), str...]
  transfers between devices with their start and end apart: 20 -> 20, of which waited for: 3 -> 2; matrix products, arithmetic and copies ran while one was open for 0% -> 0% of each run, Pallas kernels for 20% -> 22%
where the time goes in v3:
time: 72.8 us; the launch traced here: 73.1 us
  Pallas kernels  35.5 us (49%)
  starting transfers between devices  25.1 us (34%)
  waiting for transfers between devices  8.58 us (12%)
  local copies, waits for them, and re-layouts  1.85 us (3%)
  other arithmetic  1.04 us (1%)
  between operations  0.96 us (1%)
    ppermute x20, starting transfers between devices, shifted(): lax.ppermute(x, axis, [(i, (i + step) % count) for i in range(count)])  25.1 us
    ppermute x20, waiting for transfers between devices, shifted(): lax.ppermute(x, axis, [(i, (i + step) % count) for i in range(count)])  8.58 us
    pallas_call x1, Pallas kernels, on_device(): call(functools.partial(advance, nbrick, cap), [struct(3, nx, ny, nz), str...  8.41 us
    pallas_call x1, Pallas kernels, on_device(): call(functools.partial(own_contacts, cap, columns, nz), [struct((nblocks...  7.26 us
    pallas_call x1, Pallas kernels, on_device(): call(functools.partial(ghost_contacts, nbrick, cap, 4 * per), [struct(3,...  6.64 us
    pallas_call x1, Pallas kernels, on_device(): call(functools.partial(first_deposit, nbrick, cap, ghost_rows), [struct(8...  4.96 us
    pallas_call x1, Pallas kernels, on_device(): call(functools.partial(relax, nbrick, cap), [struct(3, nblocks, width)],...  3.87 us
    pallas_call x1, Pallas kernels, on_device(): call(functools.partial(last_sample, nbrick, cap), [struct(back, width)] *...  3.71 us
  transfers between devices with their start and end apart: 20, of which 2 were waited for; matrix products, arithmetic and copies ran while one was open for 0% of the time, Pallas kernels for 22%

profile of v3, /device:TPU:0, one launch (start us, length us, event | category | flops | bytes accessed | tf_op | source)
XLA Modules:
  0.0 73.1 jit_solution(7842694136510927976)
XLA Ops:
  0.7 1.0 %pad_maximum_fusion.state = f32[7,64,128]{2,1,0:T(8,128)S(1)} fusion(f32[3,64,128]{2,1,0:T(8,128)} %bitcast.6, f32[1,64,128]{2,1,0:T(8,128)} %bitcast.9, f32[3,64,128]{2,1,0:T(8,128)} %bitcast.7), kind=kLoop, calls=%fused_computation | loop fusion | flops 114688 | bytes 458752 | tf_op jit(solution)/shard_map/concatenate | solution.py:696
  1.7 1.1 %copy-done = f32[3,4,32,512]{3,2,1,0:T(8,128)S(1)} copy-done((f32[3,4,32,512]{3,2,1,0:T(8,128)S(1)}, f32[3,4,32,512]{3,2,1,0:T(8,128)}, u32[]{:S(2)}) %copy-start) | copy-done | bytes 786456
  2.8 0.7 copy-done.3
  3.5 0.7 pack.1
  4.1 3.0 %collective-permute-start = (f32[440,128]{1,0:T(8,128)S(1)}, f32[440,128]{1,0:T(8,128)S(1)}, u32[]{:S(2)}, u32[]{:S(2)}) collective-permute-start(f32[440,128]{1,0:T(8,128)S(1)} %get-tuple-element.31), channel_id=1, source_target_pairs={{0,4},{4,8},{8,12},{12,16},{16,20},{20,24},{24,28},{28,0},{1,5},{5... | collective-permute-start | bytes 675848 | tf_op jit(solution)/shard_map/ppermute | solution.py:691
  7.2 3.1 %collective-permute-start.1 = (f32[440,128]{1,0:T(8,128)S(1)}, f32[440,128]{1,0:T(8,128)S(1)}, u32[]{:S(2)}, u32[]{:S(2)}) collective-permute-start(f32[440,128]{1,0:T(8,128)S(1)} %get-tuple-element.32), channel_id=1, source_target_pairs={{0,28},{4,0},{8,4},{12,8},{16,12},{20,16},{24,20},{28,24},{1,29},{... | collective-permute-start | bytes 675848 | tf_op jit(solution)/shard_map/ppermute | solution.py:691
  10.3 1.7 %collective-permute-start.3 = (f32[104,128]{1,0:T(8,128)S(1)}, f32[104,128]{1,0:T(8,128)S(1)}, u32[]{:S(2)}, u32[]{:S(2)}) collective-permute-start(f32[104,128]{1,0:T(8,128)S(1)} %get-tuple-element.34), channel_id=1, source_target_pairs={{0,3},{1,0},{2,1},{3,2},{4,7},{5,4},{6,5},{7,6},{8,11},{9,8},{10,9... | collective-permute-start | bytes 159752 | tf_op jit(solution)/shard_map/ppermute | solution.py:691
  12.0 7.3 %own_contacts.1 = (f32[2080,128]{1,0:T(8,128)S(1)}, f32[1040,128]{1,0:T(8,128)S(1)}, f32[64,128]{1,0:T(8,128)S(1)}, s32[64,128]{1,0:T(8,128)S(1)}, f32[16,128]{1,0:T(8,128)S(1)}) custom-call(s32[128]{0:T(128)S(1)} %copy-done.4, s32[128]{0:T(128)S(1)} %copy-done.5, f32[7,64,128]{2,1,0:T(8,128)S(1)} %pad_maximum_fusion.state, s32[64,128]{1,0:T(8,128)S(1)} %copy-done.2, ...), custom_call_target="tpu_custom_call" | custom-call | flops 419430400 | bytes 1048576 | tf_op jit(solution)/shard_map/own_contacts/pallas_call | solution.py:722
  19.3 6.6 %ghost_contacts.1 = (f32[3,64,128]{2,1,0:T(8,128)S(1)}, f32[224,128]{1,0:T(8,128)S(1)}, f32[112,128]{1,0:T(8,128)S(1)}, f32[112,128]{1,0:T(8,128)S(1)}, f32[112,128]{1,0:T(8,128)S(1)}, /*index=5*/f32[112,128]{1,0:T(8,128)S(1)}) custom-call(s32[128]{0:T(128)S(1)} %copy-done.4, s32[128]{0:T(128)S(1)} %copy-done.5, s32[64,128]{1,0:T(8,128)S(1)} %get-tuple-element.30.plan, ...), custom_call_target="tpu_custom_call" | custom-call | flops 209715200 | bytes 1048576 | tf_op jit(solution)/shard_map/ghost_contacts/pallas_call | solution.py:736
  26.1 1.7 %collective-permute-start.5 = (f32[112,128]{1,0:T(8,128)S(1)}, f32[112,128]{1,0:T(8,128)S(1)}, u32[]{:S(2)}, u32[]{:S(2)}) collective-permute-start(f32[112,128]{1,0:T(8,128)S(1)} %get-tuple-element.42), channel_id=1, source_target_pairs={{0,2},{1,3},{2,0},{3,1},{4,6},{5,7},{6,4},{7,5},{8,10},{9,11},{10,... | collective-permute-start | bytes 172040 | tf_op jit(solution)/shard_map/ppermute | solution.py:691
  27.7 1.4 %collective-permute-start.6 = (f32[112,128]{1,0:T(8,128)S(1)}, f32[112,128]{1,0:T(8,128)S(1)}, u32[]{:S(2)}, u32[]{:S(2)}) collective-permute-start(f32[112,128]{1,0:T(8,128)S(1)} %get-tuple-element.43), channel_id=1, source_target_pairs={{0,3},{1,0},{2,1},{3,2},{4,7},{5,4},{6,5},{7,6},{8,11},{9,8},{10,9... | collective-permute-start | bytes 172040 | tf_op jit(solution)/shard_map/ppermute | solution.py:691
  29.1 2.8 %collective-permute-start.8 = (f32[224,128]{1,0:T(8,128)S(1)}, f32[224,128]{1,0:T(8,128)S(1)}, u32[]{:S(2)}, u32[]{:S(2)}) collective-permute-start(f32[224,128]{1,0:T(8,128)S(1)} %get-tuple-element.46), channel_id=1, source_target_pairs={{0,28},{4,0},{8,4},{12,8},{16,12},{20,16},{24,20},{28,24},{1,29},{... | collective-permute-start | bytes 344072 | tf_op jit(solution)/shard_map/ppermute | solution.py:691
  32.1 2.2 %collective-permute-done.8 = f32[224,128]{1,0:T(8,128)S(1)} collective-permute-done((f32[224,128]{1,0:T(8,128)S(1)}, f32[224,128]{1,0:T(8,128)S(1)}, u32[]{:S(2)}, u32[]{:S(2)}) %collective-permute-start.8) | collective-permute-done | bytes 114720 | tf_op jit(solution)/shard_map/ppermute | solution.py:691
  34.4 0.7 collective-permute-start.10
  35.2 5.0 %first_deposit.1 = (f32[1024,256]{1,0:T(8,128)S(1)}, f32[3,4,32,512]{3,2,1,0:T(8,128)S(1)}) custom-call(f32[224,128]{1,0:T(8,128)S(1)} %pad_maximum_fusion.1.crossed, f32[440,128]{1,0:T(8,128)S(1)} %collective-permute-done.below, f32[440,128]{1,0:T(8,128)S(1)} %collective-permute-done.1.above, f32[104,128]{1,0:T(8,128)S(1)} %collective-permute-done.2.before, ...), custom_call_target="tpu_custom_call" | custom-call | flops 1431655808 | bytes 1048576 | tf_op jit(solution)/shard_map/first_deposit/pallas_call | solution.py:764
  40.2 8.4 %advance.1 = (f32[3,4,32,512]{3,2,1,0:T(8,128)}, bf16[1536,256]{1,0:T(8,128)(2,1)S(1)}, f32[160,128]{1,0:T(8,128)S(1)}, f32[40,128]{1,0:T(8,128)S(1)}, f32[40,12...) custom-call(f32[1024,256]{1,0:T(8,128)S(1)} %get-tuple-element.44.start, ...), custom_call_target="tpu_custom_call" | custom-call | flops 4294967296 | bytes 1048576 | tf_op jit(solution)/shard_map/advance/pallas_call | solution.py:774
  48.6 0.6 collective-permute-start.12
  49.3 3.3 %collective-permute-start.13 = (f32[40,128]{1,0:T(8,128)S(1)}, f32[40,128]{1,0:T(8,128)S(1)}, u32[]{:S(2)}, u32[]{:S(2)}) collective-permute-start(f32[40,128]{1,0:T(8,128)S(1)} %get-tuple-element.49), channel_id=1, source_target_pairs={{0,2},{1,3},{2,0},{3,1},{4,6},{5,7},{6,4},{7,5},{8,10},{9,11},{10,... | collective-permute-start | bytes 61448 | tf_op jit(solution)/shard_map/ppermute | solution.py:691
  52.6 5.6 %collective-permute-start.16 = (f32[160,128]{1,0:T(8,128)S(1)}, f32[160,128]{1,0:T(8,128)S(1)}, u32[]{:S(2)}, u32[]{:S(2)}) collective-permute-start(f32[160,128]{1,0:T(8,128)S(1)} %get-tuple-element.53), channel_id=1, source_target_pairs={{0,28},{4,0},{8,4},{12,8},{16,12},{20,16},{24,20},{28,24},{1,29},{... | collective-permute-start | bytes 245768 | tf_op jit(solution)/shard_map/ppermute | solution.py:691
  58.2 3.7 %last_sample.1 = (f32[40,128]{1,0:T(8,128)S(1)}, f32[40,128]{1,0:T(8,128)S(1)}, f32[40,128]{1,0:T(8,128)S(1)}, f32[40,128]{1,0:T(8,128)S(1)}) custom-call(f32[224,128]{1,0:T(8,128)S(1)} %pad_maximum_fusion.1.crossed, bf16[1536,256]{1,0:T(8,128)(2,1)S(1)} %get-tuple-element.51.table), custom_call_target="tpu_custom_call" | custom-call | flops 67108864 | bytes 1048576 | tf_op jit(solution)/shard_map/last_sample/pallas_call | solution.py:800
  62.1 0.3 collective-permute-start.17
  62.4 0.4 collective-permute-start.18
  62.9 6.3 %collective-permute-done.15.down = f32[160,128]{1,0:T(8,128)S(1)} collective-permute-done((f32[160,128]{1,0:T(8,128)S(1)}, f32[160,128]{1,0:T(8,128)S(1)}, u32[]{:S(2)}, u32[]{:S(2)}) %collective-permute-start.15) | collective-permute-done | bytes 81952 | tf_op jit(solution)/shard_map/ppermute | solution.py:691
  69.2 3.9 %relax.1 = f32[3,64,128]{2,1,0:T(8,128)} custom-call(s32[64,128]{1,0:T(8,128)S(1)} %get-tuple-element.30.plan, f32[3,64,128]{2,1,0:T(8,128)S(1)} %get-tuple-element.39.updated, f32[64,128]{1,0:T(8,128)S(1)} %get-tuple-element.37.spots, f32[160,128]{1,0:T(8,128)S(1)} %collective-permute-done.15.down, f32[80,128]{1,0:T(8,128)S(1)} %pad_maximum_fusion.4.rest_0_, ...), custom_call_target="tpu_custom_call" | custom-call | bytes 1048576 | tf_op jit(solution)/shard_map/relax/pallas_call | solution.py:813
  (51 shorter events, 0.6 us)
Async XLA Ops:
  0.6 11.4 %copy-start.5 = (s32[128]{0:T(128)S(1)}, s32[128]{0:T(128)}, u32[]{:S(2)}) copy-start(s32[128]{0:T(128)} %partner_list.3) | copy-start | bytes 1540
  0.6 11.4 %copy-start.4 = (s32[128]{0:T(128)S(1)}, s32[128]{0:T(128)}, u32[]{:S(2)}) copy-start(s32[128]{0:T(128)} %home_list.3) | copy-start | bytes 1540
  0.7 11.4 %copy-start.2 = (s32[64,128]{1,0:T(8,128)S(1)}, s32[64,128]{1,0:T(8,128)}, u32[]{:S(2)}) copy-start(s32[64,128]{1,0:T(8,128)} %cell.3) | copy-start | bytes 98308
  0.7 11.4 %copy-start.6 = (s32[64,1]{0,1:T(1,128)S(1)}, s32[64,1]{0,1:T(1,128)}, u32[]{:S(2)}) copy-start(s32[64,1]{0,1:T(1,128)} %param.13) | copy-start | bytes 772
  4.1 15.2 %collective-permute-start = (f32[440,128]{1,0:T(8,128)S(1)}, f32[440,128]{1,0:T(8,128)S(1)}, u32[]{:S(2)}, u32[]{:S(2)}) collective-permute-start(f32[440,128]{1,0:T(8,128)S(1)} %get-tuple-element.31), channel_id=1, source_target_pairs={{0,4},{4,8},{8,12},{12,16},{16,20},{20,24},{24,28},{28,0},{1,5},{5... | collective-permute-start | bytes 675848 | tf_op jit(solution)/shard_map/ppermute | solution.py:691
  7.2 12.2 %collective-permute-start.1 = (f32[440,128]{1,0:T(8,128)S(1)}, f32[440,128]{1,0:T(8,128)S(1)}, u32[]{:S(2)}, u32[]{:S(2)}) collective-permute-start(f32[440,128]{1,0:T(8,128)S(1)} %get-tuple-element.32), channel_id=1, source_target_pairs={{0,28},{4,0},{8,4},{12,8},{16,12},{20,16},{24,20},{28,24},{1,29},{... | collective-permute-start | bytes 675848 | tf_op jit(solution)/shard_map/ppermute | solution.py:691
  10.3 9.0 %collective-permute-start.2 = (f32[104,128]{1,0:T(8,128)S(1)}, f32[104,128]{1,0:T(8,128)S(1)}, u32[]{:S(2)}, u32[]{:S(2)}) collective-permute-start(f32[104,128]{1,0:T(8,128)S(1)} %get-tuple-element.33), channel_id=1, source_target_pairs={{0,1},{1,2},{2,3},{3,0},{4,5},{5,6},{6,7},{7,4},{8,9},{9,10},{10,1... | collective-permute-start | bytes 159752 | tf_op jit(solution)/shard_map/ppermute | solution.py:691
  10.3 9.0 %collective-permute-start.3 = (f32[104,128]{1,0:T(8,128)S(1)}, f32[104,128]{1,0:T(8,128)S(1)}, u32[]{:S(2)}, u32[]{:S(2)}) collective-permute-start(f32[104,128]{1,0:T(8,128)S(1)} %get-tuple-element.34), channel_id=1, source_target_pairs={{0,3},{1,0},{2,1},{3,2},{4,7},{5,4},{6,5},{7,6},{8,11},{9,8},{10,9... | collective-permute-start | bytes 159752 | tf_op jit(solution)/shard_map/ppermute | solution.py:691
  26.0 6.0 %collective-permute-start.4 = (f32[112,128]{1,0:T(8,128)S(1)}, f32[112,128]{1,0:T(8,128)S(1)}, u32[]{:S(2)}, u32[]{:S(2)}) collective-permute-start(f32[112,128]{1,0:T(8,128)S(1)} %get-tuple-element.41), channel_id=1, source_target_pairs={{0,1},{1,2},{2,3},{3,0},{4,5},{5,6},{6,7},{7,4},{8,9},{9,10},{10,1... | collective-permute-start | bytes 172040 | tf_op jit(solution)/shard_map/ppermute | solution.py:691
  26.1 5.9 %collective-permute-start.5 = (f32[112,128]{1,0:T(8,128)S(1)}, f32[112,128]{1,0:T(8,128)S(1)}, u32[]{:S(2)}, u32[]{:S(2)}) collective-permute-start(f32[112,128]{1,0:T(8,128)S(1)} %get-tuple-element.42), channel_id=1, source_target_pairs={{0,2},{1,3},{2,0},{3,1},{4,6},{5,7},{6,4},{7,5},{8,10},{9,11},{10,... | collective-permute-start | bytes 172040 | tf_op jit(solution)/shard_map/ppermute | solution.py:691
  27.7 4.3 %collective-permute-start.6 = (f32[112,128]{1,0:T(8,128)S(1)}, f32[112,128]{1,0:T(8,128)S(1)}, u32[]{:S(2)}, u32[]{:S(2)}) collective-permute-start(f32[112,128]{1,0:T(8,128)S(1)} %get-tuple-element.43), channel_id=1, source_target_pairs={{0,3},{1,0},{2,1},{3,2},{4,7},{5,4},{6,5},{7,6},{8,11},{9,8},{10,9... | collective-permute-start | bytes 172040 | tf_op jit(solution)/shard_map/ppermute | solution.py:691
  29.1 5.2 %collective-permute-start.8 = (f32[224,128]{1,0:T(8,128)S(1)}, f32[224,128]{1,0:T(8,128)S(1)}, u32[]{:S(2)}, u32[]{:S(2)}) collective-permute-start(f32[224,128]{1,0:T(8,128)S(1)} %get-tuple-element.46), channel_id=1, source_target_pairs={{0,28},{4,0},{8,4},{12,8},{16,12},{20,16},{24,20},{28,24},{1,29},{... | collective-permute-start | bytes 344072 | tf_op jit(solution)/shard_map/ppermute | solution.py:691
  32.0 8.2 %collective-permute-start.7 = (f32[224,128]{1,0:T(8,128)S(1)}, f32[224,128]{1,0:T(8,128)S(1)}, u32[]{:S(2)}, u32[]{:S(2)}) collective-permute-start(f32[224,128]{1,0:T(8,128)S(1)} %pad_maximum_fusion.2), channel_id=1, source_target_pairs={{0,4},{4,8},{8,12},{12,16},{16,20},{20,24},{24,28},{28,0},{1,5},{5... | collective-permute-start | bytes 344072 | tf_op jit(solution)/shard_map/ppermute | solution.py:691
  34.3 5.9 %collective-permute-start.11 = (f32[56,128]{1,0:T(8,128)S(1)}, f32[56,128]{1,0:T(8,128)S(1)}, u32[]{:S(2)}, u32[]{:S(2)}) collective-permute-start(f32[56,128]{1,0:T(8,128)S(1)} %get-tuple-element.58), channel_id=1, source_target_pairs={{0,3},{1,0},{2,1},{3,2},{4,7},{5,4},{6,5},{7,6},{8,11},{9,8},{10,9... | collective-permute-start | bytes 86024 | tf_op jit(solution)/shard_map/ppermute | solution.py:691
  34.4 5.8 %collective-permute-start.10 = (f32[56,128]{1,0:T(8,128)S(1)}, f32[56,128]{1,0:T(8,128)S(1)}, u32[]{:S(2)}, u32[]{:S(2)}) collective-permute-start(f32[56,128]{1,0:T(8,128)S(1)} %get-tuple-element.59), channel_id=1, source_target_pairs={{0,2},{1,3},{2,0},{3,1},{4,6},{5,7},{6,4},{7,5},{8,10},{9,11},{10,... | collective-permute-start | bytes 86024 | tf_op jit(solution)/shard_map/ppermute | solution.py:691
  35.1 5.2 %collective-permute-start.9 = (f32[56,128]{1,0:T(8,128)S(1)}, f32[56,128]{1,0:T(8,128)S(1)}, u32[]{:S(2)}, u32[]{:S(2)}) collective-permute-start(f32[56,128]{1,0:T(8,128)S(1)} %get-tuple-element.60), channel_id=1, source_target_pairs={{0,1},{1,2},{2,3},{3,0},{4,5},{5,6},{6,7},{7,4},{8,9},{9,10},{10,1... | collective-permute-start | bytes 86024 | tf_op jit(solution)/shard_map/ppermute | solution.py:691
  48.6 13.3 %collective-permute-start.12 = (f32[40,128]{1,0:T(8,128)S(1)}, f32[40,128]{1,0:T(8,128)S(1)}, u32[]{:S(2)}, u32[]{:S(2)}) collective-permute-start(f32[40,128]{1,0:T(8,128)S(1)} %get-tuple-element.48), channel_id=1, source_target_pairs={{0,3},{1,0},{2,1},{3,2},{4,7},{5,4},{6,5},{7,6},{8,11},{9,8},{10,9... | collective-permute-start | bytes 61448 | tf_op jit(solution)/shard_map/ppermute | solution.py:691
  49.3 12.7 %collective-permute-start.13 = (f32[40,128]{1,0:T(8,128)S(1)}, f32[40,128]{1,0:T(8,128)S(1)}, u32[]{:S(2)}, u32[]{:S(2)}) collective-permute-start(f32[40,128]{1,0:T(8,128)S(1)} %get-tuple-element.49), channel_id=1, source_target_pairs={{0,2},{1,3},{2,0},{3,1},{4,6},{5,7},{6,4},{7,5},{8,10},{9,11},{10,... | collective-permute-start | bytes 61448 | tf_op jit(solution)/shard_map/ppermute | solution.py:691
  52.5 9.5 %collective-permute-start.14 = (f32[40,128]{1,0:T(8,128)S(1)}, f32[40,128]{1,0:T(8,128)S(1)}, u32[]{:S(2)}, u32[]{:S(2)}) collective-permute-start(f32[40,128]{1,0:T(8,128)S(1)} %get-tuple-element.50), channel_id=1, source_target_pairs={{0,1},{1,2},{2,3},{3,0},{4,5},{5,6},{6,7},{7,4},{8,9},{9,10},{10,1... | collective-permute-start | bytes 61448 | tf_op jit(solution)/shard_map/ppermute | solution.py:691
  52.6 9.5 %collective-permute-start.16 = (f32[160,128]{1,0:T(8,128)S(1)}, f32[160,128]{1,0:T(8,128)S(1)}, u32[]{:S(2)}, u32[]{:S(2)}) collective-permute-start(f32[160,128]{1,0:T(8,128)S(1)} %get-tuple-element.53), channel_id=1, source_target_pairs={{0,28},{4,0},{8,4},{12,8},{16,12},{20,16},{24,20},{28,24},{1,29},{... | collective-permute-start | bytes 245768 | tf_op jit(solution)/shard_map/ppermute | solution.py:691
  62.0 7.2 %collective-permute-start.15 = (f32[160,128]{1,0:T(8,128)S(1)}, f32[160,128]{1,0:T(8,128)S(1)}, u32[]{:S(2)}, u32[]{:S(2)}) collective-permute-start(f32[160,128]{1,0:T(8,128)S(1)} %pad_maximum_fusion.3), channel_id=1, source_target_pairs={{0,4},{4,8},{8,12},{12,16},{16,20},{20,24},{24,28},{28,0},{1,5},{5... | collective-permute-start | bytes 245768 | tf_op jit(solution)/shard_map/ppermute | solution.py:691
  62.1 7.1 %collective-permute-start.17 = (f32[80,128]{1,0:T(8,128)S(1)}, f32[80,128]{1,0:T(8,128)S(1)}, u32[]{:S(2)}, u32[]{:S(2)}) collective-permute-start(f32[80,128]{1,0:T(8,128)S(1)} %pad_maximum_fusion.5), channel_id=1, source_target_pairs={{0,3},{1,0},{2,1},{3,2},{4,7},{5,4},{6,5},{7,6},{8,11},{9,8},{10,9... | collective-permute-start | bytes 122888 | tf_op jit(solution)/shard_map/ppermute | solution.py:691
  62.4 6.8 %collective-permute-start.18 = (f32[80,128]{1,0:T(8,128)S(1)}, f32[80,128]{1,0:T(8,128)S(1)}, u32[]{:S(2)}, u32[]{:S(2)}) collective-permute-start(f32[80,128]{1,0:T(8,128)S(1)} %pad_maximum_fusion.6), channel_id=1, source_target_pairs={{0,2},{1,3},{2,0},{3,1},{4,6},{5,7},{6,4},{7,5},{8,10},{9,11},{10,... | collective-permute-start | bytes 122888 | tf_op jit(solution)/shard_map/ppermute | solution.py:691
  62.9 6.3 %collective-permute-start.19 = (f32[80,128]{1,0:T(8,128)S(1)}, f32[80,128]{1,0:T(8,128)S(1)}, u32[]{:S(2)}, u32[]{:S(2)}) collective-permute-start(f32[80,128]{1,0:T(8,128)S(1)} %pad_maximum_fusion.7), channel_id=1, source_target_pairs={{0,1},{1,2},{2,3},{3,0},{4,5},{5,6},{6,7},{7,4},{8,9},{9,10},{10,1... | collective-permute-start | bytes 122888 | tf_op jit(solution)/shard_map/ppermute | solution.py:691
  (3 other events, 11.0 us)

commit v4 on v3

--- a/solution.py
+++ b/solution.py
@@ -20,8 +20,10 @@
 SMEM = pl.BlockSpec(memory_space=pltpu.SMEM)
 ANY = pl.BlockSpec(memory_space=pl.ANY)
 HBM = pl.BlockSpec(memory_space=pltpu.HBM)
-UNROLL = 16
-GROUP = 2
+UNROLL = 32
+TAIL = 8
+GROUP = 4
+REST = 2
 
 
 def rows_up(count):
@@ -156,17 +158,30 @@
         return count + jnp.where((partner >= lower) & (partner < upper), 1, 0)
 
     count = lax.fori_loop(0, home_ref.shape[0], one, 0, unroll=4)
-    for pad in range(UNROLL):
+    for pad in range(TAIL):
         homes[count + pad] = spare
         partners[count + pad] = 0
     return count
 
 
+def in_groups(count, large, small, work):
+    steps = count // large
+    left = (count - steps * large + small - 1) // small
+
+    def one(size, first, step, _):
+        work(size, first + step * size)
+        return 0
+
+    lax.fori_loop(0, steps, functools.partial(one, large, 0), 0)
+    lax.fori_loop(0, left, functools.partial(one, small, steps * large), 0)
+
+
 def add_tiles(count, homes, partners, home_side, partner_side, values, sums):
-    def some(step, _):
-        for k in range(UNROLL):
-            home = homes[step * UNROLL + k]
-            partner = partners[step * UNROLL + k]
+    def some(tiles, start):
+        added = []
+        for k in range(tiles):
+            home = homes[start + k]
+            partner = partners[start + k]
             factors = home_side[pl.ds(pl.multiple_of(home * 32, 32), 32), :].astype(bf16)
             weight = jnp.dot(partner_side[partner], factors, preferred_element_type=f32)
             weight = jnp.maximum(weight, 0.0)
@@ -174,14 +189,16 @@
             low = (weight - high.astype(f32)).astype(bf16)
             value = values[pl.ds(pl.multiple_of(partner * 16, 16), 16), :].astype(bf16)
             at = pl.ds(pl.multiple_of(home * 16, 16), 16)
-            sums[at, :] += jnp.dot(
+            term = jnp.dot(
                 jnp.concatenate([value, value], axis=1),
                 jnp.concatenate([high, low], axis=0),
                 preferred_element_type=f32,
             )
-        return 0
-
-    lax.fori_loop(0, (count + UNROLL - 1) // UNROLL, some, 0)
+            added.append((at, term))
+        for at, term in added:
+            sums[at, :] += term
+
+    in_groups(count, UNROLL, TAIL, some)
 
 
 def dot(left, right):
@@ -274,8 +291,8 @@
             pltpu.store(tiles.at[tile + 1], moved, mask=lane < at + length - width)
         return 0
 
-    lax.fori_loop(0, nblocks, order, 0, unroll=16)
-    lax.fori_loop(0, nblocks, spread, 0, unroll=16)
+    lax.fori_loop(0, nblocks, order, 0, unroll=32)
+    lax.fori_loop(0, nblocks, spread, 0, unroll=32)
 
 
 def own_contacts(cap, columns, depth, home_list, partner_list, state, cell, route,
@@ -444,11 +461,8 @@
     return jnp.where(hit, jnp.ones((), bf16), jnp.zeros((), bf16))
 
 
-def steps_of(counts):
-    longest = jnp.maximum(
-        jnp.maximum(counts[0], counts[1]), jnp.maximum(counts[2], counts[3])
-    )
-    return lax.shift_right_logical(longest + GROUP - 1, GROUP.bit_length() - 1)
+def longest(counts):
+    return jnp.maximum(jnp.maximum(counts[0], counts[1]), jnp.maximum(counts[2], counts[3]))
 
 
 def tile_of(counts, bucket, index, width):
@@ -464,12 +478,12 @@
     numbers = iota((columns, width), 0).astype(f32).astype(bf16)
     levels = all_levels(depth, width)
 
-    def some(step, _):
+    def some(size, first):
         sums = []
         for bucket in range(4):
             high_of, low_of, level_of = [], [], []
-            for k in range(GROUP):
-                index, real = tile_of(counts, bucket, step * GROUP + k, width)
+            for k in range(size):
+                index, real = tile_of(counts, bucket, first + k, width)
                 row = base[bucket * stride + index]
                 column, level = cell_parts(arrived, row, cap, columns, depth, bucket)
                 radius = arrived[pl.ds(row, 1), :]
@@ -498,9 +512,8 @@
             sums.append(both[0 : 4 * columns] + both[4 * columns :])
         for bucket in range(4):
             total[bucket * 4 * columns : (bucket + 1) * 4 * columns, :] += sums[bucket]
-        return 0
-
-    lax.fori_loop(0, steps_of(counts), some, 0)
+
+    in_groups(longest(counts), GROUP, REST, some)
 
 
 def sample(segments, counts, arrived, places, cap, table, answers):
@@ -511,12 +524,12 @@
     numbers = iota((columns, width), 0).astype(f32)
     answers[...] = jnp.zeros(answers.shape, f32)
 
-    def some(step, _):
+    def some(size, first):
         found = []
         for bucket in range(4):
             hots, hits = [], []
-            for k in range(GROUP):
-                index, real = tile_of(counts, bucket, step * GROUP + k, width)
+            for k in range(size):
+                index, real = tile_of(counts, bucket, first + k, width)
                 row = places[0][bucket * stride + index]
                 column, level = cell_parts(arrived, row, cap, columns, depth, bucket)
                 hots.append(level_hot(level, levels))
@@ -535,9 +548,8 @@
                     found.append((goal + c * cap, jnp.where(real, value, 0.0)))
         for goal, value in found:
             answers[pl.ds(goal, 1), :] += value
-        return 0
-
-    lax.fori_loop(0, steps_of(counts), some, 0)
+
+    in_groups(longest(counts), GROUP, REST, some)
 
 
 def first_deposit(nbrick, cap, skip, crossed, below, above, before, after, fluid, total, diffused,
@@ -657,8 +669,8 @@
         picked[b] = both[0:8] + both[8:16]
         return 0
 
-    lax.fori_loop(0, nblocks, gather, 0, unroll=16)
-    lax.fori_loop(0, nblocks, order, 0, unroll=16)
+    lax.fori_loop(0, nblocks, gather, 0, unroll=32)
+    lax.fori_loop(0, nblocks, order, 0, unroll=32)
     flat = picked.reshape(nblocks * 8, width)
     for c in range(3):
         now = updated[c]
@@ -714,7 +726,7 @@
             pltpu.VMEM((count * 16, width), f32),
         ]
 
-    lists = [ints(tiles + UNROLL)] * 2
+    lists = [ints(tiles + TAIL)] * 2
     contact_flops = tiles * width * width * 200
     chunk_tiles = pltpu.VMEM((codes * (cap + 2), 8, width), f32)
     block_tiles = pltpu.VMEM((nblocks, 8, width), f32)

time: 72.8 us -> 69.9 us (0.960)
  Pallas kernels: 35.5 us -> 33.6 us
  starting transfers between devices: 25.1 us -> 23.9 us
    pallas_call x1, Pallas kernels: 8.41 us -> 10.9 us  [on_device(): call(functools.partial(advance, nbrick, cap), [struct(3, nx, ny, nz), str...]
    pallas_call x1, Pallas kernels: 4.96 us -> 3.05 us  [on_device(): call(functools.partial(first_deposit, nbrick, cap, ghost_rows), [struct(8...]
    pallas_call x1, Pallas kernels: 3.71 us -> 2.12 us  [on_device(): call(functools.partial(last_sample, nbrick, cap), [struct(back, width)] *...]
    ppermute x20, starting transfers between devices: 25.1 us -> 23.9 us  [shifted(): lax.ppermute(x, axis, [(i, (i + step) % count) for i in range(count)])]
  transfers between devices with their start and end apart: 20 -> 20, of which waited for: 2 -> 3; matrix products, arithmetic and copies ran while one was open for 0% -> 0% of each run, Pallas kernels for 22% -> 17%
where the time goes in v4:
time: 69.9 us; the launch traced here: 70 us
  Pallas kernels  33.6 us (48%)
  starting transfers between devices  23.9 us (34%)
  waiting for transfers between devices  8.48 us (12%)
  local copies, waits for them, and re-layouts  1.85 us (3%)
  between operations  1.12 us (2%)
  other arithmetic  1.04 us (1%)
    ppermute x20, starting transfers between devices, shifted(): lax.ppermute(x, axis, [(i, (i + step) % count) for i in range(count)])  23.9 us
    pallas_call x1, Pallas kernels, on_device(): call(functools.partial(advance, nbrick, cap), [struct(3, nx, ny, nz), str...  10.9 us
    ppermute x20, waiting for transfers between devices, shifted(): lax.ppermute(x, axis, [(i, (i + step) % count) for i in range(count)])  8.48 us
    pallas_call x1, Pallas kernels, on_device(): call(functools.partial(own_contacts, cap, columns, nz), [struct((nblocks...  6.9 us
    pallas_call x1, Pallas kernels, on_device(): call(functools.partial(ghost_contacts, nbrick, cap, 4 * per), [struct(3,...  6.4 us
    pallas_call x1, Pallas kernels, on_device(): call(functools.partial(relax, nbrick, cap), [struct(3, nblocks, width)],...  3.56 us
    pallas_call x1, Pallas kernels, on_device(): call(functools.partial(first_deposit, nbrick, cap, ghost_rows), [struct(8...  3.05 us
    pallas_call x1, Pallas kernels, on_device(): call(functools.partial(last_sample, nbrick, cap), [struct(back, width)] *...  2.12 us
  transfers between devices with their start and end apart: 20, of which 3 were waited for; matrix products, arithmetic and copies ran while one was open for 0% of the time, Pallas kernels for 17%

profile of v4, /device:TPU:0, one launch (start us, length us, event | category | flops | bytes accessed | tf_op | source)
XLA Modules:
  0.0 70.0 jit_solution(11721439820394099815)
XLA Ops:
  0.7 1.0 %pad_maximum_fusion.state = f32[7,64,128]{2,1,0:T(8,128)S(1)} fusion(f32[3,64,128]{2,1,0:T(8,128)} %bitcast.6, f32[1,64,128]{2,1,0:T(8,128)} %bitcast.9, f32[3,64,128]{2,1,0:T(8,128)} %bitcast.7), kind=kLoop, calls=%fused_computation | loop fusion | flops 114688 | bytes 458752 | tf_op jit(solution)/shard_map/concatenate | solution.py:708
  1.7 1.1 %copy-done = f32[3,4,32,512]{3,2,1,0:T(8,128)S(1)} copy-done((f32[3,4,32,512]{3,2,1,0:T(8,128)S(1)}, f32[3,4,32,512]{3,2,1,0:T(8,128)}, u32[]{:S(2)}) %copy-start) | copy-done | bytes 786456
  2.8 0.7 copy-done.3
  3.5 0.7 pack.1
  4.1 3.0 %collective-permute-start = (f32[440,128]{1,0:T(8,128)S(1)}, f32[440,128]{1,0:T(8,128)S(1)}, u32[]{:S(2)}, u32[]{:S(2)}) collective-permute-start(f32[440,128]{1,0:T(8,128)S(1)} %get-tuple-element.31), channel_id=1, source_target_pairs={{0,4},{4,8},{8,12},{12,16},{16,20},{20,24},{24,28},{28,0},{1,5},{5... | collective-permute-start | bytes 675848 | tf_op jit(solution)/shard_map/ppermute | solution.py:703
  7.2 3.1 %collective-permute-start.1 = (f32[440,128]{1,0:T(8,128)S(1)}, f32[440,128]{1,0:T(8,128)S(1)}, u32[]{:S(2)}, u32[]{:S(2)}) collective-permute-start(f32[440,128]{1,0:T(8,128)S(1)} %get-tuple-element.32), channel_id=1, source_target_pairs={{0,28},{4,0},{8,4},{12,8},{16,12},{20,16},{24,20},{28,24},{1,29},{... | collective-permute-start | bytes 675848 | tf_op jit(solution)/shard_map/ppermute | solution.py:703
  10.3 1.7 %collective-permute-start.3 = (f32[104,128]{1,0:T(8,128)S(1)}, f32[104,128]{1,0:T(8,128)S(1)}, u32[]{:S(2)}, u32[]{:S(2)}) collective-permute-start(f32[104,128]{1,0:T(8,128)S(1)} %get-tuple-element.34), channel_id=1, source_target_pairs={{0,3},{1,0},{2,1},{3,2},{4,7},{5,4},{6,5},{7,6},{8,11},{9,8},{10,9... | collective-permute-start | bytes 159752 | tf_op jit(solution)/shard_map/ppermute | solution.py:703
  12.0 6.9 %own_contacts.1 = (f32[2080,128]{1,0:T(8,128)S(1)}, f32[1040,128]{1,0:T(8,128)S(1)}, f32[64,128]{1,0:T(8,128)S(1)}, s32[64,128]{1,0:T(8,128)S(1)}, f32[16,128]{1,0:T(8,128)S(1)}) custom-call(s32[128]{0:T(128)S(1)} %copy-done.4, s32[128]{0:T(128)S(1)} %copy-done.5, f32[7,64,128]{2,1,0:T(8,128)S(1)} %pad_maximum_fusion.state, s32[64,128]{1,0:T(8,128)S(1)} %copy-done.2, ...), custom_call_target="tpu_custom_call" | custom-call | flops 419430400 | bytes 1048576 | tf_op jit(solution)/shard_map/own_contacts/pallas_call | solution.py:734
  19.0 6.4 %ghost_contacts.1 = (f32[3,64,128]{2,1,0:T(8,128)S(1)}, f32[224,128]{1,0:T(8,128)S(1)}, f32[112,128]{1,0:T(8,128)S(1)}, f32[112,128]{1,0:T(8,128)S(1)}, f32[112,128]{1,0:T(8,128)S(1)}, /*index=5*/f32[112,128]{1,0:T(8,128)S(1)}) custom-call(s32[128]{0:T(128)S(1)} %copy-done.4, s32[128]{0:T(128)S(1)} %copy-done.5, s32[64,128]{1,0:T(8,128)S(1)} %get-tuple-element.30.plan, ...), custom_call_target="tpu_custom_call" | custom-call | flops 209715200 | bytes 1048576 | tf_op jit(solution)/shard_map/ghost_contacts/pallas_call | solution.py:748
  25.5 1.7 %collective-permute-start.5 = (f32[112,128]{1,0:T(8,128)S(1)}, f32[112,128]{1,0:T(8,128)S(1)}, u32[]{:S(2)}, u32[]{:S(2)}) collective-permute-start(f32[112,128]{1,0:T(8,128)S(1)} %get-tuple-element.42), channel_id=1, source_target_pairs={{0,2},{1,3},{2,0},{3,1},{4,6},{5,7},{6,4},{7,5},{8,10},{9,11},{10,... | collective-permute-start | bytes 172040 | tf_op jit(solution)/shard_map/ppermute | solution.py:703
  27.1 1.4 %collective-permute-start.6 = (f32[112,128]{1,0:T(8,128)S(1)}, f32[112,128]{1,0:T(8,128)S(1)}, u32[]{:S(2)}, u32[]{:S(2)}) collective-permute-start(f32[112,128]{1,0:T(8,128)S(1)} %get-tuple-element.43), channel_id=1, source_target_pairs={{0,3},{1,0},{2,1},{3,2},{4,7},{5,4},{6,5},{7,6},{8,11},{9,8},{10,9... | collective-permute-start | bytes 172040 | tf_op jit(solution)/shard_map/ppermute | solution.py:703
  28.5 3.2 %collective-permute-start.8 = (f32[224,128]{1,0:T(8,128)S(1)}, f32[224,128]{1,0:T(8,128)S(1)}, u32[]{:S(2)}, u32[]{:S(2)}) collective-permute-start(f32[224,128]{1,0:T(8,128)S(1)} %get-tuple-element.46), channel_id=1, source_target_pairs={{0,28},{4,0},{8,4},{12,8},{16,12},{20,16},{24,20},{28,24},{1,29},{... | collective-permute-start | bytes 344072 | tf_op jit(solution)/shard_map/ppermute | solution.py:703
  31.9 2.2 %collective-permute-done.8 = f32[224,128]{1,0:T(8,128)S(1)} collective-permute-done((f32[224,128]{1,0:T(8,128)S(1)}, f32[224,128]{1,0:T(8,128)S(1)}, u32[]{:S(2)}, u32[]{:S(2)}) %collective-permute-start.8) | collective-permute-done | bytes 114720 | tf_op jit(solution)/shard_map/ppermute | solution.py:703
  34.2 1.0 %collective-permute-start.10 = (f32[56,128]{1,0:T(8,128)S(1)}, f32[56,128]{1,0:T(8,128)S(1)}, u32[]{:S(2)}, u32[]{:S(2)}) collective-permute-start(f32[56,128]{1,0:T(8,128)S(1)} %get-tuple-element.59), channel_id=1, source_target_pairs={{0,2},{1,3},{2,0},{3,1},{4,6},{5,7},{6,4},{7,5},{8,10},{9,11},{10,... | collective-permute-start | bytes 86024 | tf_op jit(solution)/shard_map/ppermute | solution.py:703
  35.3 3.1 %first_deposit.1 = (f32[1024,256]{1,0:T(8,128)S(1)}, f32[3,4,32,512]{3,2,1,0:T(8,128)S(1)}) custom-call(f32[224,128]{1,0:T(8,128)S(1)} %pad_maximum_fusion.1.crossed, f32[440,128]{1,0:T(8,128)S(1)} %collective-permute-done.below, f32[440,128]{1,0:T(8,128)S(1)} %collective-permute-done.1.above, f32[104,128]{1,0:T(8,128)S(1)} %collective-permute-done.2.before, ...), custom_call_target="tpu_custom_call" | custom-call | flops 1431655808 | bytes 1048576 | tf_op jit(solution)/shard_map/first_deposit/pallas_call | solution.py:776
  38.4 0.9 %collective-permute-done.7.below = f32[224,128]{1,0:T(8,128)S(1)} collective-permute-done((f32[224,128]{1,0:T(8,128)S(1)}, f32[224,128]{1,0:T(8,128)S(1)}, u32[]{:S(2)}, u32[]{:S(2)}) %collective-permute-start.7) | collective-permute-done | bytes 114720 | tf_op jit(solution)/shard_map/ppermute | solution.py:703
  39.3 10.9 %advance.1 = (f32[3,4,32,512]{3,2,1,0:T(8,128)}, bf16[1536,256]{1,0:T(8,128)(2,1)S(1)}, f32[160,128]{1,0:T(8,128)S(1)}, f32[40,128]{1,0:T(8,128)S(1)}, f32[40,12...) custom-call(f32[1024,256]{1,0:T(8,128)S(1)} %get-tuple-element.44.start, ...), custom_call_target="tpu_custom_call" | custom-call | flops 4294967296 | bytes 1048576 | tf_op jit(solution)/shard_map/advance/pallas_call | solution.py:786
  50.5 0.4 collective-permute-start.14
  51.0 5.2 %collective-permute-start.16 = (f32[160,128]{1,0:T(8,128)S(1)}, f32[160,128]{1,0:T(8,128)S(1)}, u32[]{:S(2)}, u32[]{:S(2)}) collective-permute-start(f32[160,128]{1,0:T(8,128)S(1)} %get-tuple-element.53), channel_id=1, source_target_pairs={{0,28},{4,0},{8,4},{12,8},{16,12},{20,16},{24,20},{28,24},{1,29},{... | collective-permute-start | bytes 245768 | tf_op jit(solution)/shard_map/ppermute | solution.py:703
  56.2 2.1 %last_sample.1 = (f32[40,128]{1,0:T(8,128)S(1)}, f32[40,128]{1,0:T(8,128)S(1)}, f32[40,128]{1,0:T(8,128)S(1)}, f32[40,128]{1,0:T(8,128)S(1)}) custom-call(f32[224,128]{1,0:T(8,128)S(1)} %pad_maximum_fusion.1.crossed, bf16[1536,256]{1,0:T(8,128)(2,1)S(1)} %get-tuple-element.51.table), custom_call_target="tpu_custom_call" | custom-call | flops 67108864 | bytes 1048576 | tf_op jit(solution)/shard_map/last_sample/pallas_call | solution.py:812
  58.4 0.8 %collective-permute-start.17 = (f32[80,128]{1,0:T(8,128)S(1)}, f32[80,128]{1,0:T(8,128)S(1)}, u32[]{:S(2)}, u32[]{:S(2)}) collective-permute-start(f32[80,128]{1,0:T(8,128)S(1)} %pad_maximum_fusion.5), channel_id=1, source_target_pairs={{0,3},{1,0},{2,1},{3,2},{4,7},{5,4},{6,5},{7,6},{8,11},{9,8},{10,9... | collective-permute-start | bytes 122888 | tf_op jit(solution)/shard_map/ppermute | solution.py:703
  59.2 1.7 %collective-permute-start.18 = (f32[80,128]{1,0:T(8,128)S(1)}, f32[80,128]{1,0:T(8,128)S(1)}, u32[]{:S(2)}, u32[]{:S(2)}) collective-permute-start(f32[80,128]{1,0:T(8,128)S(1)} %pad_maximum_fusion.6), channel_id=1, source_target_pairs={{0,2},{1,3},{2,0},{3,1},{4,6},{5,7},{6,4},{7,5},{8,10},{9,11},{10,... | collective-permute-start | bytes 122888 | tf_op jit(solution)/shard_map/ppermute | solution.py:703
  60.9 5.3 %collective-permute-done.15.down = f32[160,128]{1,0:T(8,128)S(1)} collective-permute-done((f32[160,128]{1,0:T(8,128)S(1)}, f32[160,128]{1,0:T(8,128)S(1)}, u32[]{:S(2)}, u32[]{:S(2)}) %collective-permute-start.15) | collective-permute-done | bytes 81952 | tf_op jit(solution)/shard_map/ppermute | solution.py:703
  66.2 3.6 %relax.1 = f32[3,64,128]{2,1,0:T(8,128)} custom-call(s32[64,128]{1,0:T(8,128)S(1)} %get-tuple-element.30.plan, f32[3,64,128]{2,1,0:T(8,128)S(1)} %get-tuple-element.39.updated, f32[64,128]{1,0:T(8,128)S(1)} %get-tuple-element.37.spots, f32[160,128]{1,0:T(8,128)S(1)} %collective-permute-done.15.down, f32[80,128]{1,0:T(8,128)S(1)} %pad_maximum_fusion.4.rest_0_, ...), custom_call_target="tpu_custom_call" | custom-call | bytes 1048576 | tf_op jit(solution)/shard_map/relax/pallas_call | solution.py:825
  (51 shorter events, 0.9 us)
Async XLA Ops:
  0.6 11.4 %copy-start.5 = (s32[128]{0:T(128)S(1)}, s32[128]{0:T(128)}, u32[]{:S(2)}) copy-start(s32[128]{0:T(128)} %partner_list.3) | copy-start | bytes 1540
  0.6 11.4 %copy-start.4 = (s32[128]{0:T(128)S(1)}, s32[128]{0:T(128)}, u32[]{:S(2)}) copy-start(s32[128]{0:T(128)} %home_list.3) | copy-start | bytes 1540
  0.7 11.4 %copy-start.2 = (s32[64,128]{1,0:T(8,128)S(1)}, s32[64,128]{1,0:T(8,128)}, u32[]{:S(2)}) copy-start(s32[64,128]{1,0:T(8,128)} %cell.3) | copy-start | bytes 98308
  0.7 11.4 %copy-start.6 = (s32[64,1]{0,1:T(1,128)S(1)}, s32[64,1]{0,1:T(1,128)}, u32[]{:S(2)}) copy-start(s32[64,1]{0,1:T(1,128)} %param.13) | copy-start | bytes 772
  4.1 14.8 %collective-permute-start = (f32[440,128]{1,0:T(8,128)S(1)}, f32[440,128]{1,0:T(8,128)S(1)}, u32[]{:S(2)}, u32[]{:S(2)}) collective-permute-start(f32[440,128]{1,0:T(8,128)S(1)} %get-tuple-element.31), channel_id=1, source_target_pairs={{0,4},{4,8},{8,12},{12,16},{16,20},{20,24},{24,28},{28,0},{1,5},{5... | collective-permute-start | bytes 675848 | tf_op jit(solution)/shard_map/ppermute | solution.py:703
  7.2 11.8 %collective-permute-start.1 = (f32[440,128]{1,0:T(8,128)S(1)}, f32[440,128]{1,0:T(8,128)S(1)}, u32[]{:S(2)}, u32[]{:S(2)}) collective-permute-start(f32[440,128]{1,0:T(8,128)S(1)} %get-tuple-element.32), channel_id=1, source_target_pairs={{0,28},{4,0},{8,4},{12,8},{16,12},{20,16},{24,20},{28,24},{1,29},{... | collective-permute-start | bytes 675848 | tf_op jit(solution)/shard_map/ppermute | solution.py:703
  10.3 8.7 %collective-permute-start.2 = (f32[104,128]{1,0:T(8,128)S(1)}, f32[104,128]{1,0:T(8,128)S(1)}, u32[]{:S(2)}, u32[]{:S(2)}) collective-permute-start(f32[104,128]{1,0:T(8,128)S(1)} %get-tuple-element.33), channel_id=1, source_target_pairs={{0,1},{1,2},{2,3},{3,0},{4,5},{5,6},{6,7},{7,4},{8,9},{9,10},{10,1... | collective-permute-start | bytes 159752 | tf_op jit(solution)/shard_map/ppermute | solution.py:703
  10.3 8.7 %collective-permute-start.3 = (f32[104,128]{1,0:T(8,128)S(1)}, f32[104,128]{1,0:T(8,128)S(1)}, u32[]{:S(2)}, u32[]{:S(2)}) collective-permute-start(f32[104,128]{1,0:T(8,128)S(1)} %get-tuple-element.34), channel_id=1, source_target_pairs={{0,3},{1,0},{2,1},{3,2},{4,7},{5,4},{6,5},{7,6},{8,11},{9,8},{10,9... | collective-permute-start | bytes 159752 | tf_op jit(solution)/shard_map/ppermute | solution.py:703
  25.4 6.3 %collective-permute-start.4 = (f32[112,128]{1,0:T(8,128)S(1)}, f32[112,128]{1,0:T(8,128)S(1)}, u32[]{:S(2)}, u32[]{:S(2)}) collective-permute-start(f32[112,128]{1,0:T(8,128)S(1)} %get-tuple-element.41), channel_id=1, source_target_pairs={{0,1},{1,2},{2,3},{3,0},{4,5},{5,6},{6,7},{7,4},{8,9},{9,10},{10,1... | collective-permute-start | bytes 172040 | tf_op jit(solution)/shard_map/ppermute | solution.py:703
  25.5 6.3 %collective-permute-start.5 = (f32[112,128]{1,0:T(8,128)S(1)}, f32[112,128]{1,0:T(8,128)S(1)}, u32[]{:S(2)}, u32[]{:S(2)}) collective-permute-start(f32[112,128]{1,0:T(8,128)S(1)} %get-tuple-element.42), channel_id=1, source_target_pairs={{0,2},{1,3},{2,0},{3,1},{4,6},{5,7},{6,4},{7,5},{8,10},{9,11},{10,... | collective-permute-start | bytes 172040 | tf_op jit(solution)/shard_map/ppermute | solution.py:703
  27.1 4.6 %collective-permute-start.6 = (f32[112,128]{1,0:T(8,128)S(1)}, f32[112,128]{1,0:T(8,128)S(1)}, u32[]{:S(2)}, u32[]{:S(2)}) collective-permute-start(f32[112,128]{1,0:T(8,128)S(1)} %get-tuple-element.43), channel_id=1, source_target_pairs={{0,3},{1,0},{2,1},{3,2},{4,7},{5,4},{6,5},{7,6},{8,11},{9,8},{10,9... | collective-permute-start | bytes 172040 | tf_op jit(solution)/shard_map/ppermute | solution.py:703
  28.5 5.6 %collective-permute-start.8 = (f32[224,128]{1,0:T(8,128)S(1)}, f32[224,128]{1,0:T(8,128)S(1)}, u32[]{:S(2)}, u32[]{:S(2)}) collective-permute-start(f32[224,128]{1,0:T(8,128)S(1)} %get-tuple-element.46), channel_id=1, source_target_pairs={{0,28},{4,0},{8,4},{12,8},{16,12},{20,16},{24,20},{28,24},{1,29},{... | collective-permute-start | bytes 344072 | tf_op jit(solution)/shard_map/ppermute | solution.py:703
  31.8 7.5 %collective-permute-start.7 = (f32[224,128]{1,0:T(8,128)S(1)}, f32[224,128]{1,0:T(8,128)S(1)}, u32[]{:S(2)}, u32[]{:S(2)}) collective-permute-start(f32[224,128]{1,0:T(8,128)S(1)} %pad_maximum_fusion.2), channel_id=1, source_target_pairs={{0,4},{4,8},{8,12},{12,16},{16,20},{20,24},{24,28},{28,0},{1,5},{5... | collective-permute-start | bytes 344072 | tf_op jit(solution)/shard_map/ppermute | solution.py:703
  34.1 4.3 %collective-permute-start.11 = (f32[56,128]{1,0:T(8,128)S(1)}, f32[56,128]{1,0:T(8,128)S(1)}, u32[]{:S(2)}, u32[]{:S(2)}) collective-permute-start(f32[56,128]{1,0:T(8,128)S(1)} %get-tuple-element.58), channel_id=1, source_target_pairs={{0,3},{1,0},{2,1},{3,2},{4,7},{5,4},{6,5},{7,6},{8,11},{9,8},{10,9... | collective-permute-start | bytes 86024 | tf_op jit(solution)/shard_map/ppermute | solution.py:703
  34.2 4.2 %collective-permute-start.10 = (f32[56,128]{1,0:T(8,128)S(1)}, f32[56,128]{1,0:T(8,128)S(1)}, u32[]{:S(2)}, u32[]{:S(2)}) collective-permute-start(f32[56,128]{1,0:T(8,128)S(1)} %get-tuple-element.59), channel_id=1, source_target_pairs={{0,2},{1,3},{2,0},{3,1},{4,6},{5,7},{6,4},{7,5},{8,10},{9,11},{10,... | collective-permute-start | bytes 86024 | tf_op jit(solution)/shard_map/ppermute | solution.py:703
  35.1 3.3 %collective-permute-start.9 = (f32[56,128]{1,0:T(8,128)S(1)}, f32[56,128]{1,0:T(8,128)S(1)}, u32[]{:S(2)}, u32[]{:S(2)}) collective-permute-start(f32[56,128]{1,0:T(8,128)S(1)} %get-tuple-element.60), channel_id=1, source_target_pairs={{0,1},{1,2},{2,3},{3,0},{4,5},{5,6},{6,7},{7,4},{8,9},{9,10},{10,1... | collective-permute-start | bytes 86024 | tf_op jit(solution)/shard_map/ppermute | solution.py:703
  50.2 8.1 %collective-permute-start.12 = (f32[40,128]{1,0:T(8,128)S(1)}, f32[40,128]{1,0:T(8,128)S(1)}, u32[]{:S(2)}, u32[]{:S(2)}) collective-permute-start(f32[40,128]{1,0:T(8,128)S(1)} %get-tuple-element.48), channel_id=1, source_target_pairs={{0,3},{1,0},{2,1},{3,2},{4,7},{5,4},{6,5},{7,6},{8,11},{9,8},{10,9... | collective-permute-start | bytes 61448 | tf_op jit(solution)/shard_map/ppermute | solution.py:703
  50.5 7.8 %collective-permute-start.13 = (f32[40,128]{1,0:T(8,128)S(1)}, f32[40,128]{1,0:T(8,128)S(1)}, u32[]{:S(2)}, u32[]{:S(2)}) collective-permute-start(f32[40,128]{1,0:T(8,128)S(1)} %get-tuple-element.49), channel_id=1, source_target_pairs={{0,2},{1,3},{2,0},{3,1},{4,6},{5,7},{6,4},{7,5},{8,10},{9,11},{10,... | collective-permute-start | bytes 61448 | tf_op jit(solution)/shard_map/ppermute | solution.py:703
  50.5 7.8 %collective-permute-start.14 = (f32[40,128]{1,0:T(8,128)S(1)}, f32[40,128]{1,0:T(8,128)S(1)}, u32[]{:S(2)}, u32[]{:S(2)}) collective-permute-start(f32[40,128]{1,0:T(8,128)S(1)} %get-tuple-element.50), channel_id=1, source_target_pairs={{0,1},{1,2},{2,3},{3,0},{4,5},{5,6},{6,7},{7,4},{8,9},{9,10},{10,1... | collective-permute-start | bytes 61448 | tf_op jit(solution)/shard_map/ppermute | solution.py:703
  51.0 7.4 %collective-permute-start.16 = (f32[160,128]{1,0:T(8,128)S(1)}, f32[160,128]{1,0:T(8,128)S(1)}, u32[]{:S(2)}, u32[]{:S(2)}) collective-permute-start(f32[160,128]{1,0:T(8,128)S(1)} %get-tuple-element.53), channel_id=1, source_target_pairs={{0,28},{4,0},{8,4},{12,8},{16,12},{20,16},{24,20},{28,24},{1,29},{... | collective-permute-start | bytes 245768 | tf_op jit(solution)/shard_map/ppermute | solution.py:703
  58.3 7.9 %collective-permute-start.15 = (f32[160,128]{1,0:T(8,128)S(1)}, f32[160,128]{1,0:T(8,128)S(1)}, u32[]{:S(2)}, u32[]{:S(2)}) collective-permute-start(f32[160,128]{1,0:T(8,128)S(1)} %pad_maximum_fusion.3), channel_id=1, source_target_pairs={{0,4},{4,8},{8,12},{12,16},{16,20},{20,24},{24,28},{28,0},{1,5},{5... | collective-permute-start | bytes 245768 | tf_op jit(solution)/shard_map/ppermute | solution.py:703
  58.4 7.8 %collective-permute-start.17 = (f32[80,128]{1,0:T(8,128)S(1)}, f32[80,128]{1,0:T(8,128)S(1)}, u32[]{:S(2)}, u32[]{:S(2)}) collective-permute-start(f32[80,128]{1,0:T(8,128)S(1)} %pad_maximum_fusion.5), channel_id=1, source_target_pairs={{0,3},{1,0},{2,1},{3,2},{4,7},{5,4},{6,5},{7,6},{8,11},{9,8},{10,9... | collective-permute-start | bytes 122888 | tf_op jit(solution)/shard_map/ppermute | solution.py:703
  59.2 7.0 %collective-permute-start.18 = (f32[80,128]{1,0:T(8,128)S(1)}, f32[80,128]{1,0:T(8,128)S(1)}, u32[]{:S(2)}, u32[]{:S(2)}) collective-permute-start(f32[80,128]{1,0:T(8,128)S(1)} %pad_maximum_fusion.6), channel_id=1, source_target_pairs={{0,2},{1,3},{2,0},{3,1},{4,6},{5,7},{6,4},{7,5},{8,10},{9,11},{10,... | collective-permute-start | bytes 122888 | tf_op jit(solution)/shard_map/ppermute | solution.py:703
  60.9 5.3 %collective-permute-start.19 = (f32[80,128]{1,0:T(8,128)S(1)}, f32[80,128]{1,0:T(8,128)S(1)}, u32[]{:S(2)}, u32[]{:S(2)}) collective-permute-start(f32[80,128]{1,0:T(8,128)S(1)} %pad_maximum_fusion.7), channel_id=1, source_target_pairs={{0,1},{1,2},{2,3},{3,0},{4,5},{5,6},{6,7},{7,4},{8,9},{9,10},{10,1... | collective-permute-start | bytes 122888 | tf_op jit(solution)/shard_map/ppermute | solution.py:703
  (3 other events, 11.7 us)

commit v5 on v4

--- a/solution.py
+++ b/solution.py
@@ -414,14 +414,17 @@
     return (segments + 1) * cap
 
 
-def list_arrived(arrived, starts, ends, cap, places, counts):
+def list_arrived(arrived, starts, ends, cap, places, counts, early=None):
     base, goal = places
     width = arrived.shape[1]
     stride = list_stride(len(starts), cap)
     shift = width.bit_length() - 1
     lane = iota((1, width), 1)
     filled = [jnp.int32(0)] * 4
-    for start, end in zip(starts, ends):
+    for segment, (start, end) in enumerate(zip(starts, ends)):
+        if early is not None and 2 * segment == len(starts):
+            for j in range(4):
+                early[j] = filled[j]
         row = arrived[start + 5 * cap : start + 5 * cap + 1, :]
         edge = jnp.int32(0)
         for j in range(4):
@@ -566,9 +569,9 @@
 
 def advance(nbrick, cap, start, fluid, diffused, below, *rest):
     above, rest = rest[:nbrick], rest[nbrick:]
-    fluid_next, table, answers_below = rest[:3]
-    answers_above, rest = rest[3 : 3 + nbrick], rest[3 + nbrick :]
-    arrived, answers, total, flow, fresh_flow, base, goal, counts, sems = rest
+    fluid_next, table = rest[:2]
+    answers_above, rest = rest[2 : 2 + nbrick], rest[2 + nbrick :]
+    arrived, answers, total, flow, fresh_flow, base, goal, counts, early, sems = rest
     reading = pltpu.make_async_copy(fluid, flow, sems.at[0])
     reading.start()
     chunk = rows_up(5 * cap + 1)
@@ -580,7 +583,7 @@
     starts = [i * chunk for i in range(2 * nbrick)]
     ends = [i * back for i in range(2 * nbrick)]
     total[...] = start[...]
-    list_arrived(arrived, starts, ends, cap, (base, goal), counts)
+    list_arrived(arrived, starts, ends, cap, (base, goal), counts, early)
     deposit(2 * nbrick, counts, arrived, base, cap, total)
     reading.wait()
 
@@ -608,11 +611,19 @@
                 table[spot + 3 * columns : spot + 3 * columns + ny, :] = low[:, half]
     writing = pltpu.make_async_copy(fresh_flow, fluid_next, sems.at[1])
     writing.start()
-    sample(2 * nbrick, counts, arrived, (base, goal), cap, table, answers)
+    sample(2 * nbrick, early, arrived, (base, goal), cap, table, answers)
     for b, part in enumerate(answers_above):
         part[...] = answers[b * back : (b + 1) * back, :]
-    answers_below[...] = answers[nbrick * back :, :]
     writing.wait()
+
+
+def below_sample(nbrick, cap, below, table, answers, base, goal, counts):
+    chunk = rows_up(5 * cap + 1)
+    back = rows_up(3 * cap)
+    starts = [b * chunk for b in range(nbrick)]
+    ends = [b * back for b in range(nbrick)]
+    list_arrived(below, starts, ends, cap, (base, goal), counts)
+    sample(nbrick, counts, below, (base, goal), cap, table, answers)
 
 
 def last_sample(nbrick, cap, crossed, table, *rest):
@@ -783,27 +794,35 @@
         "first_deposit",
         block_flops * nblocks // 3,
     )(crossed, below, above, before, after, fluid)
-    fluid_next, table, answers_below, *answers_above = call(
+    fluid_next, table, *answers_above = call(
         functools.partial(advance, nbrick, cap),
         [
             struct(3, nx, ny, nz),
             struct(12 * columns, nz // 2, dtype=bf16),
-            struct(nbrick * back, width),
         ]
         + [struct(back, width)] * nbrick,
         [VMEM, HBM] + [VMEM] * (2 + nbrick),
         [
             pltpu.VMEM((2 * nbrick * chunk, width), f32),
-            pltpu.VMEM((2 * nbrick * back, width), f32),
+            pltpu.VMEM((nbrick * back, width), f32),
             pltpu.VMEM((8 * columns, nz // 2), f32),
         ]
         + [pltpu.VMEM((3, nx, ny, nz), f32)] * 2
         + places(2 * nbrick)
+        + [ints(4)]
         + [pltpu.SemaphoreType.DMA((2,))],
         "advance",
         block_flops * nblocks,
-        places=[HBM] + [VMEM] * (2 + nbrick),
+        places=[HBM] + [VMEM] * (1 + nbrick),
     )(started, fluid, diffused, from_below, *from_above)
+    (answers_below,) = call(
+        functools.partial(below_sample, nbrick, cap),
+        [struct(nbrick * back, width)],
+        [VMEM] * 2,
+        places(nbrick),
+        "below_sample",
+        block_flops * nblocks // 64,
+    )(from_below, table)
     answers_below = shifted(answers_below, "slab", -1)
     answers_above = [
         shifted(part, "brick", -behind) for behind, part in enumerate(answers_above)

time: 69.9 us -> 70 us (level)
  Pallas kernels: 33.6 us -> 32.1 us
  starting transfers between devices: 23.9 us -> 25.4 us
    pallas_call x1, Pallas kernels: 10.9 us -> 6.68 us  [on_device(): call(functools.partial(advance, nbrick, cap), [struct(3, nx, ny, nz), str...]
    pallas_call x0 -> x1, Pallas kernels: none -> 2.73 us  [on_device(): call(functools.partial(below_sample, nbrick, cap), [struct(nbrick * back,...]
    ppermute x20, starting transfers between devices: 23.9 us -> 25.4 us  [shifted(): lax.ppermute(x, axis, [(i, (i + step) % count) for i in range(count)])]
  transfers between devices with their start and end apart: 20 -> 20, of which waited for: 3 -> 4; matrix products, arithmetic and copies ran while one was open for 0% -> 0% of each run, Pallas kernels for 17% -> 22%
where the time goes in v5:
time: 70 us; the launch traced here: 70.4 us
  Pallas kernels  32.1 us (46%)
  starting transfers between devices  25.4 us (36%)
  waiting for transfers between devices  8.84 us (13%)
  local copies, waits for them, and re-layouts  1.85 us (3%)
  between operations  1.11 us (2%)
  other arithmetic  1.05 us (2%)
    ppermute x20, starting transfers between devices, shifted(): lax.ppermute(x, axis, [(i, (i + step) % count) for i in range(count)])  25.4 us
    ppermute x20, waiting for transfers between devices, shifted(): lax.ppermute(x, axis, [(i, (i + step) % count) for i in range(count)])  8.84 us
    pallas_call x1, Pallas kernels, on_device(): call(functools.partial(own_contacts, cap, columns, nz), [struct((nblocks...  7.28 us
    pallas_call x1, Pallas kernels, on_device(): call(functools.partial(advance, nbrick, cap), [struct(3, nx, ny, nz), str...  6.68 us
    pallas_call x1, Pallas kernels, on_device(): call(functools.partial(ghost_contacts, nbrick, cap, 4 * per), [struct(3,...  6.01 us
    pallas_call x1, Pallas kernels, on_device(): call(functools.partial(relax, nbrick, cap), [struct(3, nblocks, width)],...  3.56 us
    pallas_call x1, Pallas kernels, on_device(): call(functools.partial(first_deposit, nbrick, cap, ghost_rows), [struct(8...  3.06 us
    pallas_call x1, Pallas kernels, on_device(): call(functools.partial(below_sample, nbrick, cap), [struct(nbrick * back,...  2.73 us
  transfers between devices with their start and end apart: 20, of which 4 were waited for; matrix products, arithmetic and copies ran while one was open for 0% of the time, Pallas kernels for 22%

profile of v5, /device:TPU:0, one launch (start us, length us, event | category | flops | bytes accessed | tf_op | source)
XLA Modules:
  0.0 70.4 jit_solution(16990380628936947043)
XLA Ops:
  0.7 1.0 %pad_maximum_fusion.state = f32[7,64,128]{2,1,0:T(8,128)S(1)} fusion(f32[3,64,128]{2,1,0:T(8,128)} %bitcast.6, f32[1,64,128]{2,1,0:T(8,128)} %bitcast.9, f32[3,64,128]{2,1,0:T(8,128)} %bitcast.7), kind=kLoop, calls=%fused_computation | loop fusion | flops 114688 | bytes 458752 | tf_op jit(solution)/shard_map/concatenate | solution.py:719
  1.7 1.1 %copy-done = f32[3,4,32,512]{3,2,1,0:T(8,128)S(1)} copy-done((f32[3,4,32,512]{3,2,1,0:T(8,128)S(1)}, f32[3,4,32,512]{3,2,1,0:T(8,128)}, u32[]{:S(2)}) %copy-start) | copy-done | bytes 786456
  2.8 0.7 copy-done.3
  3.5 0.7 pack.1
  4.1 3.0 %collective-permute-start = (f32[440,128]{1,0:T(8,128)S(1)}, f32[440,128]{1,0:T(8,128)S(1)}, u32[]{:S(2)}, u32[]{:S(2)}) collective-permute-start(f32[440,128]{1,0:T(8,128)S(1)} %get-tuple-element.30), channel_id=1, source_target_pairs={{0,4},{4,8},{8,12},{12,16},{16,20},{20,24},{24,28},{28,0},{1,5},{5... | collective-permute-start | bytes 675848 | tf_op jit(solution)/shard_map/ppermute | solution.py:714
  7.2 3.1 %collective-permute-start.1 = (f32[440,128]{1,0:T(8,128)S(1)}, f32[440,128]{1,0:T(8,128)S(1)}, u32[]{:S(2)}, u32[]{:S(2)}) collective-permute-start(f32[440,128]{1,0:T(8,128)S(1)} %get-tuple-element.31), channel_id=1, source_target_pairs={{0,28},{4,0},{8,4},{12,8},{16,12},{20,16},{24,20},{28,24},{1,29},{... | collective-permute-start | bytes 675848 | tf_op jit(solution)/shard_map/ppermute | solution.py:714
  10.3 1.7 %collective-permute-start.3 = (f32[104,128]{1,0:T(8,128)S(1)}, f32[104,128]{1,0:T(8,128)S(1)}, u32[]{:S(2)}, u32[]{:S(2)}) collective-permute-start(f32[104,128]{1,0:T(8,128)S(1)} %get-tuple-element.33), channel_id=1, source_target_pairs={{0,3},{1,0},{2,1},{3,2},{4,7},{5,4},{6,5},{7,6},{8,11},{9,8},{10,9... | collective-permute-start | bytes 159752 | tf_op jit(solution)/shard_map/ppermute | solution.py:714
  12.0 7.3 %own_contacts.1 = (f32[2080,128]{1,0:T(8,128)S(1)}, f32[1040,128]{1,0:T(8,128)S(1)}, f32[64,128]{1,0:T(8,128)S(1)}, s32[64,128]{1,0:T(8,128)S(1)}, f32[16,128]{1,0:T(8,128)S(1)}) custom-call(s32[128]{0:T(128)S(1)} %copy-done.4, s32[128]{0:T(128)S(1)} %copy-done.5, f32[7,64,128]{2,1,0:T(8,128)S(1)} %pad_maximum_fusion.state, s32[64,128]{1,0:T(8,128)S(1)} %copy-done.2, ...), custom_call_target="tpu_custom_call" | custom-call | flops 419430400 | bytes 1048576 | tf_op jit(solution)/shard_map/own_contacts/pallas_call | solution.py:745
  19.3 6.0 %ghost_contacts.1 = (f32[3,64,128]{2,1,0:T(8,128)S(1)}, f32[224,128]{1,0:T(8,128)S(1)}, f32[112,128]{1,0:T(8,128)S(1)}, f32[112,128]{1,0:T(8,128)S(1)}, f32[112,128]{1,0:T(8,128)S(1)}, /*index=5*/f32[112,128]{1,0:T(8,128)S(1)}) custom-call(s32[128]{0:T(128)S(1)} %copy-done.4, s32[128]{0:T(128)S(1)} %copy-done.5, s32[64,128]{1,0:T(8,128)S(1)} %get-tuple-element.29.plan, ...), custom_call_target="tpu_custom_call" | custom-call | flops 209715200 | bytes 1048576 | tf_op jit(solution)/shard_map/ghost_contacts/pallas_call | solution.py:759
  25.5 1.5 %collective-permute-start.5 = (f32[112,128]{1,0:T(8,128)S(1)}, f32[112,128]{1,0:T(8,128)S(1)}, u32[]{:S(2)}, u32[]{:S(2)}) collective-permute-start(f32[112,128]{1,0:T(8,128)S(1)} %get-tuple-element.41), channel_id=1, source_target_pairs={{0,2},{1,3},{2,0},{3,1},{4,6},{5,7},{6,4},{7,5},{8,10},{9,11},{10,... | collective-permute-start | bytes 172040 | tf_op jit(solution)/shard_map/ppermute | solution.py:714
  27.0 1.4 %collective-permute-start.6 = (f32[112,128]{1,0:T(8,128)S(1)}, f32[112,128]{1,0:T(8,128)S(1)}, u32[]{:S(2)}, u32[]{:S(2)}) collective-permute-start(f32[112,128]{1,0:T(8,128)S(1)} %get-tuple-element.42), channel_id=1, source_target_pairs={{0,3},{1,0},{2,1},{3,2},{4,7},{5,4},{6,5},{7,6},{8,11},{9,8},{10,9... | collective-permute-start | bytes 172040 | tf_op jit(solution)/shard_map/ppermute | solution.py:714
  28.4 3.3 %collective-permute-start.8 = (f32[224,128]{1,0:T(8,128)S(1)}, f32[224,128]{1,0:T(8,128)S(1)}, u32[]{:S(2)}, u32[]{:S(2)}) collective-permute-start(f32[224,128]{1,0:T(8,128)S(1)} %get-tuple-element.45), channel_id=1, source_target_pairs={{0,28},{4,0},{8,4},{12,8},{16,12},{20,16},{24,20},{28,24},{1,29},{... | collective-permute-start | bytes 344072 | tf_op jit(solution)/shard_map/ppermute | solution.py:714
  31.9 2.2 %collective-permute-done.8 = f32[224,128]{1,0:T(8,128)S(1)} collective-permute-done((f32[224,128]{1,0:T(8,128)S(1)}, f32[224,128]{1,0:T(8,128)S(1)}, u32[]{:S(2)}, u32[]{:S(2)}) %collective-permute-start.8) | collective-permute-done | bytes 114720 | tf_op jit(solution)/shard_map/ppermute | solution.py:714
  34.2 0.7 collective-permute-start.10
  35.0 3.1 %first_deposit.1 = (f32[1024,256]{1,0:T(8,128)S(1)}, f32[3,4,32,512]{3,2,1,0:T(8,128)S(1)}) custom-call(f32[224,128]{1,0:T(8,128)S(1)} %pad_maximum_fusion.1.crossed, f32[440,128]{1,0:T(8,128)S(1)} %collective-permute-done.below, f32[440,128]{1,0:T(8,128)S(1)} %collective-permute-done.1.above, f32[104,128]{1,0:T(8,128)S(1)} %collective-permute-done.2.before, ...), custom_call_target="tpu_custom_call" | custom-call | flops 1431655808 | bytes 1048576 | tf_op jit(solution)/shard_map/first_deposit/pallas_call | solution.py:787
  38.4 0.9 %collective-permute-done.7.below = f32[224,128]{1,0:T(8,128)S(1)} collective-permute-done((f32[224,128]{1,0:T(8,128)S(1)}, f32[224,128]{1,0:T(8,128)S(1)}, u32[]{:S(2)}, u32[]{:S(2)}) %collective-permute-start.7) | collective-permute-done | bytes 114720 | tf_op jit(solution)/shard_map/ppermute | solution.py:714
  39.3 6.7 %advance.1 = (f32[3,4,32,512]{3,2,1,0:T(8,128)}, bf16[1536,256]{1,0:T(8,128)(2,1)S(1)}, f32[40,128]{1,0:T(8,128)S(1)}, f32[40,128]{1,0:T(8,128)S(1)}, f32[40,128]{1,0:T(8,128)S(1)}, /*index=5*/f32[40,128]{1,0:T(8,128)S(1)}) custom-call(f32[1024,256]{1,0:T(8,128)S(1)} %get-tuple-element.43.start, f32[3,4,32,512]{3,2,1,0:T(8,128)S(1)} %copy-done.1, ...), custom_call_target="tpu_custom_call" | custom-call | flops 4294967296 | bytes 1048576 | tf_op jit(solution)/shard_map/advance/pallas_call | solution.py:797
  46.3 2.5 %collective-permute-start.13 = (f32[40,128]{1,0:T(8,128)S(1)}, f32[40,128]{1,0:T(8,128)S(1)}, u32[]{:S(2)}, u32[]{:S(2)}) collective-permute-start(f32[40,128]{1,0:T(8,128)S(1)} %get-tuple-element.48), channel_id=1, source_target_pairs={{0,2},{1,3},{2,0},{3,1},{4,6},{5,7},{6,4},{7,5},{8,10},{9,11},{10,... | collective-permute-start | bytes 61448 | tf_op jit(solution)/shard_map/ppermute | solution.py:714
  48.7 2.7 %below_sample.1 = f32[160,128]{1,0:T(8,128)S(1)} custom-call(f32[224,128]{1,0:T(8,128)S(1)} %collective-permute-done.7.below, bf16[1536,256]{1,0:T(8,128)(2,1)S(1)} %get-tuple-element.50.table), custom_call_target="tpu_custom_call" | custom-call | flops 67108864 | bytes 1048576 | tf_op jit(solution)/shard_map/below_sample/pallas_call | solution.py:818
  51.5 5.8 %collective-permute-start.16 = (f32[160,128]{1,0:T(8,128)S(1)}, f32[160,128]{1,0:T(8,128)S(1)}, u32[]{:S(2)}, u32[]{:S(2)}) collective-permute-start(f32[160,128]{1,0:T(8,128)S(1)} %below_sample.1), channel_id=1, source_target_pairs={{0,28},{4,0},{8,4},{12,8},{16,12},{20,16},{24,20},{28,24},{1,29},{... | collective-permute-start | bytes 245768 | tf_op jit(solution)/shard_map/ppermute | solution.py:714
  57.3 2.1 %last_sample.1 = (f32[40,128]{1,0:T(8,128)S(1)}, f32[40,128]{1,0:T(8,128)S(1)}, f32[40,128]{1,0:T(8,128)S(1)}, f32[40,128]{1,0:T(8,128)S(1)}) custom-call(f32[224,128]{1,0:T(8,128)S(1)} %pad_maximum_fusion.1.crossed, bf16[1536,256]{1,0:T(8,128)(2,1)S(1)} %get-tuple-element.50.table), custom_call_target="tpu_custom_call" | custom-call | flops 67108864 | bytes 1048576 | tf_op jit(solution)/shard_map/last_sample/pallas_call | solution.py:831
  60.0 1.3 %collective-permute-start.18 = (f32[80,128]{1,0:T(8,128)S(1)}, f32[80,128]{1,0:T(8,128)S(1)}, u32[]{:S(2)}, u32[]{:S(2)}) collective-permute-start(f32[80,128]{1,0:T(8,128)S(1)} %pad_maximum_fusion.6), channel_id=1, source_target_pairs={{0,2},{1,3},{2,0},{3,1},{4,6},{5,7},{6,4},{7,5},{8,10},{9,11},{10,... | collective-permute-start | bytes 122888 | tf_op jit(solution)/shard_map/ppermute | solution.py:714
  61.3 5.3 %collective-permute-done.15.down = f32[160,128]{1,0:T(8,128)S(1)} collective-permute-done((f32[160,128]{1,0:T(8,128)S(1)}, f32[160,128]{1,0:T(8,128)S(1)}, u32[]{:S(2)}, u32[]{:S(2)}) %collective-permute-start.15) | collective-permute-done | bytes 81952 | tf_op jit(solution)/shard_map/ppermute | solution.py:714
  66.6 3.6 %relax.1 = f32[3,64,128]{2,1,0:T(8,128)} custom-call(s32[64,128]{1,0:T(8,128)S(1)} %get-tuple-element.29.plan, f32[3,64,128]{2,1,0:T(8,128)S(1)} %get-tuple-element.38.updated, f32[64,128]{1,0:T(8,128)S(1)} %get-tuple-element.36.spots, f32[160,128]{1,0:T(8,128)S(1)} %collective-permute-done.15.down, f32[80,128]{1,0:T(8,128)S(1)} %pad_maximum_fusion.4.rest_0_, ...), custom_call_target="tpu_custom_call" | custom-call | bytes 1048576 | tf_op jit(solution)/shard_map/relax/pallas_call | solution.py:844
  (52 shorter events, 1.6 us)
Async XLA Ops:
  0.6 11.4 %copy-start.5 = (s32[128]{0:T(128)S(1)}, s32[128]{0:T(128)}, u32[]{:S(2)}) copy-start(s32[128]{0:T(128)} %partner_list.3) | copy-start | bytes 1540
  0.6 11.4 %copy-start.4 = (s32[128]{0:T(128)S(1)}, s32[128]{0:T(128)}, u32[]{:S(2)}) copy-start(s32[128]{0:T(128)} %home_list.3) | copy-start | bytes 1540
  0.7 11.4 %copy-start.2 = (s32[64,128]{1,0:T(8,128)S(1)}, s32[64,128]{1,0:T(8,128)}, u32[]{:S(2)}) copy-start(s32[64,128]{1,0:T(8,128)} %cell.3) | copy-start | bytes 98308
  0.7 11.4 %copy-start.6 = (s32[64,1]{0,1:T(1,128)S(1)}, s32[64,1]{0,1:T(1,128)}, u32[]{:S(2)}) copy-start(s32[64,1]{0,1:T(1,128)} %param.13) | copy-start | bytes 772
  4.1 15.2 %collective-permute-start = (f32[440,128]{1,0:T(8,128)S(1)}, f32[440,128]{1,0:T(8,128)S(1)}, u32[]{:S(2)}, u32[]{:S(2)}) collective-permute-start(f32[440,128]{1,0:T(8,128)S(1)} %get-tuple-element.30), channel_id=1, source_target_pairs={{0,4},{4,8},{8,12},{12,16},{16,20},{20,24},{24,28},{28,0},{1,5},{5... | collective-permute-start | bytes 675848 | tf_op jit(solution)/shard_map/ppermute | solution.py:714
  7.2 12.2 %collective-permute-start.1 = (f32[440,128]{1,0:T(8,128)S(1)}, f32[440,128]{1,0:T(8,128)S(1)}, u32[]{:S(2)}, u32[]{:S(2)}) collective-permute-start(f32[440,128]{1,0:T(8,128)S(1)} %get-tuple-element.31), channel_id=1, source_target_pairs={{0,28},{4,0},{8,4},{12,8},{16,12},{20,16},{24,20},{28,24},{1,29},{... | collective-permute-start | bytes 675848 | tf_op jit(solution)/shard_map/ppermute | solution.py:714
  10.3 9.1 %collective-permute-start.2 = (f32[104,128]{1,0:T(8,128)S(1)}, f32[104,128]{1,0:T(8,128)S(1)}, u32[]{:S(2)}, u32[]{:S(2)}) collective-permute-start(f32[104,128]{1,0:T(8,128)S(1)} %get-tuple-element.32), channel_id=1, source_target_pairs={{0,1},{1,2},{2,3},{3,0},{4,5},{5,6},{6,7},{7,4},{8,9},{9,10},{10,1... | collective-permute-start | bytes 159752 | tf_op jit(solution)/shard_map/ppermute | solution.py:714
  10.3 9.1 %collective-permute-start.3 = (f32[104,128]{1,0:T(8,128)S(1)}, f32[104,128]{1,0:T(8,128)S(1)}, u32[]{:S(2)}, u32[]{:S(2)}) collective-permute-start(f32[104,128]{1,0:T(8,128)S(1)} %get-tuple-element.33), channel_id=1, source_target_pairs={{0,3},{1,0},{2,1},{3,2},{4,7},{5,4},{6,5},{7,6},{8,11},{9,8},{10,9... | collective-permute-start | bytes 159752 | tf_op jit(solution)/shard_map/ppermute | solution.py:714
  25.4 6.3 %collective-permute-start.4 = (f32[112,128]{1,0:T(8,128)S(1)}, f32[112,128]{1,0:T(8,128)S(1)}, u32[]{:S(2)}, u32[]{:S(2)}) collective-permute-start(f32[112,128]{1,0:T(8,128)S(1)} %get-tuple-element.40), channel_id=1, source_target_pairs={{0,1},{1,2},{2,3},{3,0},{4,5},{5,6},{6,7},{7,4},{8,9},{9,10},{10,1... | collective-permute-start | bytes 172040 | tf_op jit(solution)/shard_map/ppermute | solution.py:714
  25.5 6.3 %collective-permute-start.5 = (f32[112,128]{1,0:T(8,128)S(1)}, f32[112,128]{1,0:T(8,128)S(1)}, u32[]{:S(2)}, u32[]{:S(2)}) collective-permute-start(f32[112,128]{1,0:T(8,128)S(1)} %get-tuple-element.41), channel_id=1, source_target_pairs={{0,2},{1,3},{2,0},{3,1},{4,6},{5,7},{6,4},{7,5},{8,10},{9,11},{10,... | collective-permute-start | bytes 172040 | tf_op jit(solution)/shard_map/ppermute | solution.py:714
  27.0 4.7 %collective-permute-start.6 = (f32[112,128]{1,0:T(8,128)S(1)}, f32[112,128]{1,0:T(8,128)S(1)}, u32[]{:S(2)}, u32[]{:S(2)}) collective-permute-start(f32[112,128]{1,0:T(8,128)S(1)} %get-tuple-element.42), channel_id=1, source_target_pairs={{0,3},{1,0},{2,1},{3,2},{4,7},{5,4},{6,5},{7,6},{8,11},{9,8},{10,9... | collective-permute-start | bytes 172040 | tf_op jit(solution)/shard_map/ppermute | solution.py:714
  28.4 5.7 %collective-permute-start.8 = (f32[224,128]{1,0:T(8,128)S(1)}, f32[224,128]{1,0:T(8,128)S(1)}, u32[]{:S(2)}, u32[]{:S(2)}) collective-permute-start(f32[224,128]{1,0:T(8,128)S(1)} %get-tuple-element.45), channel_id=1, source_target_pairs={{0,28},{4,0},{8,4},{12,8},{16,12},{20,16},{24,20},{28,24},{1,29},{... | collective-permute-start | bytes 344072 | tf_op jit(solution)/shard_map/ppermute | solution.py:714
  31.8 7.5 %collective-permute-start.7 = (f32[224,128]{1,0:T(8,128)S(1)}, f32[224,128]{1,0:T(8,128)S(1)}, u32[]{:S(2)}, u32[]{:S(2)}) collective-permute-start(f32[224,128]{1,0:T(8,128)S(1)} %pad_maximum_fusion.2), channel_id=1, source_target_pairs={{0,4},{4,8},{8,12},{12,16},{16,20},{20,24},{24,28},{28,0},{1,5},{5... | collective-permute-start | bytes 344072 | tf_op jit(solution)/shard_map/ppermute | solution.py:714
  34.1 4.0 %collective-permute-start.11 = (f32[56,128]{1,0:T(8,128)S(1)}, f32[56,128]{1,0:T(8,128)S(1)}, u32[]{:S(2)}, u32[]{:S(2)}) collective-permute-start(f32[56,128]{1,0:T(8,128)S(1)} %get-tuple-element.56), channel_id=1, source_target_pairs={{0,3},{1,0},{2,1},{3,2},{4,7},{5,4},{6,5},{7,6},{8,11},{9,8},{10,9... | collective-permute-start | bytes 86024 | tf_op jit(solution)/shard_map/ppermute | solution.py:714
  34.2 4.2 %collective-permute-start.10 = (f32[56,128]{1,0:T(8,128)S(1)}, f32[56,128]{1,0:T(8,128)S(1)}, u32[]{:S(2)}, u32[]{:S(2)}) collective-permute-start(f32[56,128]{1,0:T(8,128)S(1)} %get-tuple-element.57), channel_id=1, source_target_pairs={{0,2},{1,3},{2,0},{3,1},{4,6},{5,7},{6,4},{7,5},{8,10},{9,11},{10,... | collective-permute-start | bytes 86024 | tf_op jit(solution)/shard_map/ppermute | solution.py:714
  34.8 3.6 %collective-permute-start.9 = (f32[56,128]{1,0:T(8,128)S(1)}, f32[56,128]{1,0:T(8,128)S(1)}, u32[]{:S(2)}, u32[]{:S(2)}) collective-permute-start(f32[56,128]{1,0:T(8,128)S(1)} %get-tuple-element.58), channel_id=1, source_target_pairs={{0,1},{1,2},{2,3},{3,0},{4,5},{5,6},{6,7},{7,4},{8,9},{9,10},{10,1... | collective-permute-start | bytes 86024 | tf_op jit(solution)/shard_map/ppermute | solution.py:714
  46.0 13.4 %collective-permute-start.12 = (f32[40,128]{1,0:T(8,128)S(1)}, f32[40,128]{1,0:T(8,128)S(1)}, u32[]{:S(2)}, u32[]{:S(2)}) collective-permute-start(f32[40,128]{1,0:T(8,128)S(1)} %get-tuple-element.47), channel_id=1, source_target_pairs={{0,3},{1,0},{2,1},{3,2},{4,7},{5,4},{6,5},{7,6},{8,11},{9,8},{10,9... | collective-permute-start | bytes 61448 | tf_op jit(solution)/shard_map/ppermute | solution.py:714
  46.3 13.1 %collective-permute-start.13 = (f32[40,128]{1,0:T(8,128)S(1)}, f32[40,128]{1,0:T(8,128)S(1)}, u32[]{:S(2)}, u32[]{:S(2)}) collective-permute-start(f32[40,128]{1,0:T(8,128)S(1)} %get-tuple-element.48), channel_id=1, source_target_pairs={{0,2},{1,3},{2,0},{3,1},{4,6},{5,7},{6,4},{7,5},{8,10},{9,11},{10,... | collective-permute-start | bytes 61448 | tf_op jit(solution)/shard_map/ppermute | solution.py:714
  48.7 10.7 %collective-permute-start.14 = (f32[40,128]{1,0:T(8,128)S(1)}, f32[40,128]{1,0:T(8,128)S(1)}, u32[]{:S(2)}, u32[]{:S(2)}) collective-permute-start(f32[40,128]{1,0:T(8,128)S(1)} %get-tuple-element.49), channel_id=1, source_target_pairs={{0,1},{1,2},{2,3},{3,0},{4,5},{5,6},{6,7},{7,4},{8,9},{9,10},{10,1... | collective-permute-start | bytes 61448 | tf_op jit(solution)/shard_map/ppermute | solution.py:714
  51.5 8.1 %collective-permute-start.16 = (f32[160,128]{1,0:T(8,128)S(1)}, f32[160,128]{1,0:T(8,128)S(1)}, u32[]{:S(2)}, u32[]{:S(2)}) collective-permute-start(f32[160,128]{1,0:T(8,128)S(1)} %below_sample.1), channel_id=1, source_target_pairs={{0,28},{4,0},{8,4},{12,8},{16,12},{20,16},{24,20},{28,24},{1,29},{... | collective-permute-start | bytes 245768 | tf_op jit(solution)/shard_map/ppermute | solution.py:714
  59.4 7.2 %collective-permute-start.15 = (f32[160,128]{1,0:T(8,128)S(1)}, f32[160,128]{1,0:T(8,128)S(1)}, u32[]{:S(2)}, u32[]{:S(2)}) collective-permute-start(f32[160,128]{1,0:T(8,128)S(1)} %pad_maximum_fusion.3), channel_id=1, source_target_pairs={{0,4},{4,8},{8,12},{12,16},{16,20},{20,24},{24,28},{28,0},{1,5},{5... | collective-permute-start | bytes 245768 | tf_op jit(solution)/shard_map/ppermute | solution.py:714
  59.5 7.1 %collective-permute-start.17 = (f32[80,128]{1,0:T(8,128)S(1)}, f32[80,128]{1,0:T(8,128)S(1)}, u32[]{:S(2)}, u32[]{:S(2)}) collective-permute-start(f32[80,128]{1,0:T(8,128)S(1)} %pad_maximum_fusion.5), channel_id=1, source_target_pairs={{0,3},{1,0},{2,1},{3,2},{4,7},{5,4},{6,5},{7,6},{8,11},{9,8},{10,9... | collective-permute-start | bytes 122888 | tf_op jit(solution)/shard_map/ppermute | solution.py:714
  60.0 6.6 %collective-permute-start.18 = (f32[80,128]{1,0:T(8,128)S(1)}, f32[80,128]{1,0:T(8,128)S(1)}, u32[]{:S(2)}, u32[]{:S(2)}) collective-permute-start(f32[80,128]{1,0:T(8,128)S(1)} %pad_maximum_fusion.6), channel_id=1, source_target_pairs={{0,2},{1,3},{2,0},{3,1},{4,6},{5,7},{6,4},{7,5},{8,10},{9,11},{10,... | collective-permute-start | bytes 122888 | tf_op jit(solution)/shard_map/ppermute | solution.py:714
  61.3 5.3 %collective-permute-start.19 = (f32[80,128]{1,0:T(8,128)S(1)}, f32[80,128]{1,0:T(8,128)S(1)}, u32[]{:S(2)}, u32[]{:S(2)}) collective-permute-start(f32[80,128]{1,0:T(8,128)S(1)} %pad_maximum_fusion.7), channel_id=1, source_target_pairs={{0,1},{1,2},{2,3},{3,0},{4,5},{5,6},{6,7},{7,4},{8,9},{9,10},{10,1... | collective-permute-start | bytes 122888 | tf_op jit(solution)/shard_map/ppermute | solution.py:714
  (3 other events, 11.4 us)

commit v6 on v5

--- a/solution.py
+++ b/solution.py
@@ -626,7 +626,7 @@
     sample(nbrick, counts, below, (base, goal), cap, table, answers)
 
 
-def last_sample(nbrick, cap, crossed, table, *rest):
+def last_sample(nbrick, cap, _, crossed, table, *rest):
     answers, base, goal, counts = rest[nbrick:]
     chunk = rows_up(5 * cap + 1)
     back = rows_up(3 * cap)
@@ -827,15 +827,16 @@
     answers_above = [
         shifted(part, "brick", -behind) for behind, part in enumerate(answers_above)
     ]
-    returned_down = shifted(jnp.concatenate(answers_above, axis=0), "slab", 1)
+    joined = jnp.concatenate(answers_above, axis=0)
+    returned_down = shifted(joined, "slab", 1)
     answers = call(
         functools.partial(last_sample, nbrick, cap),
         [struct(back, width)] * nbrick,
-        [VMEM] * 2,
+        [ANY] + [VMEM] * 2,
         [pltpu.VMEM((nbrick * back, width), f32)] + places(nbrick),
         "last_sample",
         block_flops * nblocks // 64,
-    )(crossed, table)
+    )(joined, crossed, table)
     returned = []
     for behind in range(nbrick):
         at = slice(behind * back, (behind + 1) * back)

time: 70 us -> 69 us (0.986)
  waiting for transfers between devices: 8.84 us -> 6.24 us
  starting transfers between devices: 25.4 us -> 26.5 us
    ppermute x20, waiting for transfers between devices: 8.84 us -> 6.24 us  [shifted(): lax.ppermute(x, axis, [(i, (i + step) % count) for i in range(count)])]
    pallas_call x1, Pallas kernels: 2.73 us -> 1.5 us  [on_device(): call(functools.partial(below_sample, nbrick, cap), [struct(nbrick * back,...]
    ppermute x20, starting transfers between devices: 25.4 us -> 26.5 us  [shifted(): lax.ppermute(x, axis, [(i, (i + step) % count) for i in range(count)])]
    pallas_call x1, Pallas kernels: 3.06 us -> 4.09 us  [on_device(): call(functools.partial(first_deposit, nbrick, cap, ghost_rows), [struct(8...]
    pallas_call x1, Pallas kernels: 2.12 us -> 2.95 us  [on_device(): call(functools.partial(last_sample, nbrick, cap), [struct(back, width)] *...]
    unnamed x14 -> x17, local copies, waits for them, and re-layouts: 1.81 us -> 1.82 us
where the time goes in v6:
time: 69 us; the launch traced here: 68.9 us
  Pallas kernels  32.2 us (47%)
  starting transfers between devices  26.5 us (38%)
  waiting for transfers between devices  6.24 us (9%)
  local copies, waits for them, and re-layouts  1.86 us (3%)
  between operations  1.11 us (2%)
  other arithmetic  1.04 us (2%)
    ppermute x20, starting transfers between devices, shifted(): lax.ppermute(x, axis, [(i, (i + step) % count) for i in range(count)])  26.5 us
    pallas_call x1, Pallas kernels, on_device(): call(functools.partial(own_contacts, cap, columns, nz), [struct((nblocks...  6.9 us
    pallas_call x1, Pallas kernels, on_device(): call(functools.partial(ghost_contacts, nbrick, cap, 4 * per), [struct(3,...  6.4 us
    ppermute x20, waiting for transfers between devices, shifted(): lax.ppermute(x, axis, [(i, (i + step) % count) for i in range(count)])  6.24 us
    pallas_call x1, Pallas kernels, on_device(): call(functools.partial(advance, nbrick, cap), [struct(3, nx, ny, nz), str...  6.11 us
    pallas_call x1, Pallas kernels, on_device(): call(functools.partial(first_deposit, nbrick, cap, ghost_rows), [struct(8...  4.09 us
    pallas_call x1, Pallas kernels, on_device(): call(functools.partial(relax, nbrick, cap), [struct(3, nblocks, width)],...  3.55 us
    pallas_call x1, Pallas kernels, on_device(): call(functools.partial(last_sample, nbrick, cap), [struct(back, width)] *...  2.95 us
  transfers between devices with their start and end apart: 20, of which 4 were waited for; matrix products, arithmetic and copies ran while one was open for 0% of the time, Pallas kernels for 22%

profile of v6, /device:TPU:0, one launch (start us, length us, event | category | flops | bytes accessed | tf_op | source)
XLA Modules:
  0.0 68.9 jit_solution(8251227134991942331)
XLA Ops:
  0.7 1.0 %pad_maximum_fusion.state = f32[7,64,128]{2,1,0:T(8,128)S(1)} fusion(f32[3,64,128]{2,1,0:T(8,128)} %bitcast.6, f32[1,64,128]{2,1,0:T(8,128)} %bitcast.9, f32[3,64,128]{2,1,0:T(8,128)} %bitcast.7), kind=kLoop, calls=%fused_computation | loop fusion | flops 114688 | bytes 458752 | tf_op jit(solution)/shard_map/concatenate | solution.py:719
  1.7 1.1 %copy-done = f32[3,4,32,512]{3,2,1,0:T(8,128)S(1)} copy-done((f32[3,4,32,512]{3,2,1,0:T(8,128)S(1)}, f32[3,4,32,512]{3,2,1,0:T(8,128)}, u32[]{:S(2)}) %copy-start) | copy-done | bytes 786456
  2.8 0.7 copy-done.3
  3.5 0.7 pack.1
  4.1 3.0 %collective-permute-start = (f32[440,128]{1,0:T(8,128)S(1)}, f32[440,128]{1,0:T(8,128)S(1)}, u32[]{:S(2)}, u32[]{:S(2)}) collective-permute-start(f32[440,128]{1,0:T(8,128)S(1)} %get-tuple-element.30), channel_id=1, source_target_pairs={{0,4},{4,8},{8,12},{12,16},{16,20},{20,24},{24,28},{28,0},{1,5},{5... | collective-permute-start | bytes 675848 | tf_op jit(solution)/shard_map/ppermute | solution.py:714
  7.2 3.1 %collective-permute-start.1 = (f32[440,128]{1,0:T(8,128)S(1)}, f32[440,128]{1,0:T(8,128)S(1)}, u32[]{:S(2)}, u32[]{:S(2)}) collective-permute-start(f32[440,128]{1,0:T(8,128)S(1)} %get-tuple-element.31), channel_id=1, source_target_pairs={{0,28},{4,0},{8,4},{12,8},{16,12},{20,16},{24,20},{28,24},{1,29},{... | collective-permute-start | bytes 675848 | tf_op jit(solution)/shard_map/ppermute | solution.py:714
  10.3 1.7 %collective-permute-start.3 = (f32[104,128]{1,0:T(8,128)S(1)}, f32[104,128]{1,0:T(8,128)S(1)}, u32[]{:S(2)}, u32[]{:S(2)}) collective-permute-start(f32[104,128]{1,0:T(8,128)S(1)} %get-tuple-element.33), channel_id=1, source_target_pairs={{0,3},{1,0},{2,1},{3,2},{4,7},{5,4},{6,5},{7,6},{8,11},{9,8},{10,9... | collective-permute-start | bytes 159752 | tf_op jit(solution)/shard_map/ppermute | solution.py:714
  12.0 6.9 %own_contacts.1 = (f32[2080,128]{1,0:T(8,128)S(1)}, f32[1040,128]{1,0:T(8,128)S(1)}, f32[64,128]{1,0:T(8,128)S(1)}, s32[64,128]{1,0:T(8,128)S(1)}, f32[16,128]{1,0:T(8,128)S(1)}) custom-call(s32[128]{0:T(128)S(1)} %copy-done.4, s32[128]{0:T(128)S(1)} %copy-done.5, f32[7,64,128]{2,1,0:T(8,128)S(1)} %pad_maximum_fusion.state, s32[64,128]{1,0:T(8,128)S(1)} %copy-done.2, ...), custom_call_target="tpu_custom_call" | custom-call | flops 419430400 | bytes 1048576 | tf_op jit(solution)/shard_map/own_contacts/pallas_call | solution.py:745
  19.0 6.4 %ghost_contacts.1 = (f32[3,64,128]{2,1,0:T(8,128)S(1)}, f32[224,128]{1,0:T(8,128)S(1)}, f32[112,128]{1,0:T(8,128)S(1)}, f32[112,128]{1,0:T(8,128)S(1)}, f32[112,128]{1,0:T(8,128)S(1)}, /*index=5*/f32[112,128]{1,0:T(8,128)S(1)}) custom-call(s32[128]{0:T(128)S(1)} %copy-done.4, s32[128]{0:T(128)S(1)} %copy-done.5, s32[64,128]{1,0:T(8,128)S(1)} %get-tuple-element.29.plan, ...), custom_call_target="tpu_custom_call" | custom-call | flops 209715200 | bytes 1048576 | tf_op jit(solution)/shard_map/ghost_contacts/pallas_call | solution.py:759
  25.5 1.3 %collective-permute-start.5 = (f32[112,128]{1,0:T(8,128)S(1)}, f32[112,128]{1,0:T(8,128)S(1)}, u32[]{:S(2)}, u32[]{:S(2)}) collective-permute-start(f32[112,128]{1,0:T(8,128)S(1)} %get-tuple-element.41), channel_id=1, source_target_pairs={{0,2},{1,3},{2,0},{3,1},{4,6},{5,7},{6,4},{7,5},{8,10},{9,11},{10,... | collective-permute-start | bytes 172040 | tf_op jit(solution)/shard_map/ppermute | solution.py:714
  26.7 1.4 %collective-permute-start.6 = (f32[112,128]{1,0:T(8,128)S(1)}, f32[112,128]{1,0:T(8,128)S(1)}, u32[]{:S(2)}, u32[]{:S(2)}) collective-permute-start(f32[112,128]{1,0:T(8,128)S(1)} %get-tuple-element.42), channel_id=1, source_target_pairs={{0,3},{1,0},{2,1},{3,2},{4,7},{5,4},{6,5},{7,6},{8,11},{9,8},{10,9... | collective-permute-start | bytes 172040 | tf_op jit(solution)/shard_map/ppermute | solution.py:714
  28.1 3.6 %collective-permute-start.8 = (f32[224,128]{1,0:T(8,128)S(1)}, f32[224,128]{1,0:T(8,128)S(1)}, u32[]{:S(2)}, u32[]{:S(2)}) collective-permute-start(f32[224,128]{1,0:T(8,128)S(1)} %get-tuple-element.45), channel_id=1, source_target_pairs={{0,28},{4,0},{8,4},{12,8},{16,12},{20,16},{24,20},{28,24},{1,29},{... | collective-permute-start | bytes 344072 | tf_op jit(solution)/shard_map/ppermute | solution.py:714
  31.9 2.2 %collective-permute-done.8 = f32[224,128]{1,0:T(8,128)S(1)} collective-permute-done((f32[224,128]{1,0:T(8,128)S(1)}, f32[224,128]{1,0:T(8,128)S(1)}, u32[]{:S(2)}, u32[]{:S(2)}) %collective-permute-start.8) | collective-permute-done | bytes 114720 | tf_op jit(solution)/shard_map/ppermute | solution.py:714
  34.2 0.7 collective-permute-start.10
  35.0 4.1 %first_deposit.1 = (f32[1024,256]{1,0:T(8,128)S(1)}, f32[3,4,32,512]{3,2,1,0:T(8,128)S(1)}) custom-call(f32[224,128]{1,0:T(8,128)S(1)} %pad_maximum_fusion.1.crossed, f32[440,128]{1,0:T(8,128)S(1)} %collective-permute-done.below, f32[440,128]{1,0:T(8,128)S(1)} %collective-permute-done.1.above, f32[104,128]{1,0:T(8,128)S(1)} %collective-permute-done.2.before, ...), custom_call_target="tpu_custom_call" | custom-call | flops 1431655808 | bytes 1048576 | tf_op jit(solution)/shard_map/first_deposit/pallas_call | solution.py:787
  39.3 6.1 %advance.1 = (f32[3,4,32,512]{3,2,1,0:T(8,128)}, bf16[1536,256]{1,0:T(8,128)(2,1)S(1)}, f32[40,128]{1,0:T(8,128)S(1)}, f32[40,128]{1,0:T(8,128)S(1)}, f32[40,128]{1,0:T(8,128)S(1)}, /*index=5*/f32[40,128]{1,0:T(8,128)S(1)}) custom-call(f32[1024,256]{1,0:T(8,128)S(1)} %get-tuple-element.43.start, f32[3,4,32,512]{3,2,1,0:T(8,128)S(1)} %copy-done.1, ...), custom_call_target="tpu_custom_call" | custom-call | flops 4294967296 | bytes 1048576 | tf_op jit(solution)/shard_map/advance/pallas_call | solution.py:797
  45.5 0.9 %collective-permute-start.12 = (f32[40,128]{1,0:T(8,128)S(1)}, f32[40,128]{1,0:T(8,128)S(1)}, u32[]{:S(2)}, u32[]{:S(2)}) collective-permute-start(f32[40,128]{1,0:T(8,128)S(1)} %get-tuple-element.47), channel_id=1, source_target_pairs={{0,3},{1,0},{2,1},{3,2},{4,7},{5,4},{6,5},{7,6},{8,11},{9,8},{10,9... | collective-permute-start | bytes 61448 | tf_op jit(solution)/shard_map/ppermute | solution.py:714
  46.3 2.8 %collective-permute-start.13 = (f32[40,128]{1,0:T(8,128)S(1)}, f32[40,128]{1,0:T(8,128)S(1)}, u32[]{:S(2)}, u32[]{:S(2)}) collective-permute-start(f32[40,128]{1,0:T(8,128)S(1)} %get-tuple-element.48), channel_id=1, source_target_pairs={{0,2},{1,3},{2,0},{3,1},{4,6},{5,7},{6,4},{7,5},{8,10},{9,11},{10,... | collective-permute-start | bytes 61448 | tf_op jit(solution)/shard_map/ppermute | solution.py:714
  49.1 1.5 %below_sample.1 = f32[160,128]{1,0:T(8,128)S(1)} custom-call(f32[224,128]{1,0:T(8,128)S(1)} %collective-permute-done.7.below, bf16[1536,256]{1,0:T(8,128)(2,1)S(1)} %get-tuple-element.50.table), custom_call_target="tpu_custom_call" | custom-call | flops 67108864 | bytes 1048576 | tf_op jit(solution)/shard_map/below_sample/pallas_call | solution.py:818
  50.6 6.6 %collective-permute-start.16 = (f32[160,128]{1,0:T(8,128)S(1)}, f32[160,128]{1,0:T(8,128)S(1)}, u32[]{:S(2)}, u32[]{:S(2)}) collective-permute-start(f32[160,128]{1,0:T(8,128)S(1)} %below_sample.1), channel_id=1, source_target_pairs={{0,28},{4,0},{8,4},{12,8},{16,12},{20,16},{24,20},{28,24},{1,29},{... | collective-permute-start | bytes 245768 | tf_op jit(solution)/shard_map/ppermute | solution.py:714
  57.3 3.0 %last_sample.1 = (f32[40,128]{1,0:T(8,128)S(1)}, f32[40,128]{1,0:T(8,128)S(1)}, f32[40,128]{1,0:T(8,128)S(1)}, f32[40,128]{1,0:T(8,128)S(1)}) custom-call(f32[160,128]{1,0:T(8,128)S(1)} %constant_dynamic-update-slice_fusion._, f32[224,128]{1,0:T(8,128)S(1)} %pad_maximum_fusion.1.crossed, bf16[1536,256]{1,0:T(8,128)(2,1)S(1)} %get-tuple-element.50.table), custom_call_target="tpu_custom_call" | custom-call | flops 67108864 | bytes 1048576 | tf_op jit(solution)/shard_map/last_sample/pallas_call | solution.py:832
  60.3 0.9 %collective-permute-start.17 = (f32[80,128]{1,0:T(8,128)S(1)}, f32[80,128]{1,0:T(8,128)S(1)}, u32[]{:S(2)}, u32[]{:S(2)}) collective-permute-start(f32[80,128]{1,0:T(8,128)S(1)} %pad_maximum_fusion.4), channel_id=1, source_target_pairs={{0,3},{1,0},{2,1},{3,2},{4,7},{5,4},{6,5},{7,6},{8,11},{9,8},{10,9... | collective-permute-start | bytes 122888 | tf_op jit(solution)/shard_map/ppermute | solution.py:714
  61.4 3.2 %collective-permute-done.15.down = f32[160,128]{1,0:T(8,128)S(1)} collective-permute-done((f32[160,128]{1,0:T(8,128)S(1)}, f32[160,128]{1,0:T(8,128)S(1)}, u32[]{:S(2)}, u32[]{:S(2)}) %collective-permute-start.15) | collective-permute-done | bytes 81952 | tf_op jit(solution)/shard_map/ppermute | solution.py:714
  65.2 3.6 %relax.1 = f32[3,64,128]{2,1,0:T(8,128)} custom-call(s32[64,128]{1,0:T(8,128)S(1)} %get-tuple-element.29.plan, f32[3,64,128]{2,1,0:T(8,128)S(1)} %get-tuple-element.38.updated, f32[64,128]{1,0:T(8,128)S(1)} %get-tuple-element.36.spots, f32[160,128]{1,0:T(8,128)S(1)} %collective-permute-done.15.down, f32[80,128]{1,0:T(8,128)S(1)} %pad_maximum_fusion.3.rest_0_, ...), custom_call_target="tpu_custom_call" | custom-call | bytes 1048576 | tf_op jit(solution)/shard_map/relax/pallas_call | solution.py:845
  (55 shorter events, 1.5 us)
Async XLA Ops:
  0.6 11.4 %copy-start.5 = (s32[128]{0:T(128)S(1)}, s32[128]{0:T(128)}, u32[]{:S(2)}) copy-start(s32[128]{0:T(128)} %partner_list.3) | copy-start | bytes 1540
  0.6 11.4 %copy-start.4 = (s32[128]{0:T(128)S(1)}, s32[128]{0:T(128)}, u32[]{:S(2)}) copy-start(s32[128]{0:T(128)} %home_list.3) | copy-start | bytes 1540
  0.7 11.4 %copy-start.2 = (s32[64,128]{1,0:T(8,128)S(1)}, s32[64,128]{1,0:T(8,128)}, u32[]{:S(2)}) copy-start(s32[64,128]{1,0:T(8,128)} %cell.3) | copy-start | bytes 98308
  0.7 11.4 %copy-start.6 = (s32[64,1]{0,1:T(1,128)S(1)}, s32[64,1]{0,1:T(1,128)}, u32[]{:S(2)}) copy-start(s32[64,1]{0,1:T(1,128)} %param.13) | copy-start | bytes 772
  4.1 14.8 %collective-permute-start = (f32[440,128]{1,0:T(8,128)S(1)}, f32[440,128]{1,0:T(8,128)S(1)}, u32[]{:S(2)}, u32[]{:S(2)}) collective-permute-start(f32[440,128]{1,0:T(8,128)S(1)} %get-tuple-element.30), channel_id=1, source_target_pairs={{0,4},{4,8},{8,12},{12,16},{16,20},{20,24},{24,28},{28,0},{1,5},{5... | collective-permute-start | bytes 675848 | tf_op jit(solution)/shard_map/ppermute | solution.py:714
  7.2 11.8 %collective-permute-start.1 = (f32[440,128]{1,0:T(8,128)S(1)}, f32[440,128]{1,0:T(8,128)S(1)}, u32[]{:S(2)}, u32[]{:S(2)}) collective-permute-start(f32[440,128]{1,0:T(8,128)S(1)} %get-tuple-element.31), channel_id=1, source_target_pairs={{0,28},{4,0},{8,4},{12,8},{16,12},{20,16},{24,20},{28,24},{1,29},{... | collective-permute-start | bytes 675848 | tf_op jit(solution)/shard_map/ppermute | solution.py:714
  10.3 8.7 %collective-permute-start.2 = (f32[104,128]{1,0:T(8,128)S(1)}, f32[104,128]{1,0:T(8,128)S(1)}, u32[]{:S(2)}, u32[]{:S(2)}) collective-permute-start(f32[104,128]{1,0:T(8,128)S(1)} %get-tuple-element.32), channel_id=1, source_target_pairs={{0,1},{1,2},{2,3},{3,0},{4,5},{5,6},{6,7},{7,4},{8,9},{9,10},{10,1... | collective-permute-start | bytes 159752 | tf_op jit(solution)/shard_map/ppermute | solution.py:714
  10.3 8.7 %collective-permute-start.3 = (f32[104,128]{1,0:T(8,128)S(1)}, f32[104,128]{1,0:T(8,128)S(1)}, u32[]{:S(2)}, u32[]{:S(2)}) collective-permute-start(f32[104,128]{1,0:T(8,128)S(1)} %get-tuple-element.33), channel_id=1, source_target_pairs={{0,3},{1,0},{2,1},{3,2},{4,7},{5,4},{6,5},{7,6},{8,11},{9,8},{10,9... | collective-permute-start | bytes 159752 | tf_op jit(solution)/shard_map/ppermute | solution.py:714
  25.4 6.3 %collective-permute-start.4 = (f32[112,128]{1,0:T(8,128)S(1)}, f32[112,128]{1,0:T(8,128)S(1)}, u32[]{:S(2)}, u32[]{:S(2)}) collective-permute-start(f32[112,128]{1,0:T(8,128)S(1)} %get-tuple-element.40), channel_id=1, source_target_pairs={{0,1},{1,2},{2,3},{3,0},{4,5},{5,6},{6,7},{7,4},{8,9},{9,10},{10,1... | collective-permute-start | bytes 172040 | tf_op jit(solution)/shard_map/ppermute | solution.py:714
  25.5 6.3 %collective-permute-start.5 = (f32[112,128]{1,0:T(8,128)S(1)}, f32[112,128]{1,0:T(8,128)S(1)}, u32[]{:S(2)}, u32[]{:S(2)}) collective-permute-start(f32[112,128]{1,0:T(8,128)S(1)} %get-tuple-element.41), channel_id=1, source_target_pairs={{0,2},{1,3},{2,0},{3,1},{4,6},{5,7},{6,4},{7,5},{8,10},{9,11},{10,... | collective-permute-start | bytes 172040 | tf_op jit(solution)/shard_map/ppermute | solution.py:714
  26.7 5.0 %collective-permute-start.6 = (f32[112,128]{1,0:T(8,128)S(1)}, f32[112,128]{1,0:T(8,128)S(1)}, u32[]{:S(2)}, u32[]{:S(2)}) collective-permute-start(f32[112,128]{1,0:T(8,128)S(1)} %get-tuple-element.42), channel_id=1, source_target_pairs={{0,3},{1,0},{2,1},{3,2},{4,7},{5,4},{6,5},{7,6},{8,11},{9,8},{10,9... | collective-permute-start | bytes 172040 | tf_op jit(solution)/shard_map/ppermute | solution.py:714
  28.1 6.0 %collective-permute-start.8 = (f32[224,128]{1,0:T(8,128)S(1)}, f32[224,128]{1,0:T(8,128)S(1)}, u32[]{:S(2)}, u32[]{:S(2)}) collective-permute-start(f32[224,128]{1,0:T(8,128)S(1)} %get-tuple-element.45), channel_id=1, source_target_pairs={{0,28},{4,0},{8,4},{12,8},{16,12},{20,16},{24,20},{28,24},{1,29},{... | collective-permute-start | bytes 344072 | tf_op jit(solution)/shard_map/ppermute | solution.py:714
  31.8 7.5 %collective-permute-start.7 = (f32[224,128]{1,0:T(8,128)S(1)}, f32[224,128]{1,0:T(8,128)S(1)}, u32[]{:S(2)}, u32[]{:S(2)}) collective-permute-start(f32[224,128]{1,0:T(8,128)S(1)} %pad_maximum_fusion.2), channel_id=1, source_target_pairs={{0,4},{4,8},{8,12},{12,16},{16,20},{20,24},{24,28},{28,0},{1,5},{5... | collective-permute-start | bytes 344072 | tf_op jit(solution)/shard_map/ppermute | solution.py:714
  34.1 5.0 %collective-permute-start.11 = (f32[56,128]{1,0:T(8,128)S(1)}, f32[56,128]{1,0:T(8,128)S(1)}, u32[]{:S(2)}, u32[]{:S(2)}) collective-permute-start(f32[56,128]{1,0:T(8,128)S(1)} %get-tuple-element.56), channel_id=1, source_target_pairs={{0,3},{1,0},{2,1},{3,2},{4,7},{5,4},{6,5},{7,6},{8,11},{9,8},{10,9... | collective-permute-start | bytes 86024 | tf_op jit(solution)/shard_map/ppermute | solution.py:714
  34.2 4.9 %collective-permute-start.10 = (f32[56,128]{1,0:T(8,128)S(1)}, f32[56,128]{1,0:T(8,128)S(1)}, u32[]{:S(2)}, u32[]{:S(2)}) collective-permute-start(f32[56,128]{1,0:T(8,128)S(1)} %get-tuple-element.57), channel_id=1, source_target_pairs={{0,2},{1,3},{2,0},{3,1},{4,6},{5,7},{6,4},{7,5},{8,10},{9,11},{10,... | collective-permute-start | bytes 86024 | tf_op jit(solution)/shard_map/ppermute | solution.py:714
  34.8 4.3 %collective-permute-start.9 = (f32[56,128]{1,0:T(8,128)S(1)}, f32[56,128]{1,0:T(8,128)S(1)}, u32[]{:S(2)}, u32[]{:S(2)}) collective-permute-start(f32[56,128]{1,0:T(8,128)S(1)} %get-tuple-element.58), channel_id=1, source_target_pairs={{0,1},{1,2},{2,3},{3,0},{4,5},{5,6},{6,7},{7,4},{8,9},{9,10},{10,1... | collective-permute-start | bytes 86024 | tf_op jit(solution)/shard_map/ppermute | solution.py:714
  45.5 11.8 %collective-permute-start.12 = (f32[40,128]{1,0:T(8,128)S(1)}, f32[40,128]{1,0:T(8,128)S(1)}, u32[]{:S(2)}, u32[]{:S(2)}) collective-permute-start(f32[40,128]{1,0:T(8,128)S(1)} %get-tuple-element.47), channel_id=1, source_target_pairs={{0,3},{1,0},{2,1},{3,2},{4,7},{5,4},{6,5},{7,6},{8,11},{9,8},{10,9... | collective-permute-start | bytes 61448 | tf_op jit(solution)/shard_map/ppermute | solution.py:714
  46.3 10.9 %collective-permute-start.13 = (f32[40,128]{1,0:T(8,128)S(1)}, f32[40,128]{1,0:T(8,128)S(1)}, u32[]{:S(2)}, u32[]{:S(2)}) collective-permute-start(f32[40,128]{1,0:T(8,128)S(1)} %get-tuple-element.48), channel_id=1, source_target_pairs={{0,2},{1,3},{2,0},{3,1},{4,6},{5,7},{6,4},{7,5},{8,10},{9,11},{10,... | collective-permute-start | bytes 61448 | tf_op jit(solution)/shard_map/ppermute | solution.py:714
  49.1 8.1 %collective-permute-start.14 = (f32[40,128]{1,0:T(8,128)S(1)}, f32[40,128]{1,0:T(8,128)S(1)}, u32[]{:S(2)}, u32[]{:S(2)}) collective-permute-start(f32[40,128]{1,0:T(8,128)S(1)} %get-tuple-element.49), channel_id=1, source_target_pairs={{0,1},{1,2},{2,3},{3,0},{4,5},{5,6},{6,7},{7,4},{8,9},{9,10},{10,1... | collective-permute-start | bytes 61448 | tf_op jit(solution)/shard_map/ppermute | solution.py:714
  50.6 9.7 %collective-permute-start.16 = (f32[160,128]{1,0:T(8,128)S(1)}, f32[160,128]{1,0:T(8,128)S(1)}, u32[]{:S(2)}, u32[]{:S(2)}) collective-permute-start(f32[160,128]{1,0:T(8,128)S(1)} %below_sample.1), channel_id=1, source_target_pairs={{0,28},{4,0},{8,4},{12,8},{16,12},{20,16},{24,20},{28,24},{1,29},{... | collective-permute-start | bytes 245768 | tf_op jit(solution)/shard_map/ppermute | solution.py:714
  57.2 7.4 %collective-permute-start.15 = (f32[160,128]{1,0:T(8,128)S(1)}, f32[160,128]{1,0:T(8,128)S(1)}, u32[]{:S(2)}, u32[]{:S(2)}) collective-permute-start(f32[160,128]{1,0:T(8,128)S(1)} %constant_dynamic-update-slice_fusion._), channel_id=1, source_target_pairs={{0,4},{4,8},{8,12},{12,16},{16,20},{20,24},{24,28},{28,0},{1,5},{5... | collective-permute-start | bytes 245768 | tf_op jit(solution)/shard_map/ppermute | solution.py:714
  60.3 4.3 %collective-permute-start.17 = (f32[80,128]{1,0:T(8,128)S(1)}, f32[80,128]{1,0:T(8,128)S(1)}, u32[]{:S(2)}, u32[]{:S(2)}) collective-permute-start(f32[80,128]{1,0:T(8,128)S(1)} %pad_maximum_fusion.4), channel_id=1, source_target_pairs={{0,3},{1,0},{2,1},{3,2},{4,7},{5,4},{6,5},{7,6},{8,11},{9,8},{10,9... | collective-permute-start | bytes 122888 | tf_op jit(solution)/shard_map/ppermute | solution.py:714
  61.2 4.0 %collective-permute-start.18 = (f32[80,128]{1,0:T(8,128)S(1)}, f32[80,128]{1,0:T(8,128)S(1)}, u32[]{:S(2)}, u32[]{:S(2)}) collective-permute-start(f32[80,128]{1,0:T(8,128)S(1)} %pad_maximum_fusion.5), channel_id=1, source_target_pairs={{0,2},{1,3},{2,0},{3,1},{4,6},{5,7},{6,4},{7,5},{8,10},{9,11},{10,... | collective-permute-start | bytes 122888 | tf_op jit(solution)/shard_map/ppermute | solution.py:714
  61.2 4.0 %collective-permute-start.19 = (f32[80,128]{1,0:T(8,128)S(1)}, f32[80,128]{1,0:T(8,128)S(1)}, u32[]{:S(2)}, u32[]{:S(2)}) collective-permute-start(f32[80,128]{1,0:T(8,128)S(1)} %pad_maximum_fusion.6), channel_id=1, source_target_pairs={{0,1},{1,2},{2,3},{3,0},{4,5},{5,6},{6,7},{7,4},{8,9},{9,10},{10,1... | collective-permute-start | bytes 122888 | tf_op jit(solution)/shard_map/ppermute | solution.py:714
  (3 other events, 11.4 us)
